TPU v7x, 32 devices: a whole 2x2x4 slice. The times are simulated.
32 devices in a mesh: dp: 4 (over y, x), fsdp: 8 (over z, core).
Axes of the slice: x: 2, y: 2, z: 4, core: 2. Of those that a mesh axis runs over, the one named last changes fastest.
Arguments:
- tokens: bfloat16 [32768, 768], P(('dp', 'fsdp')), may hold values from -6 to 6
- doc_ids: int32 [32, 1024], P(('dp', 'fsdp')), may hold values from 0 to 5, never falling along the last dimension, each value on 1 to 512 neighbouring positions
- cotangent: bfloat16 [32768, 768], P(('dp', 'fsdp')), may hold values from -6 to 6
- first_gain: bfloat16 [768], P(('dp', 'fsdp')), may hold values from 0.099609375 to 1.8984375
- first_offset: bfloat16 [768], P(('dp', 'fsdp')), may hold values from -1.75 to 1.75
- qkv_weight: bfloat16 [768, 2304], P(('dp', 'fsdp')), may hold values from -0.21875 to 0.21875
- query_bias: bfloat16 [768], P(('dp', 'fsdp')), may hold values from -3 to 3
- value_bias: bfloat16 [768], P(('dp', 'fsdp')), may hold values from -3 to 3
- out_weight: bfloat16 [768, 768], P(('dp', 'fsdp')), may hold values from -5 to 5
- out_bias: bfloat16 [768], P(('dp', 'fsdp')), may hold values from -6 to 6
- second_gain: bfloat16 [768], P(('dp', 'fsdp')), may hold values from 0.099609375 to 1.8984375
- second_offset: bfloat16 [768], P(('dp', 'fsdp')), may hold values from -1.75 to 1.75
- up_weight: bfloat16 [768, 3072], P(('dp', 'fsdp')), may hold values from -0.21875 to 0.21875
- up_bias: bfloat16 [3072], P(('dp', 'fsdp')), may hold values from -3 to 3
- down_weight: bfloat16 [3072, 768], P(('dp', 'fsdp')), may hold values from -0.625 to 0.625
- down_bias: bfloat16 [768], P(('dp', 'fsdp')), may hold values from -6 to 6
Outputs:
- layer_out: bfloat16 [32768, 768], P(('dp', 'fsdp'))
- grad_tokens: float32 [32768, 768], P(('dp', 'fsdp'))
- grad_first_gain: float32 [768], P(('dp', 'fsdp'))
- grad_first_offset: float32 [768], P(('dp', 'fsdp'))
- grad_qkv_weight: float32 [768, 2304], P(('dp', 'fsdp'))
- grad_query_bias: float32 [768], P(('dp', 'fsdp'))
- grad_value_bias: float32 [768], P(('dp', 'fsdp'))
- grad_out_weight: float32 [768, 768], P(('dp', 'fsdp'))
- grad_out_bias: float32 [768], P(('dp', 'fsdp'))
- grad_second_gain: float32 [768], P(('dp', 'fsdp'))
- grad_second_offset: float32 [768], P(('dp', 'fsdp'))
- grad_up_weight: float32 [768, 3072], P(('dp', 'fsdp'))
- grad_up_bias: float32 [3072], P(('dp', 'fsdp'))
- grad_down_weight: float32 [3072, 768], P(('dp', 'fsdp'))
- grad_down_bias: float32 [768], P(('dp', 'fsdp'))
Inputs may be any that keep to these rules, and one draw needn't show every extreme that they name: `doc_ids`: in each packed row document numbers never fall, every document 0 to 5 has 1 to 512 tokens and one has exactly 512.
All inputs are finite; a program needn't handle non-finite values.
Results may differ from a plain program's by a relative error of at most 0.013.
Values may be sent and summed in bfloat16 or wider, within the bound.
A program may use at most 256 MiB of HBM per device.

v0:
```python
import jax
import jax.numpy as jnp
from jax import lax
from jax.sharding import PartitionSpec as P

HEADS = 12
HEAD_DIM = 64


norm_eps = 1e-05
branch_scale = 48.0 ** (-0.5)


def layer_norm(values, gains, offsets):
    average = jnp.mean(values, axis=-1, keepdims=True)
    centred = values - average
    variance = jnp.mean(centred * centred, axis=-1, keepdims=True)
    return centred * lax.rsqrt(variance + norm_eps) * gains + offsets


def scaled_norm(values, gains):
    return layer_norm(values, gains, 0.0)


def dense(former, latter):
    return jnp.dot(former, latter, preferred_element_type=jnp.float32)


def contract_rows(former, latter):
    return lax.dot_general(
        former, latter, (((0,), (0,)), ((), ())), preferred_element_type=jnp.float32
    )


def contract_cols(former, latter):
    return lax.dot_general(
        former, latter, (((1,), (1,)), ((), ())), preferred_element_type=jnp.float32
    )


def block_scores(queries, keys, documents, row_start, row_stop):
    score_scale = queries.shape[2] ** (-0.5)
    scores = (
        jnp.einsum(
            "qhd,khd->hqk",
            queries[row_start:row_stop],
            keys[:row_stop],
            preferred_element_type=jnp.float32,
        )
        * score_scale
    )
    positions = jnp.arange(row_stop)
    allowed = (documents[row_start:row_stop, None] == documents[None, :row_stop]) & (
        positions[None, :] <= positions[row_start:row_stop, None]
    )
    return jnp.where(allowed[None], scores, -1e30)


def attend_row(queries, keys, values, documents):
    seq_len = queries.shape[0]
    block_rows = min(512, seq_len)
    outputs = []
    logsums = []
    for row_start in range(0, seq_len, block_rows):
        row_stop = row_start + block_rows
        scores = block_scores(queries, keys, documents, row_start, row_stop)
        highest = jnp.max(scores, axis=-1, keepdims=True)
        raised = jnp.exp(scores - highest)
        summed = jnp.sum(raised, axis=-1, keepdims=True)
        weights = (raised / summed).astype(jnp.bfloat16)
        outputs.append(
            jnp.einsum(
                "hqk,khd->qhd", weights, values[:row_stop], preferred_element_type=jnp.float32
            )
        )
        logsums.append((highest + jnp.log(summed))[..., 0])
    return (jnp.concatenate(outputs, axis=0).astype(jnp.bfloat16), jnp.concatenate(logsums, axis=1))


def attend_row_back(queries, keys, values, documents, logsums, grad_out):
    seq_len = queries.shape[0]
    block_rows = min(512, seq_len)
    score_scale = queries.shape[2] ** (-0.5)
    query_parts = []
    grad_keys = jnp.zeros(keys.shape, jnp.float32)
    grad_values = jnp.zeros(values.shape, jnp.float32)
    for row_start in range(0, seq_len, block_rows):
        row_stop = row_start + block_rows
        scores = block_scores(queries, keys, documents, row_start, row_stop)
        probs = jnp.exp(scores - logsums[:, row_start:row_stop, None])
        incoming = grad_out[row_start:row_stop]
        grad_probs = jnp.einsum(
            "qhd,khd->hqk", incoming, values[:row_stop], preferred_element_type=jnp.float32
        )
        inner_sum = jnp.sum(probs * grad_probs, axis=-1, keepdims=True)
        grad_scores = (probs * (grad_probs - inner_sum)).astype(jnp.bfloat16)
        query_parts.append(
            jnp.einsum(
                "hqk,khd->qhd", grad_scores, keys[:row_stop], preferred_element_type=jnp.float32
            )
            * score_scale
        )
        key_term = (
            jnp.einsum(
                "hqk,qhd->khd",
                grad_scores,
                queries[row_start:row_stop],
                preferred_element_type=jnp.float32,
            )
            * score_scale
        )
        value_term = jnp.einsum(
            "hqk,qhd->khd", probs.astype(jnp.bfloat16), incoming, preferred_element_type=jnp.float32
        )
        padding = ((0, seq_len - row_stop), (0, 0), (0, 0))
        grad_keys = grad_keys + jnp.pad(key_term, padding)
        grad_values = grad_values + jnp.pad(value_term, padding)
    return (jnp.concatenate(query_parts, axis=0), grad_keys, grad_values)


def per_device(
    tokens,
    doc_ids,
    cotangent,
    first_gain,
    first_offset,
    qkv_weight,
    query_bias,
    value_bias,
    out_weight,
    out_bias,
    second_gain,
    second_offset,
    up_weight,
    up_bias,
    down_weight,
    down_bias,
):
    attn_full = (
        lax.all_gather(first_gain, ("dp", "fsdp"), axis=0, tiled=True),
        lax.all_gather(first_offset, ("dp", "fsdp"), axis=0, tiled=True),
        lax.all_gather(qkv_weight, ("dp", "fsdp"), axis=0, tiled=True),
        lax.all_gather(query_bias, ("dp", "fsdp"), axis=0, tiled=True),
        lax.all_gather(value_bias, ("dp", "fsdp"), axis=0, tiled=True),
        lax.all_gather(out_weight, ("dp", "fsdp"), axis=0, tiled=True),
        lax.all_gather(out_bias, ("dp", "fsdp"), axis=0, tiled=True),
    )
    model_width = tokens.shape[1]
    rows_here = doc_ids.shape[0]
    seq_len = doc_ids.shape[1]
    inputs = tokens.astype(jnp.float32)
    gain_one = attn_full[0].astype(jnp.float32)
    normed_one = layer_norm(inputs, gain_one, attn_full[1].astype(jnp.float32)).astype(jnp.bfloat16)
    projected = dense(normed_one, attn_full[2])
    queries = (projected[:, :model_width] + attn_full[3].astype(jnp.float32)).astype(jnp.bfloat16)
    keys = projected[:, model_width : 2 * model_width].astype(jnp.bfloat16)
    values = (projected[:, 2 * model_width :] + attn_full[4].astype(jnp.float32)).astype(
        jnp.bfloat16
    )
    row_shape = (rows_here, seq_len, HEADS, HEAD_DIM)
    queries = queries.reshape(row_shape)
    keys = keys.reshape(row_shape)
    values = values.reshape(row_shape)
    attended, logsums = lax.map(
        lambda row_item: attend_row(*row_item), (queries, keys, values, doc_ids)
    )
    attended = attended.reshape(-1, model_width)
    branch = dense(attended, attn_full[5]) + attn_full[6].astype(jnp.float32)
    middle = inputs + branch_scale * branch
    mlp_full = (
        lax.all_gather(second_gain, ("dp", "fsdp"), axis=0, tiled=True),
        lax.all_gather(second_offset, ("dp", "fsdp"), axis=0, tiled=True),
        lax.all_gather(up_weight, ("dp", "fsdp"), axis=0, tiled=True),
        lax.all_gather(up_bias, ("dp", "fsdp"), axis=0, tiled=True),
        lax.all_gather(down_weight, ("dp", "fsdp"), axis=0, tiled=True),
        lax.all_gather(down_bias, ("dp", "fsdp"), axis=0, tiled=True),
    )
    gain_two = mlp_full[0].astype(jnp.float32)
    normed_two = layer_norm(middle, gain_two, mlp_full[1].astype(jnp.float32)).astype(jnp.bfloat16)
    hidden = dense(normed_two, mlp_full[2]) + mlp_full[3].astype(jnp.float32)
    active, gelu_back = jax.vjp(lambda pre_act: jax.nn.gelu(pre_act, approximate=True), hidden)
    active = active.astype(jnp.bfloat16)
    outer = dense(active, mlp_full[4]) + mlp_full[5].astype(jnp.float32)
    layer_out = (middle + branch_scale * outer).astype(jnp.bfloat16)
    mlp_back = (
        lax.all_gather(second_gain, ("dp", "fsdp"), axis=0, tiled=True),
        lax.all_gather(up_weight, ("dp", "fsdp"), axis=0, tiled=True),
        lax.all_gather(down_weight, ("dp", "fsdp"), axis=0, tiled=True),
    )
    seed = cotangent.astype(jnp.float32)
    grad_outer = (branch_scale * seed).astype(jnp.bfloat16)
    grad_down_bias = jnp.sum(grad_outer.astype(jnp.float32), axis=0)
    grad_down_weight = contract_rows(active, grad_outer)
    grad_active = contract_cols(grad_outer, mlp_back[2])
    grad_hidden = gelu_back(grad_active)[0].astype(jnp.bfloat16)
    grad_up_bias = jnp.sum(grad_hidden.astype(jnp.float32), axis=0)
    grad_up_weight = contract_rows(normed_two, grad_hidden)
    grad_normed_two = contract_cols(grad_hidden, mlp_back[1])
    _, norm_two_back = jax.vjp(scaled_norm, middle, mlp_back[0].astype(jnp.float32))
    grad_middle_part, grad_second_gain = norm_two_back(grad_normed_two)
    grad_second_offset = jnp.sum(grad_normed_two, axis=0)
    grad_middle = seed + grad_middle_part
    mlp_shares = (
        grad_second_gain,
        grad_second_offset,
        grad_up_weight,
        grad_up_bias,
        grad_down_weight,
        grad_down_bias,
    )
    attn_back = (
        lax.all_gather(first_gain, ("dp", "fsdp"), axis=0, tiled=True),
        lax.all_gather(qkv_weight, ("dp", "fsdp"), axis=0, tiled=True),
        lax.all_gather(out_weight, ("dp", "fsdp"), axis=0, tiled=True),
    )
    grad_branch = (branch_scale * grad_middle).astype(jnp.bfloat16)
    grad_out_bias = jnp.sum(grad_branch.astype(jnp.float32), axis=0)
    grad_out_weight = contract_rows(attended, grad_branch)
    grad_attended = contract_cols(grad_branch, attn_back[2]).astype(jnp.bfloat16).reshape(row_shape)
    grad_queries, grad_keys, grad_values = lax.map(
        lambda row_item: attend_row_back(*row_item),
        (queries, keys, values, doc_ids, logsums, grad_attended),
    )
    grad_projected = jnp.concatenate(
        [
            grad_queries.reshape(-1, model_width),
            grad_keys.reshape(-1, model_width),
            grad_values.reshape(-1, model_width),
        ],
        axis=1,
    ).astype(jnp.bfloat16)
    grad_wide = grad_projected.astype(jnp.float32)
    grad_query_bias = jnp.sum(grad_wide[:, :model_width], axis=0)
    grad_value_bias = jnp.sum(grad_wide[:, 2 * model_width :], axis=0)
    grad_qkv_weight = contract_rows(normed_one, grad_projected)
    grad_normed_one = contract_cols(grad_projected, attn_back[1])
    _, norm_one_back = jax.vjp(scaled_norm, inputs, attn_back[0].astype(jnp.float32))
    grad_input_part, grad_first_gain = norm_one_back(grad_normed_one)
    grad_first_offset = jnp.sum(grad_normed_one, axis=0)
    grad_tokens = grad_middle + grad_input_part
    every_share = (
        lax.psum_scatter(grad_second_gain, ("dp", "fsdp"), scatter_dimension=0, tiled=True),
        lax.psum_scatter(grad_second_offset, ("dp", "fsdp"), scatter_dimension=0, tiled=True),
        lax.psum_scatter(grad_up_weight, ("dp", "fsdp"), scatter_dimension=0, tiled=True),
        lax.psum_scatter(grad_up_bias, ("dp", "fsdp"), scatter_dimension=0, tiled=True),
        lax.psum_scatter(grad_down_weight, ("dp", "fsdp"), scatter_dimension=0, tiled=True),
        lax.psum_scatter(grad_down_bias, ("dp", "fsdp"), scatter_dimension=0, tiled=True),
        lax.psum_scatter(grad_first_gain, ("dp", "fsdp"), scatter_dimension=0, tiled=True),
        lax.psum_scatter(grad_first_offset, ("dp", "fsdp"), scatter_dimension=0, tiled=True),
        lax.psum_scatter(grad_qkv_weight, ("dp", "fsdp"), scatter_dimension=0, tiled=True),
        lax.psum_scatter(grad_query_bias, ("dp", "fsdp"), scatter_dimension=0, tiled=True),
        lax.psum_scatter(grad_value_bias, ("dp", "fsdp"), scatter_dimension=0, tiled=True),
        lax.psum_scatter(grad_out_weight, ("dp", "fsdp"), scatter_dimension=0, tiled=True),
        lax.psum_scatter(grad_out_bias, ("dp", "fsdp"), scatter_dimension=0, tiled=True),
    )
    mlp_shares = every_share[:6]
    attn_shares = every_share[6:]
    return (
        layer_out,
        grad_tokens,
        attn_shares[0],
        attn_shares[1],
        attn_shares[2],
        attn_shares[3],
        attn_shares[4],
        attn_shares[5],
        attn_shares[6],
        mlp_shares[0],
        mlp_shares[1],
        mlp_shares[2],
        mlp_shares[3],
        mlp_shares[4],
        mlp_shares[5],
    )


def solution(mesh):
    placed = (
        P(("dp", "fsdp"), None),
        P(("dp", "fsdp"), None),
        P(("dp", "fsdp"), None),
        P(("dp", "fsdp")),
        P(("dp", "fsdp")),
        P(("dp", "fsdp"), None),
        P(("dp", "fsdp")),
        P(("dp", "fsdp")),
        P(("dp", "fsdp"), None),
        P(("dp", "fsdp")),
        P(("dp", "fsdp")),
        P(("dp", "fsdp")),
        P(("dp", "fsdp"), None),
        P(("dp", "fsdp")),
        P(("dp", "fsdp"), None),
        P(("dp", "fsdp")),
    )
    return jax.shard_map(
        per_device,
        mesh=mesh,
        in_specs=placed,
        out_specs=(
            P(("dp", "fsdp"), None),
            P(("dp", "fsdp"), None),
            P(("dp", "fsdp")),
            P(("dp", "fsdp")),
            P(("dp", "fsdp"), None),
            P(("dp", "fsdp")),
            P(("dp", "fsdp")),
            P(("dp", "fsdp"), None),
            P(("dp", "fsdp")),
            P(("dp", "fsdp")),
            P(("dp", "fsdp")),
            P(("dp", "fsdp"), None),
            P(("dp", "fsdp")),
            P(("dp", "fsdp"), None),
            P(("dp", "fsdp")),
        ),
        check_vma=False,
    )
```

profile of v0, /device:TPU:0, one launch (start us, length us, event | category | flops | bytes accessed | tf_op | source)
XLA Modules:
  0.0 841.5 jit_solution(366811450142850498)
XLA Ops:
  18.3 42.8 %all-reduce.21 = (bf16[768]{0:T(1024)(128)(2,1)S(1)}, bf16[768]{0:T(1024)(128)(2,1)S(1)}, bf16[768]{0:T(1024)(128)(2,1)S(1)}, bf16[768]{0:T(1024)(128)(2,1)S(1)}...) all-reduce(bf16[768]{0:T(1024)(128)(2,1)S(1)} %dynamic-update-slice, ...), channel_id=1, replica_groups=mesh['dp'=4,'fsdp'=8] {'dp','fsdp'}, use_global_device_ids=true, to_apply=%add.6 | all-reduce | flops 9216 | bytes 36864
  68.8 5.3 all-gather.5.cloned.1.call-done
  74.1 6.3 fusion.79
  85.7 2.3 copy.77
  88.0 2.3 copy.81
  90.3 2.8 copy.82
  93.1 2.3 copy.78
  95.4 14.4 %fusion.15 = (f32[12,512]{1,0:T(8,128)S(1)}, f32[12,512,1024]{2,1,0:T(8,128)}) fusion(pred[512,1024]{1,0:T(8,128)(4,1)} %fusion.37, bf16[512,12,64]{0,2,1:T(8,128)(2,1)} %bitcast.74, bf16[1024,12,64]{0,2,1:T(8,128)(2,1)} %bitcast.70), kind=kOutput, calls=%fused_computation.30 | convolution fusion | flops 824174592 | bytes 28073984 | tf_op jit(solution)/shard_map/while/body/eval_jaxpr/qhd,khd->hqk/dot_general | solution.py:44
  109.8 11.9 %fusion = f32[12,512]{1,0:T(8,128)S(1)} fusion(f32[12,512]{1,0:T(8,128)S(1)} %get-tuple-element.151, f32[12,512,1024]{2,1,0:T(8,128)} %get-tuple-element.152, pred[512,1024]{1,0:T(8,128)(4,1)S(1)} %copy-done.12), kind=kLoop, calls=%fused_computation.6 | loop fusion | flops 25159680 | bytes 25739264 | tf_op jit(solution)/shard_map/while/body/eval_jaxpr/reduce_sum | solution.py:69
  123.8 2.6 fusion.13
  130.5 3.0 copy.80
  133.5 2.3 copy.76
  135.8 9.5 %fusion.43 = bf16[12,64,512]{2,1,0:T(8,128)(2,1)} fusion(bf16[512,12,64]{0,2,1:T(8,128)(2,1)} %bitcast.86, f32[12,512]{1,0:T(8,128)S(1)} %fusion.13, f32[12,512]{1,0:T(8,128)S(1)} %get-tuple-element.153, f32[12,512,512]{1,2,0:T(8,128)} %copy-done, pred[512,512]{0,1:T(8,128)(4,1)S(1)} %fusion.50), kind=kOutput, calls=%fused_computation.83 | convolution fusion | flops 418775040 | bytes 14467072 | tf_op jit(solution)/shard_map/while/body/eval_jaxpr/hqk,khd->qhd/dot_general | solution.py:72
  145.3 12.8 %fusion.44 = bf16[12,64,512]{2,1,0:T(8,128)(2,1)} fusion(bf16[1024,12,64]{0,2,1:T(8,128)(2,1)S(1)} %bitcast.81, f32[12,512]{1,0:T(8,128)S(1)} %fusion, f32[12,512]{1,0:T(8,128)S(1)} %get-tuple-element.151, f32[12,512,1024]{2,1,0:T(8,128)} %get-tuple-element.152, pred[512,1024]{1,0:T(8,128)(4,1)S(1)} %copy-done.13), kind=kOutput, calls=%fused_computation.84 | convolution fusion | flops 837156864 | bytes 28098560 | tf_op jit(solution)/shard_map/while/body/eval_jaxpr/hqk,khd->qhd/dot_general | solution.py:72
  158.0 3.5 fusion.80
  164.2 31.7 %all-gather.9.cloned.1.call-done = bf16[768,3072]{1,0:T(8,128)(2,1)} async-done(((bf16[24,3072]{1,0:T(8,128)(2,1)}), bf16[768,3072]{1,0:T(8,128)(2,1)}) %all-gather.9.cloned.1.call-update) | async-done | bytes 4718608 | tf_op jit(solution)/shard_map/all_gather | solution.py:173
  195.9 11.0 %fusion.74 = f32[1024,3072]{1,0:T(8,128)} fusion(bf16[768,3072]{1,0:T(8,128)(2,1)} %all-gather.9.cloned.1.call-done, f32[1024,768]{0,1:T(8,128)} %copy-done.3, f32[768]{0:T(1024)S(1)} %convert_element_type.122, f32[768]{0:T(1024)S(1)} %convert_element_type.121, f32[1024]{0:T(1024)S(1)} %fusion.54, f32[1024]{0:T(1024)S(1)} %broadcast_multiply_fusion), kind=kOutput, calls=%fused_computation.121 | convolution fusion | flops 4835770368 | bytes 20461568 | tf_op jit(solution)/shard_map/dot_general | solution.py:26
  206.9 54.4 %all-gather.11.cloned.1.call-done = bf16[3072,768]{1,0:T(8,128)(2,1)} async-done(((bf16[96,768]{1,0:T(8,128)(2,1)}), bf16[3072,768]{1,0:T(8,128)(2,1)}) %all-gather.11.cloned.1.call-update) | async-done | bytes 4718608 | tf_op jit(solution)/shard_map/all_gather | solution.py:175
  261.3 16.5 %convert_reduce_fusion = (f32[3072]{0:T(1024)}, bf16[1024,3072]{1,0:T(8,128)(2,1)S(1)}) fusion(f32[1024,3072]{1,0:T(8,128)} %fusion.74, f32[3072]{0:T(1024)S(1)} %copy-done.51, bf16[3072,768]{1,0:T(8,128)(2,1)} %all-gather.11.cloned.1.call-done, bf16[1024,768]{0,1:T(8,128)(2,1)S(1)} %copy.84), kind=kOutput, calls=%fused_computation.18 | convolution fusion | flops 4906546176 | bytes 25190400 | tf_op jit(solution)/shard_map/dot_general | solution.py:36
  277.8 7.3 fusion.82
  285.1 3.7 copy.85
  288.8 3.5 multiply_reduce_fusion.2
  295.7 2.8 fusion.51
  300.1 8.0 fusion.40
  308.2 6.9 multiply_reduce_fusion.1
  315.0 7.0 multiply_convert_fusion.1
  324.1 3.2 multiply_bitcast_fusion
  328.7 21.9 %multiply_reduce_fusion = (f32[12,512]{1,0:T(8,128)S(1)}, f32[12,512,1024]{2,1,0:T(8,128)}) fusion(f32[12,512]{1,0:T(8,128)S(1)} %log_add_fusion, f32[12,512,1024]{2,1,0:T(8,128)} %get-tuple-element.152, pred[512,1024]{1,0:T(8,128)(4,1)S(1)} %copy-done.14, bf16[512,12,64]{0,2,1:T(8,128)(2,1)S(1)} %bitcast.90, bf16[1024,12,64]{0,2,1:T(8,128)(2,1)S(1)} %bitcast.82), kind=kOutput, calls=%fused_computation.1 | convolution fusion | flops 836757504 | bytes 53264384 | tf_op jit(solution)/shard_map/while/body/eval_jaxpr/qhd,khd->hqk/dot_general | solution.py:92
  350.6 17.8 %multiply_convert_fusion = bf16[12,512,1024]{2,1,0:T(8,128)(2,1)S(1)} fusion(f32[12,512,1024]{2,1,0:T(8,128)} %get-tuple-element.160, f32[12,512]{1,0:T(8,128)S(1)} %get-tuple-element.159, f32[12,512]{1,0:T(8,128)S(1)} %log_add_fusion, f32[12,512,1024]{2,1,0:T(8,128)} %get-tuple-element.152, pred[512,1024]{1,0:T(8,128)(4,1)} %fusion.37), kind=kLoop, calls=%fused_computation | loop fusion | flops 37748736 | bytes 63488000 | tf_op jit(solution)/shard_map/while/body/eval_jaxpr/convert_element_type | solution.py:96
  368.4 6.3 fusion.45
  374.7 2.9 pad_maximum_fusion.2
  377.6 3.5 fusion.36
  381.1 12.9 %fusion.35 = bf16[1024,12,64]{0,2,1:T(8,128)(2,1)S(1)} fusion(f32[512,12,64]{0,2,1:T(8,128)} %fusion.40, bf16[512,12,64]{0,2,1:T(8,128)(2,1)} %bitcast.91, f32[12,512]{1,0:T(8,128)S(1)} %log_add_fusion, f32[12,512,1024]{2,1,0:T(8,128)} %get-tuple-element.152, pred[512,1024]{1,0:T(8,128)(4,1)S(1)} %copy-done.15), kind=kOutput, calls=%fused_computation.62 | convolution fusion | flops 832045056 | bytes 29646848 | tf_op jit(solution)/shard_map/while/body/eval_jaxpr/hqk,qhd->khd/dot_general | solution.py:112
  395.2 7.0 fusion.67
  403.7 14.0 %fusion.47 = f32[3072,768]{1,0:T(8,128)} fusion(bf16[1024,768]{0,1:T(8,128)(2,1)S(1)} %copy-done.11, f32[1024,3072]{1,0:T(8,128)} %fusion.74, f32[3072]{0:T(1024)S(1)} %copy-done.51), kind=kOutput, calls=%fused_computation.87 | convolution fusion | flops 4865654784 | bytes 23605248 | tf_op jit(solution)/shard_map/dot_general | solution.py:30
  418.3 10.8 %fusion.73 = f32[768,3072]{1,0:T(8,128)} fusion(bf16[1024,3072]{1,0:T(8,128)(2,1)} %copy-done.61, f32[1024,768]{0,1:T(8,128)} %copy-done.3, f32[768]{0:T(1024)S(1)} %copy-done.33, f32[768]{0:T(1024)S(1)} %convert_element_type.121, f32[1024]{0:T(1024)S(1)} %fusion.54, f32[1024]{0:T(1024)S(1)} %broadcast_multiply_fusion), kind=kOutput, calls=%fused_computation.120 | convolution fusion | flops 4835770368 | bytes 18888704 | tf_op jit(solution)/shard_map/dot_general | solution.py:30
  429.7 12.2 %add_convert_fusion = bf16[1024,768]{0,1:T(8,128)(2,1)} fusion(f32[1024,768]{0,1:T(8,128)} %copy-done.3, bf16[3072,768]{1,0:T(8,128)(2,1)} %all-gather.11.cloned.1.call-done, f32[768]{0:T(1024)S(1)} %convert_element_type.126, f32[1024,3072]{1,0:T(8,128)} %fusion.74, f32[3072]{0:T(1024)S(1)} %copy-done.51), kind=kOutput, calls=%fused_computation.71 | convolution fusion | flops 4866441216 | bytes 22035456 | tf_op jit(solution)/shard_map/dot_general | solution.py:26
  442.0 2.6 copy.92
  444.6 9.3 %fusion.81 = (f32[768]{0:T(1024)S(1)}, f32[1024,768]{1,0:T(8,128)}) fusion(bf16[768,2304]{1,0:T(8,128)(2,1)} %all-gather.5.cloned.1.call-done, bf16[1024,768]{0,1:T(8,128)(2,1)} %bitcast.93, bf16[1024,768]{0,1:T(8,128)(2,1)} %bitcast.76, bf16[1024,768]{0,1:T(8,128)(2,1)} %bitcast.83), kind=kOutput, calls=%fused_computation.128 | convolution fusion | flops 3638820096 | bytes 11406336 | tf_op jit(solution)/shard_map/dot_general | solution.py:36
  453.9 3.6 copy.89
  457.5 2.7 fusion.32
  460.6 2.7 fusion.71
  465.6 3.3 convert_reduce_fusion.2
  468.9 42.2 %all-reduce.20 = (f32[768]{0:T(1024)S(1)}, f32[768]{0:T(1024)S(1)}, f32[768]{0:T(1024)S(1)}, f32[768]{0:T(1024)S(1)}, f32[768]{0:T(1024)S(1)}, /*index=5*/f32[76...) all-reduce(f32[768]{0:T(1024)S(1)} %get-tuple-element.115, ...), channel_id=2, replica_groups=mesh['dp'=4,'fsdp'=8] {'dp','fsdp'}, use_global_device_ids=true, to_apply=%region_15.16.clone | all-reduce | flops 9216 | bytes 73728
  515.8 3.5 copy.93
  519.9 30.8 %reduce-scatter.5.cloned.1.call-done = f32[24,2304]{1,0:T(8,128)} async-done(((f32[768,2304]{1,0:T(8,128)}), f32[24,2304]{1,0:T(8,128)}) %reduce-scatter.5.cloned.1.call-update) | async-done | bytes 221200 | tf_op jit(solution)/shard_map/reduce_scatter | solution.py:250
  550.7 141.4 %reduce-scatter.11.cloned.1.call-done = f32[96,768]{1,0:T(8,128)} async-done(((f32[3072,768]{1,0:T(8,128)}), f32[96,768]{1,0:T(8,128)}) %reduce-scatter.11.cloned.1.call-update) | async-done | bytes 294928 | tf_op jit(solution)/shard_map/reduce_scatter | solution.py:246
  692.1 142.1 %reduce-scatter.9.cloned.1.call-done = f32[24,3072]{1,0:T(8,128)} async-done(((f32[768,3072]{1,0:T(8,128)}), f32[24,3072]{1,0:T(8,128)}) %reduce-scatter.9.cloned.1.call-update) | async-done | bytes 294928 | tf_op jit(solution)/shard_map/reduce_scatter | solution.py:244
  (217 shorter events, 52.8 us)
Async XLA Ops:
  7.2 66.9 %all-gather.5.cloned.1.call-start = ((), (), s32[]{:S(2)}) async-start(), calls=%async_computation.4 | async-start | bytes 3649536 | tf_op jit(solution)/shard_map/all_gather | solution.py:142
  7.9 150.1 %all-gather.7.cloned.1.call-start = ((), (), s32[]{:S(2)}) async-start(), calls=%async_computation.5 | async-start | bytes 1216512 | tf_op jit(solution)/shard_map/all_gather | solution.py:145
  8.7 187.2 %all-gather.9.cloned.1.call-start = ((), (), s32[]{:S(2)}) async-start(), calls=%async_computation.6 | async-start | bytes 4866048 | tf_op jit(solution)/shard_map/all_gather | solution.py:173
  9.4 251.9 %all-gather.11.cloned.1.call-start = ((), (), s32[]{:S(2)}) async-start(), calls=%async_computation.7 | async-start | bytes 4866048 | tf_op jit(solution)/shard_map/all_gather | solution.py:175
  10.0 509.9 %reduce-scatter.7.cloned.1.call-start = ((), (), s32[]{:S(2)}) async-start(), calls=%async_computation.9 | async-start | bytes 2433024 | tf_op jit(solution)/shard_map/reduce_scatter | solution.py:253
  61.7 12.4 %copy-start.38 = (f32[768]{0:T(1024)}, f32[768]{0:T(1024)S(1)}, u32[]{:S(2)}) copy-start(f32[768]{0:T(1024)S(1)} %convert_element_type.111) | copy-start | bytes 9220
  61.7 12.4 %copy-start.53 = (f32[768]{0:T(1024)}, f32[768]{0:T(1024)S(1)}, u32[]{:S(2)}) copy-start(f32[768]{0:T(1024)S(1)} %convert_element_type.112) | copy-start | bytes 9220
  61.7 134.2 %copy-start.32 = (f32[768]{0:T(1024)}, f32[768]{0:T(1024)S(1)}, u32[]{:S(2)}) copy-start(f32[768]{0:T(1024)S(1)} %convert_element_type.122) | copy-start | bytes 9220
  64.3 93.7 %copy-start.1 = (bf16[1024,768]{0,1:T(8,128)(2,1)}, bf16[1024,768]{0,1:T(8,128)(2,1)S(1)}, u32[]{:S(2)}) copy-start(bf16[1024,768]{0,1:T(8,128)(2,1)S(1)} %copy.75) | copy-start | bytes 4718596
  64.6 15.8 %copy-start.36 = (f32[1024]{0:T(1024)}, f32[1024]{0:T(1024)S(1)}, u32[]{:S(2)}) copy-start(f32[1024]{0:T(1024)S(1)} %broadcast_multiply_fusion.1) | copy-start | bytes 12292
  65.7 14.8 %copy-start.40 = (f32[1024]{0:T(1024)}, f32[1024]{0:T(1024)S(1)}, u32[]{:S(2)}) copy-start(f32[1024]{0:T(1024)S(1)} %fusion.53) | copy-start | bytes 12292
  67.4 193.9 %copy-start.9 = (bf16[1024,768]{0,1:T(8,128)(2,1)}, bf16[1024,768]{0,1:T(8,128)(2,1)S(1)}, u32[]{:S(2)}) copy-start(bf16[1024,768]{0,1:T(8,128)(2,1)S(1)} %copy.84) | copy-start | bytes 4718596
  95.4 14.4 %copy-start.12 = (pred[512,1024]{1,0:T(8,128)(4,1)S(1)}, pred[512,1024]{1,0:T(8,128)(4,1)}, u32[]{:S(2)}) copy-start(pred[512,1024]{1,0:T(8,128)(4,1)} %fusion.37) | copy-start | bytes 1572868
  109.8 11.9 %copy-start.16 = (bf16[512,768]{0,1:T(8,128)(2,1)S(1)}, bf16[512,768]{0,1:T(8,128)(2,1)}, u32[]{:S(2)}) copy-start(bf16[512,768]{0,1:T(8,128)(2,1)} %copy.78) | copy-start | bytes 2359300
  109.8 11.9 %copy-start.21 = (bf16[512,768]{0,1:T(8,128)(2,1)S(1)}, bf16[512,768]{0,1:T(8,128)(2,1)}, u32[]{:S(2)}) copy-start(bf16[512,768]{0,1:T(8,128)(2,1)} %copy.77) | copy-start | bytes 2359300
  123.8 4.6 copy-start
  128.4 7.4 copy-start.34
  135.8 9.5 %copy-start.13 = (pred[512,1024]{1,0:T(8,128)(4,1)S(1)}, pred[512,1024]{1,0:T(8,128)(4,1)}, u32[]{:S(2)}) copy-start(pred[512,1024]{1,0:T(8,128)(4,1)} %fusion.37) | copy-start | bytes 1572868
  135.8 9.5 %copy-start.23 = (bf16[1024,768]{0,1:T(8,128)(2,1)S(1)}, bf16[1024,768]{0,1:T(8,128)(2,1)}, u32[]{:S(2)}) copy-start(bf16[1024,768]{0,1:T(8,128)(2,1)} %copy.80) | copy-start | bytes 4718596
  145.3 12.8 %copy-start.55 = (f32[768]{0:T(1024)S(1)}, f32[768]{0:T(1024)}, u32[]{:S(2)}) copy-start(f32[768]{0:T(1024)} %convert_element_type.120) | copy-start | bytes 9220
  164.2 97.1 %copy-start.51 = (f32[3072]{0:T(1024)S(1)}, f32[3072]{0:T(1024)}, u32[]{:S(2)}) copy-start(f32[3072]{0:T(1024)} %convert_element_type.124) | copy-start | bytes 36868
  261.3 16.5 %copy-start.28 = (bf16[768,3072]{1,0:T(8,128)(2,1)S(1)}, bf16[768,3072]{1,0:T(8,128)(2,1)}, u32[]{:S(2)}) copy-start(bf16[768,3072]{1,0:T(8,128)(2,1)} %all-gather.9.cloned.1.call-done) | copy-start | bytes 14155780
  277.8 7.3 copy-start.61
  285.1 3.7 copy-start.4
  288.8 3.5 copy-start.47
  288.8 3.5 copy-start.8
  298.6 9.6 %slice-start = ((s8[12582912]{0:T(1024)(128)(4,1)}), s8[4194304]{0:T(1024)(128)(4,1)S(1)}, s32[]{:S(2)}) async-start(s8[12582912]{0:T(1024)(128)(4,1)} %bitcast.68), calls=%async_computation.12 | async-start | bytes 8388608
  300.0 8.2 slice-start.1
  300.1 27.3 %copy-start.30 = (bf16[512,768]{0,1:T(8,128)(2,1)}, bf16[512,768]{0,1:T(8,128)(2,1)S(1)}, u32[]{:S(2)}) copy-start(bf16[512,768]{0,1:T(8,128)(2,1)S(1)} %get-tuple-element.143) | copy-start | bytes 2359300
  300.1 8.0 slice-start.2
  300.1 8.0 copy-start.29
  315.0 7.1 copy-start.17
  324.1 3.3 copy-start.14
  327.3 223.4 %reduce-scatter.5.cloned.1.call-start = ((), (), s32[]{:S(2)}) async-start(), calls=%async_computation.8 | async-start | bytes 7299072 | tf_op jit(solution)/shard_map/reduce_scatter | solution.py:250
  377.6 3.5 copy-start.15
  381.1 14.1 %copy-start.2 = (bf16[1024,768]{0,1:T(8,128)(2,1)S(1)}, bf16[1024,768]{0,1:T(8,128)(2,1)}, u32[]{:S(2)}) copy-start(bf16[1024,768]{0,1:T(8,128)(2,1)} %copy-done.1) | copy-start | bytes 4718596
  381.1 14.1 %copy-start.19 = (bf16[1024,12,64]{0,2,1:T(8,128)(2,1)S(1)}, bf16[1024,12,64]{0,2,1:T(8,128)(2,1)}, u32[]{:S(2)}) copy-start(bf16[1024,12,64]{0,2,1:T(8,128)(2,1)} %fusion.36) | copy-start | bytes 4718596
  381.1 14.1 %copy-start.25 = (bf16[1024,12,64]{0,2,1:T(8,128)(2,1)S(1)}, bf16[1024,12,64]{0,2,1:T(8,128)(2,1)}, u32[]{:S(2)}) copy-start(bf16[1024,12,64]{0,2,1:T(8,128)(2,1)} %pad_maximum_fusion.2) | copy-start | bytes 4718596
  381.1 14.1 %copy-start.37 = (f32[1024]{0:T(1024)S(1)}, f32[1024]{0:T(1024)}, u32[]{:S(2)}) copy-start(f32[1024]{0:T(1024)} %copy-done.36) | copy-start | bytes 12292
  381.1 14.1 %copy-start.39 = (f32[768]{0:T(1024)S(1)}, f32[768]{0:T(1024)}, u32[]{:S(2)}) copy-start(f32[768]{0:T(1024)} %copy-done.38) | copy-start | bytes 9220
  381.1 14.1 %copy-start.41 = (f32[1024]{0:T(1024)S(1)}, f32[1024]{0:T(1024)}, u32[]{:S(2)}) copy-start(f32[1024]{0:T(1024)} %copy-done.40) | copy-start | bytes 12292
  381.1 14.1 %copy-start.54 = (f32[768]{0:T(1024)S(1)}, f32[768]{0:T(1024)}, u32[]{:S(2)}) copy-start(f32[768]{0:T(1024)} %copy-done.53) | copy-start | bytes 9220
  402.3 289.8 %reduce-scatter.11.cloned.1.call-start = ((), (), s32[]{:S(2)}) async-start(), calls=%async_computation.11 | async-start | bytes 9732096 | tf_op jit(solution)/shard_map/reduce_scatter | solution.py:246
  417.7 416.5 %reduce-scatter.9.cloned.1.call-start = ((), (), s32[]{:S(2)}) async-start(), calls=%async_computation.10 | async-start | bytes 9732096 | tf_op jit(solution)/shard_map/reduce_scatter | solution.py:244
  465.5 3.4 copy-start.49
  465.5 3.4 copy-start.50
  465.6 3.4 copy-start.52
  465.6 3.4 copy-start.56
  (25 other events, 48.9 us)
Sparse Core Ops, SparseCore 0:
  11.0 63.0 all-gather.4
  77.1 53.0 all-gather.6
  133.2 62.6 all-gather.8
  198.8 62.4 all-gather.10
  327.4 97.8 reduce-scatter.6
  432.4 118.3 reduce-scatter.4
  557.2 134.8 reduce-scatter.10
  699.6 134.5 reduce-scatter.8
where the time goes:
time: 850 us; the launch traced here: 841 us
  waiting for transfers between devices  408 us (48%)
  matrix products  205 us (24%)
  blocking collectives  85 us (10%)
  other arithmetic  64.5 us (8%)
  local copies, waits for them, and re-layouts  62.7 us (7%)
  between operations  15.3 us (2%)
    reduce_scatter x1, waiting for transfers between devices, per_device(): lax.psum_scatter(grad_up_weight, ('dp', 'fsdp'), scatter_dimension=0, til...  142 us
    reduce_scatter x1, waiting for transfers between devices, per_device(): lax.psum_scatter(grad_down_weight, ('dp', 'fsdp'), scatter_dimension=0, t...  141 us
    unnamed x2, blocking collectives  85 us
    all_gather x1, waiting for transfers between devices, per_device(): lax.all_gather(down_weight, ('dp', 'fsdp'), axis=0, tiled=True)  54.4 us
    dot_general x4, matrix products, contract_rows(): lax.dot_general(former, latter, (((0,), (0,)), ((), ())), preferred_eleme...  34.6 us
    dot_general x4, matrix products, contract_cols(): lax.dot_general(former, latter, (((1,), (1,)), ((), ())), preferred_eleme...  34.4 us
    unnamed x161, local copies, waits for them, and re-layouts  34 us
    dot_general x4, matrix products, dense(): return jnp.dot(former, latter, preferred_element_type=jnp.float32)  33 us
  transfers between devices with their start and end apart: 8, of which 6 were waited for; matrix products, arithmetic and copies ran while one was open for 30% of the time, Pallas kernels for 0%

commit v1 on v0

--- a/solution.py
+++ b/solution.py
@@ -1,6 +1,8 @@
 import jax
 import jax.numpy as jnp
 from jax import lax
+from jax.experimental import pallas as pl
+from jax.experimental.pallas import tpu as pltpu
 from jax.sharding import PartitionSpec as P
 
 HEADS = 12
@@ -118,7 +120,457 @@
     return (jnp.concatenate(query_parts, axis=0), grad_keys, grad_values)
 
 
-def per_device(
+MESH = pl.DeviceIdType.MESH
+WIDTH = 768
+HIDDEN = 3072
+CHIPS = 16
+CORES = 2
+VMEM_LIMIT = 60 * 2**20
+
+UNITS = (
+    ("qkv", 0, 384, 384),
+    ("qkv", 768, 384, 384),
+    ("qkv", 1536, 384, 384),
+    ("out", 0, 384, 384),
+    ("up", 0, 384, 384),
+    ("up", 768, 384, 384),
+    ("up", 1536, 384, 384),
+    ("up", 2304, 384, 384),
+    ("down", 0, 384, 128),
+    ("down", 128, 384, 128),
+    ("down", 256, 384, 128),
+)
+SHARD_ROWS = {"qkv": 24, "out": 24, "up": 24, "down": 96}
+COLUMNS = {"qkv": 2304, "out": 768, "up": 3072, "down": 768}
+NAMES = ("qkv", "out", "up", "down")
+
+
+def fits(mesh):
+    return mesh.shape["dp"] == 4 and mesh.shape["fsdp"] == 8
+
+
+def padded(rows):
+    return -(-rows // 16) * 16
+
+
+class Place:
+    def __init__(self):
+        self.dp = lax.axis_index("dp")
+        self.fsdp = lax.axis_index("fsdp")
+        self.core = lax.rem(self.fsdp, 2)
+        self.z = lax.div(self.fsdp, 2)
+        x = lax.rem(self.dp, 2)
+        y = lax.div(self.dp, 2)
+        self.dp_x = y * 2 + (1 - x)
+        self.dp_y = (1 - y) * 2 + x
+        self.dp_far = 3 - self.dp
+        core = self.core
+        self.near = self.dp_x * (1 - core) + self.dp_y * core
+        self.next = self.dp_y * (1 - core) + self.dp_x * core
+        self.chip = self.dp * 4 + self.z
+        self.partner = (self.dp, self.z * 2 + (1 - core))
+        self.at_near = (self.near, self.fsdp)
+        self.at_next = (self.next, self.fsdp)
+
+    def along_z(self, step):
+        z = lax.rem(self.z + step, 4)
+        return (self.dp, z * 2 + self.core)
+
+    def greet(self):
+        barrier = pltpu.get_barrier_semaphore()
+        others = [self.partner, (self.dp_x, self.fsdp), (self.dp_y, self.fsdp), (self.dp_far, self.fsdp)]
+        others += [self.along_z(step) for step in (1, 2, 3)]
+        for other in others:
+            pl.semaphore_signal(barrier, inc=1, device_id=other, device_id_type=MESH)
+        pl.semaphore_wait(barrier, len(others))
+
+
+def send(source, target, sems, index, device):
+    copy = pltpu.make_async_remote_copy(
+        src_ref=source,
+        dst_ref=target,
+        send_sem=sems[0].at[index],
+        recv_sem=sems[1].at[index],
+        device_id=device,
+        device_id_type=MESH,
+    )
+    copy.start()
+    return copy
+
+
+def aligned(value, step):
+    return pl.multiple_of(value, step)
+
+
+class SmallSum:
+    STAGES = 3
+
+    def __init__(self, place, buffers, landed, sems):
+        self.place, self.buffers, self.landed, self.sems = place, buffers, landed, sems
+
+    @staticmethod
+    def scratch():
+        return [
+            pltpu.VMEM((3, 16, WIDTH), jnp.float32),
+            pltpu.VMEM((7, 16, WIDTH), jnp.float32),
+            pltpu.SemaphoreType.DMA((7,)),
+            pltpu.SemaphoreType.DMA((7,)),
+        ]
+
+    def begin(self, value):
+        self.buffers[0] = value
+        p = self.place
+        self.copies = [send(self.buffers.at[0], self.landed.at[0], self.sems, 0, p.partner)]
+
+    def middle(self):
+        p = self.place
+        self.copies[0].wait()
+        self.buffers[1] = self.buffers[0] + self.landed[0]
+        self.copies = [
+            send(self.buffers.at[1], self.landed.at[1 + i], self.sems, 1 + i, (dp, p.fsdp))
+            for i, dp in enumerate((p.dp_x, p.dp_y, p.dp_far))
+        ]
+
+    def last(self):
+        p = self.place
+        for copy in self.copies:
+            copy.wait()
+        self.buffers[2] = (self.buffers[1] + self.landed[1]) + (self.landed[2] + self.landed[3])
+        self.copies = [
+            send(self.buffers.at[2], self.landed.at[4 + i], self.sems, 4 + i, p.along_z(1 + i)) for i in range(3)
+        ]
+
+    def end(self):
+        for copy in self.copies:
+            copy.wait()
+        return (self.buffers[2] + self.landed[4]) + (self.landed[5] + self.landed[6])
+
+
+class GatherUnit:
+    SEMS = 11
+
+    def __init__(self, place, unit, shard, full, pair_out, pair_in, send_sems, recv_sems):
+        self.place = place
+        name, first, step, self.width = unit
+        self.rows = SHARD_ROWS[name]
+        self.shard, self.full = shard, full
+        self.mine = aligned(first + step * place.core, 128)
+        self.other = aligned(first + step * (1 - place.core), 128)
+        self.pair_out, self.pair_in = pair_out, pair_in
+        self.sems = (send_sems, recv_sems)
+        self.sent = []
+
+    def group(self, dp):
+        rows = 8 * self.rows
+        return self.full.at[pl.ds(aligned(dp * rows, 16), rows), pl.ds(self.mine, self.width)]
+
+    def push(self, view, index, device):
+        copy = send(view, view, self.sems, index, device)
+        self.sent.append(copy)
+        return copy
+
+    def pair(self):
+        self.pair_out[0 : self.rows] = self.shard[:, pl.ds(self.other, self.width)]
+        if self.rows % 16:
+            rest = padded(self.rows) - self.rows
+            self.pair_out[self.rows :] = jnp.zeros((rest, self.width), jnp.bfloat16)
+        self.pair_copy = send(self.pair_out, self.pair_in, self.sems, 0, self.place.partner)
+
+    def along_z(self):
+        p = self.place
+        self.pair_copy.wait()
+        own = self.shard[:, pl.ds(self.mine, self.width)].astype(jnp.float32)
+        came = self.pair_in[0 : self.rows].astype(jnp.float32)
+        first = p.core == 0
+        block = jnp.concatenate([jnp.where(first, own, came), jnp.where(first, came, own)], axis=0)
+        row = aligned(p.chip * (2 * self.rows), 16)
+        view = self.full.at[pl.ds(row, 2 * self.rows), pl.ds(self.mine, self.width)]
+        view[...] = block.astype(jnp.bfloat16)
+        self.z_copies = [self.push(view, step, p.along_z(step)) for step in (1, 2, 3)]
+
+    def to_near(self):
+        p = self.place
+        for copy in self.z_copies:
+            copy.wait_recv()
+        own = self.group(p.dp)
+        self.near_copy = self.push(own, 4, p.at_near)
+        self.next_copies = [self.push(own, 5, p.at_next)]
+        self.core_copies = [self.push(own, 7, p.partner)]
+
+    def to_next(self):
+        p = self.place
+        self.near_copy.wait_recv()
+        came = self.group(p.near)
+        self.next_copies.append(self.push(came, 6, p.at_next))
+        self.core_copies.append(self.push(came, 8, p.partner))
+
+    def to_core(self):
+        p = self.place
+        for copy, dp, index in zip(self.next_copies, (p.next, p.dp_far), (9, 10)):
+            copy.wait_recv()
+            self.core_copies.append(self.push(self.group(dp), index, p.partner))
+
+    def arrived(self):
+        for copy in self.core_copies:
+            copy.wait_recv()
+
+    def finish(self):
+        for copy in self.sent:
+            copy.wait_send()
+
+
+class ScatterUnit:
+    SEMS = 8
+
+    def __init__(self, place, unit, partial, target, halves, from_next, from_near, from_z, pair, send_sems, recv_sems):
+        self.place = place
+        name, first, step, self.width = unit
+        self.rows = SHARD_ROWS[name]
+        self.partial, self.target = partial, target
+        self.mine = aligned(first + step * place.core, 128)
+        self.other = aligned(first + step * (1 - place.core), 128)
+        self.halves, self.from_next, self.from_near, self.from_z, self.pair_buffer = (
+            halves,
+            from_next,
+            from_near,
+            from_z,
+            pair,
+        )
+        self.sems = (send_sems, recv_sems)
+        self.sent = []
+
+    @staticmethod
+    def scratch(unit):
+        name, _, _, width = unit
+        rows = SHARD_ROWS[name]
+        return [
+            pltpu.VMEM((32 * rows, width), jnp.bfloat16),
+            pltpu.VMEM((2, 8 * rows, width), jnp.bfloat16),
+            pltpu.VMEM((8 * rows, width), jnp.bfloat16),
+            pltpu.VMEM((3, 2 * rows, width), jnp.bfloat16),
+            pltpu.VMEM((3, rows, width), jnp.float32),
+        ]
+
+    def push(self, source, target, index, device):
+        copy = send(source, target, self.sems, index, device)
+        self.sent.append(copy)
+        return copy
+
+    def group(self, dp):
+        rows = 8 * self.rows
+        return self.halves.at[pl.ds(aligned(dp * rows, 16), rows)]
+
+    def to_partner(self):
+        source = self.partial.at[:, pl.ds(self.other, self.width)]
+        self.copies = [self.push(source, self.halves, 0, self.place.partner)]
+
+    def landed(self):
+        for copy in self.copies:
+            copy.wait_recv()
+
+    def add(self, former, latter, rows):
+        step = 48 if rows % 48 == 0 else 64
+
+        def body(index, carry):
+            at = pl.ds(aligned(index * step, 16), step)
+            former[at] = (former[at].astype(jnp.float32) + latter(at).astype(jnp.float32)).astype(jnp.bfloat16)
+            return carry
+
+        lax.fori_loop(0, rows // step, body, 0)
+
+    def to_next(self):
+        p = self.place
+        self.landed()
+        self.add(self.halves, lambda at: self.partial[at, pl.ds(self.mine, self.width)], 32 * self.rows)
+        self.copies = [
+            self.push(self.group(dp), self.from_next.at[i], 1 + i, p.at_next)
+            for i, dp in enumerate((p.next, p.dp_far))
+        ]
+
+    def to_near(self):
+        p = self.place
+        self.landed()
+        self.add(self.group(p.near), lambda at: self.from_next[1, at], 8 * self.rows)
+        self.copies = [self.push(self.group(p.near), self.from_near, 3, p.at_near)]
+        self.add(self.group(p.dp), lambda at: self.from_next[0, at], 8 * self.rows)
+
+    def along_z(self):
+        p = self.place
+        self.landed()
+        own = self.group(p.dp)
+        self.add(own, lambda at: self.from_near[at], 8 * self.rows)
+        self.copies = []
+        for step in (1, 2, 3):
+            z = lax.rem(p.z + step, 4)
+            view = own.at[pl.ds(aligned(z * (2 * self.rows), 16), 2 * self.rows)]
+            self.copies.append(self.push(view, self.from_z.at[step - 1], 3 + step, p.along_z(step)))
+
+    def to_pair(self):
+        p = self.place
+        self.landed()
+        rows = self.rows
+        own = self.halves[pl.ds(aligned(p.chip * (2 * rows), 16), 2 * rows)].astype(jnp.float32)
+        came = [self.from_z[i].astype(jnp.float32) for i in range(3)]
+        block = (own + came[0]) + (came[1] + came[2])
+        first = p.core == 0
+        self.pair_buffer[0] = jnp.where(first, block[rows:], block[:rows])
+        self.pair_buffer[1] = jnp.where(first, block[:rows], block[rows:])
+        self.copies = [self.push(self.pair_buffer.at[0], self.pair_buffer.at[2], 7, p.partner)]
+
+    def store(self):
+        self.landed()
+        self.target[:, pl.ds(self.mine, self.width)] = self.pair_buffer[1]
+        self.target[:, pl.ds(self.other, self.width)] = self.pair_buffer[2]
+
+    def finish(self):
+        for copy in self.sent:
+            copy.wait_send()
+
+
+def staggered(units, stages):
+    for tick in range(len(units) + len(stages) - 1):
+        for late in range(len(stages) - 1, -1, -1):
+            index = tick - late
+            if 0 <= index < len(units):
+                getattr(units[index], stages[late])()
+
+
+def gather_kernel(*refs):
+    shards, refs = dict(zip(NAMES, refs[:4])), refs[4:]
+    small, refs = refs[0], refs[1:]
+    fulls, refs = dict(zip(NAMES, refs[:4])), refs[4:]
+    small_out, refs = refs[0], refs[1:]
+    buffers, refs = refs[: 2 * len(UNITS)], refs[2 * len(UNITS) :]
+    send_sems, recv_sems, *small_refs = refs
+    place = Place()
+    units = [
+        GatherUnit(
+            place, unit, shards[unit[0]], fulls[unit[0]], buffers[2 * i], buffers[2 * i + 1], send_sems.at[i], recv_sems.at[i]
+        )
+        for i, unit in enumerate(UNITS)
+    ]
+    place.greet()
+    vector = SmallSum(place, small_refs[0], small_refs[1], small_refs[2:])
+    vector.begin(small[...])
+    for unit in units:
+        unit.pair()
+    vector.middle()
+    units[0].along_z()
+    units[1].along_z()
+    vector.last()
+    count = len(units)
+    stages = ("to_near", "to_next", "to_core", "arrived")
+    for tick in range(count + 3):
+        if 2 <= tick + 2 < count:
+            units[tick + 2].along_z()
+        for late, stage in enumerate(stages):
+            if 0 <= tick - late < count:
+                getattr(units[tick - late], stage)()
+        if tick == 0:
+            small_out[...] = vector.end()
+    for unit in units:
+        unit.finish()
+
+
+def gather(shards, small):
+    vmem = pl.BlockSpec(memory_space=pltpu.VMEM)
+    scratch = []
+    for name, _, _, width in UNITS:
+        scratch += [pltpu.VMEM((padded(SHARD_ROWS[name]), width), jnp.bfloat16)] * 2
+    scratch += [pltpu.SemaphoreType.DMA((len(UNITS), GatherUnit.SEMS))] * 2
+    out_shape = [jax.ShapeDtypeStruct((32 * SHARD_ROWS[n], COLUMNS[n]), jnp.bfloat16) for n in NAMES]
+    out_shape.append(jax.ShapeDtypeStruct((16, WIDTH), jnp.float32))
+    return pl.pallas_call(
+        gather_kernel,
+        name="gather_weights",
+        out_shape=out_shape,
+        in_specs=[vmem] * 5,
+        out_specs=[vmem] * 5,
+        scratch_shapes=scratch + SmallSum.scratch(),
+        compiler_params=pltpu.CompilerParams(collective_id=0, has_side_effects=True, vmem_limit_bytes=VMEM_LIMIT),
+    )(*[shards[n] for n in NAMES], small)
+
+
+SCATTER_ORDER = (8, 9, 10, 4, 5, 6, 7, 3, 0, 1, 2)
+
+
+def scatter_kernel(*refs):
+    partials, refs = dict(zip(NAMES, refs[:4])), refs[4:]
+    small, refs = refs[0], refs[1:]
+    targets, refs = dict(zip(NAMES, refs[:4])), refs[4:]
+    small_out, refs = refs[0], refs[1:]
+    buffers, refs = refs[: 5 * len(UNITS)], refs[5 * len(UNITS) :]
+    send_sems, recv_sems, *small_refs = refs
+    place = Place()
+    units = []
+    for i in SCATTER_ORDER:
+        name = UNITS[i][0]
+        units.append(
+            ScatterUnit(
+                place, UNITS[i], partials[name], targets[name], *buffers[5 * i : 5 * i + 5], send_sems.at[i], recv_sems.at[i]
+            )
+        )
+    place.greet()
+    vector = SmallSum(place, small_refs[0], small_refs[1], small_refs[2:])
+    vector.begin(small[...])
+    units[0].to_partner()
+    vector.middle()
+    units[1].to_partner()
+    vector.last()
+    count = len(units)
+    stages = ("to_next", "to_near", "along_z", "to_pair", "store")
+    for tick in range(count + len(stages) - 1):
+        if tick + 2 < count:
+            units[tick + 2].to_partner()
+        for late, stage in enumerate(stages):
+            if 0 <= tick - late < count:
+                getattr(units[tick - late], stage)()
+        if tick == 0:
+            small_out[...] = vector.end()
+    for unit in units:
+        unit.finish()
+
+
+def scatter(partials, small):
+    vmem = pl.BlockSpec(memory_space=pltpu.VMEM)
+    scratch = []
+    for unit in UNITS:
+        scratch += ScatterUnit.scratch(unit)
+    scratch += [pltpu.SemaphoreType.DMA((len(UNITS), ScatterUnit.SEMS))] * 2
+    out_shape = [jax.ShapeDtypeStruct((SHARD_ROWS[n], COLUMNS[n]), jnp.float32) for n in NAMES]
+    out_shape.append(jax.ShapeDtypeStruct((16, WIDTH), jnp.float32))
+    return pl.pallas_call(
+        scatter_kernel,
+        name="scatter_gradients",
+        out_shape=out_shape,
+        in_specs=[vmem] * 5,
+        out_specs=[vmem] * 5,
+        scratch_shapes=scratch + SmallSum.scratch(),
+        compiler_params=pltpu.CompilerParams(collective_id=1, has_side_effects=True, vmem_limit_bytes=VMEM_LIMIT),
+    )(*[partials[n] for n in NAMES], small)
+
+
+def device_number():
+    return lax.axis_index("dp") * 8 + lax.axis_index("fsdp")
+
+
+def spread(vectors, hidden_vector):
+    number = device_number()
+    stacked = jnp.stack([v.astype(jnp.float32) for v in vectors])
+    placed = lax.dynamic_update_slice(jnp.zeros((16, WIDTH), jnp.float32), stacked, (0, 24 * number))
+    return lax.dynamic_update_slice(
+        placed, hidden_vector.astype(jnp.float32)[None], (8 + number // 8, 96 * (number % 8))
+    )
+
+
+def own_parts(total):
+    number = device_number()
+    parts = lax.dynamic_slice(total[:8], (0, 24 * number), (8, 24))
+    hidden_part = lax.dynamic_slice(total, (8 + number // 8, 96 * (number % 8)), (1, 96))
+    return [parts[i] for i in range(8)], hidden_part[0]
+
+
+def plain_device(
     tokens,
     doc_ids,
     cotangent,
@@ -274,6 +726,157 @@
     )
 
 
+def fast_device(
+    tokens,
+    doc_ids,
+    cotangent,
+    first_gain,
+    first_offset,
+    qkv_weight,
+    query_bias,
+    value_bias,
+    out_weight,
+    out_bias,
+    second_gain,
+    second_offset,
+    up_weight,
+    up_bias,
+    down_weight,
+    down_bias,
+):
+    shards = {"qkv": qkv_weight, "out": out_weight, "up": up_weight, "down": down_weight}
+    vectors = (
+        first_gain,
+        first_offset,
+        query_bias,
+        value_bias,
+        out_bias,
+        second_gain,
+        second_offset,
+        down_bias,
+    )
+    qkv_full, out_full, up_full, down_full, small = gather(shards, spread(vectors, up_bias))
+    attn_full = (small[0], small[1], qkv_full, small[2], small[3], out_full, small[4])
+    mlp_full = (small[5], small[6], up_full, small[8:12].reshape(-1), down_full, small[7])
+    attn_back = (small[0], qkv_full, out_full)
+    mlp_back = (small[5], up_full, down_full)
+    model_width = tokens.shape[1]
+    rows_here = doc_ids.shape[0]
+    seq_len = doc_ids.shape[1]
+    inputs = tokens.astype(jnp.float32)
+    gain_one = attn_full[0].astype(jnp.float32)
+    normed_one = layer_norm(inputs, gain_one, attn_full[1].astype(jnp.float32)).astype(jnp.bfloat16)
+    projected = dense(normed_one, attn_full[2])
+    queries = (projected[:, :model_width] + attn_full[3].astype(jnp.float32)).astype(jnp.bfloat16)
+    keys = projected[:, model_width : 2 * model_width].astype(jnp.bfloat16)
+    values = (projected[:, 2 * model_width :] + attn_full[4].astype(jnp.float32)).astype(
+        jnp.bfloat16
+    )
+    row_shape = (rows_here, seq_len, HEADS, HEAD_DIM)
+    queries = queries.reshape(row_shape)
+    keys = keys.reshape(row_shape)
+    values = values.reshape(row_shape)
+    attended, logsums = lax.map(
+        lambda row_item: attend_row(*row_item), (queries, keys, values, doc_ids)
+    )
+    attended = attended.reshape(-1, model_width)
+    branch = dense(attended, attn_full[5]) + attn_full[6].astype(jnp.float32)
+    middle = inputs + branch_scale * branch
+    gain_two = mlp_full[0].astype(jnp.float32)
+    normed_two = layer_norm(middle, gain_two, mlp_full[1].astype(jnp.float32)).astype(jnp.bfloat16)
+    hidden = dense(normed_two, mlp_full[2]) + mlp_full[3].astype(jnp.float32)
+    active, gelu_back = jax.vjp(lambda pre_act: jax.nn.gelu(pre_act, approximate=True), hidden)
+    active = active.astype(jnp.bfloat16)
+    outer = dense(active, mlp_full[4]) + mlp_full[5].astype(jnp.float32)
+    layer_out = (middle + branch_scale * outer).astype(jnp.bfloat16)
+    seed = cotangent.astype(jnp.float32)
+    grad_outer = (branch_scale * seed).astype(jnp.bfloat16)
+    grad_down_bias = jnp.sum(grad_outer.astype(jnp.float32), axis=0)
+    grad_down_weight = contract_rows(active, grad_outer)
+    grad_active = contract_cols(grad_outer, mlp_back[2])
+    grad_hidden = gelu_back(grad_active)[0].astype(jnp.bfloat16)
+    grad_up_bias = jnp.sum(grad_hidden.astype(jnp.float32), axis=0)
+    grad_up_weight = contract_rows(normed_two, grad_hidden)
+    grad_normed_two = contract_cols(grad_hidden, mlp_back[1])
+    _, norm_two_back = jax.vjp(scaled_norm, middle, mlp_back[0].astype(jnp.float32))
+    grad_middle_part, grad_second_gain = norm_two_back(grad_normed_two)
+    grad_second_offset = jnp.sum(grad_normed_two, axis=0)
+    grad_middle = seed + grad_middle_part
+    mlp_shares = (
+        grad_second_gain,
+        grad_second_offset,
+        grad_up_weight,
+        grad_up_bias,
+        grad_down_weight,
+        grad_down_bias,
+    )
+    grad_branch = (branch_scale * grad_middle).astype(jnp.bfloat16)
+    grad_out_bias = jnp.sum(grad_branch.astype(jnp.float32), axis=0)
+    grad_out_weight = contract_rows(attended, grad_branch)
+    grad_attended = contract_cols(grad_branch, attn_back[2]).astype(jnp.bfloat16).reshape(row_shape)
+    grad_queries, grad_keys, grad_values = lax.map(
+        lambda row_item: attend_row_back(*row_item),
+        (queries, keys, values, doc_ids, logsums, grad_attended),
+    )
+    grad_projected = jnp.concatenate(
+        [
+            grad_queries.reshape(-1, model_width),
+            grad_keys.reshape(-1, model_width),
+            grad_values.reshape(-1, model_width),
+        ],
+        axis=1,
+    ).astype(jnp.bfloat16)
+    grad_wide = grad_projected.astype(jnp.float32)
+    grad_query_bias = jnp.sum(grad_wide[:, :model_width], axis=0)
+    grad_value_bias = jnp.sum(grad_wide[:, 2 * model_width :], axis=0)
+    grad_qkv_weight = contract_rows(normed_one, grad_projected)
+    grad_normed_one = contract_cols(grad_projected, attn_back[1])
+    _, norm_one_back = jax.vjp(scaled_norm, inputs, attn_back[0].astype(jnp.float32))
+    grad_input_part, grad_first_gain = norm_one_back(grad_normed_one)
+    grad_first_offset = jnp.sum(grad_normed_one, axis=0)
+    grad_tokens = grad_middle + grad_input_part
+    partials = {
+        "qkv": grad_qkv_weight.astype(jnp.bfloat16),
+        "out": grad_out_weight.astype(jnp.bfloat16),
+        "up": grad_up_weight.astype(jnp.bfloat16),
+        "down": grad_down_weight.astype(jnp.bfloat16),
+    }
+    small_grads = jnp.stack(
+        [
+            grad_first_gain,
+            grad_first_offset,
+            grad_query_bias,
+            grad_value_bias,
+            grad_out_bias,
+            grad_second_gain,
+            grad_second_offset,
+            grad_down_bias,
+        ]
+    )
+    small_grads = jnp.concatenate(
+        [small_grads, grad_up_bias.reshape(4, WIDTH), jnp.zeros((4, WIDTH), jnp.float32)], axis=0
+    )
+    *matrices, total = scatter(partials, small_grads)
+    parts, up_part = own_parts(total)
+    return (
+        layer_out,
+        grad_tokens,
+        parts[0],
+        parts[1],
+        matrices[0],
+        parts[2],
+        parts[3],
+        matrices[1],
+        parts[4],
+        parts[5],
+        parts[6],
+        matrices[2],
+        up_part,
+        matrices[3],
+        parts[7],
+    )
+
+
 def solution(mesh):
     placed = (
         P(("dp", "fsdp"), None),
@@ -294,7 +897,7 @@
         P(("dp", "fsdp")),
     )
     return jax.shard_map(
-        per_device,
+        fast_device if fits(mesh) else plain_device,
         mesh=mesh,
         in_specs=placed,
         out_specs=(

time: 850 us -> 494 us (0.58)
  waiting for transfers between devices: 408 us -> 0 us
  Pallas kernels: 0 us -> 172 us
  blocking collectives: 85 us -> 0 us
  matrix products: 205 us -> 183 us
  between operations: 15.3 us -> 1.67 us
    reduce_scatter x4 -> x0, waiting for transfers between devices: 314 us -> none  [the longest x1 142 us: per_device(): lax.psum_scatter(grad_up_weight, ('dp', 'fsdp'), scatter_dimension=0, til...]
    pallas_call x0 -> x2, Pallas kernels: none -> 172 us  [the longest x1 86.7 us: scatter(): pl.pallas_call(scatter_kernel, name='scatter_gradients', out_shape=out_sh...]
    all_gather x4 -> x0, waiting for transfers between devices: 91.3 us -> none  [the longest x1 54.4 us: per_device(): lax.all_gather(down_weight, ('dp', 'fsdp'), axis=0, tiled=True)]
    unnamed x2 -> x0, blocking collectives: 85 us -> none
    unnamed x161 -> x128, local copies, waits for them, and re-layouts: 34 us -> 25.2 us
  transfers between devices with their start and end apart: 8 -> 0, of which waited for: 6 -> 0; matrix products, arithmetic and copies ran while one was open for 30% -> 0% of each run, Pallas kernels for 0% -> 0%
where the time goes in v1:
time: 494 us; the launch traced here: 486 us
  matrix products  183 us (37%)
  Pallas kernels  172 us (35%)
  local copies, waits for them, and re-layouts  64.9 us (13%)
  other arithmetic  64 us (13%)
    pallas_call x1, Pallas kernels, scatter(): pl.pallas_call(scatter_kernel, name='scatter_gradients', out_shape=out_sh...  86.7 us
    pallas_call x1, Pallas kernels, gather(): pl.pallas_call(gather_kernel, name='gather_weights', out_shape=out_shape,...  85.1 us
    dot_general x4, matrix products, contract_rows(): lax.dot_general(former, latter, (((0,), (0,)), ((), ())), preferred_eleme...  31.4 us
    dot_general x4, matrix products, contract_cols(): lax.dot_general(former, latter, (((1,), (1,)), ((), ())), preferred_eleme...  31.4 us
    dot_general x4, matrix products, dense(): return jnp.dot(former, latter, preferred_element_type=jnp.float32)  30.7 us
    dot_general x2, matrix products, attend_row_back(): jnp.einsum('qhd,khd->hqk', incoming, values[:row_stop], preferred_element...  28 us
    unnamed x128, local copies, waits for them, and re-layouts  25.2 us
    convert_element_type x2, other arithmetic, attend_row_back(): grad_scores = (probs * (grad_probs - inner_sum)).astype(jnp.bfloat16)  25.1 us

profile of v1, /device:TPU:0, one launch (start us, length us, event | category | flops | bytes accessed | tf_op | source)
XLA Modules:
  0.0 485.7 jit_solution(9442057809981076050)
XLA Ops:
  3.8 2.1 fusion.37
  10.7 85.1 %gather_weights.1 = (bf16[768,2304]{1,0:T(8,128)(2,1)}, bf16[768,768]{1,0:T(8,128)(2,1)}, bf16[768,3072]{1,0:T(8,128)(2,1)}, bf16[3072,768]{1,0:T(8,128)(2,1)}, f32[16,768]{1,0:T(8,128)}) custom-call(bf16[24,2304]{1,0:T(8,128)(2,1)} %refs_0_.1, bf16[24,768]{1,0:T(8,128)(2,1)} %refs_1_.1, bf16[24,3072]{1,0:T(8,128)(2,1)} %refs_2_.1, bf16[96,768]{1,0:T(8,128)(2,1)} %refs_3_.1, ...), custom_call_target="tpu_custom_call" | custom-call | tf_op jit(solution)/shard_map/gather_weights/pallas_call | solution.py:483
  97.7 8.0 %fusion.75 = (bf16[1024,2304]{1,0:T(8,128)(2,1)}, f32[1024,2304]{1,0:T(8,128)S(1)}) fusion(bf16[768,2304]{1,0:T(8,128)(2,1)} %get-tuple-element.77, bf16[1024,768]{0,1:T(8,128)(2,1)S(1)} %copy.56, f32[768]{0:T(1024)S(1)} %get-tuple-element.128, f32[768]{0:T(1024)S(1)} %get-tuple-element.129, f32[1024]{0:T(1024)S(1)} %fusion.51, ...), kind=kOutput, calls=%fused_computation.145 | convolution fusion | flops 3630956544 | bytes 19281920 | tf_op jit(solution)/shard_map/dot_general | solution.py:28
  108.8 2.3 copy.58
  111.1 2.4 copy.62
  113.4 2.1 slice.191
  115.5 2.6 copy.61
  118.1 2.3 copy.57
  120.4 2.1 slice.194
  122.5 2.7 slice.196
  125.1 3.0 copy.63
  128.1 2.3 copy.59
  130.4 3.4 fusion.24
  133.9 2.6 fusion.13
  138.5 5.6 %fusion.43 = bf16[12,64,512]{2,1,0:T(8,128)(2,1)} fusion(bf16[512,12,64]{0,2,1:T(8,128)(2,1)} %bitcast.119, f32[12,512]{1,0:T(8,128)S(1)} %fusion.13, f32[12,512]{1,0:T(8,128)S(1)} %get-tuple-element.156, f32[12,512,512]{1,2,0:T(8,128)S(1)} %get-tuple-element.157, pred[512,512]{0,1:T(8,128)(4,1)S(1)} %fusion.49), kind=kOutput, calls=%fused_computation.87 | convolution fusion | flops 418775040 | bytes 14467072 | tf_op jit(solution)/shard_map/while/body/eval_jaxpr/hqk,khd->qhd/dot_general | solution.py:74
  144.1 10.6 %fusion.15 = (f32[12,512]{1,0:T(8,128)S(1)}, f32[12,512,1024]{2,1,0:T(8,128)}) fusion(pred[512,1024]{1,0:T(8,128)(4,1)S(1)} %copy-done.14, bf16[512,12,64]{0,2,1:T(8,128)(2,1)S(1)} %bitcast.103, bf16[1024,12,64]{0,2,1:T(8,128)(2,1)S(1)} %bitcast.100), kind=kOutput, calls=%fused_computation.30 | convolution fusion | flops 824174592 | bytes 28073984 | tf_op jit(solution)/shard_map/while/body/eval_jaxpr/qhd,khd->hqk/dot_general | solution.py:46
  154.7 12.3 %fusion = f32[12,512]{1,0:T(8,128)S(1)} fusion(f32[12,512]{1,0:T(8,128)S(1)} %get-tuple-element.154, f32[12,512,1024]{2,1,0:T(8,128)} %get-tuple-element.155, pred[512,1024]{1,0:T(8,128)(4,1)S(1)} %copy-done.15), kind=kLoop, calls=%fused_computation.6 | loop fusion | flops 25159680 | bytes 25739264 | tf_op jit(solution)/shard_map/while/body/eval_jaxpr/reduce_sum | solution.py:71
  167.7 2.4 copy-done
  170.1 9.8 %fusion.44 = bf16[12,64,512]{2,1,0:T(8,128)(2,1)} fusion(bf16[1024,12,64]{0,2,1:T(8,128)(2,1)} %bitcast.110, f32[12,512]{1,0:T(8,128)S(1)} %fusion, f32[12,512]{1,0:T(8,128)S(1)} %get-tuple-element.154, f32[12,512,1024]{2,1,0:T(8,128)S(1)} %copy-done, pred[512,1024]{1,0:T(8,128)(4,1)S(1)} %copy-done.15), kind=kOutput, calls=%fused_computation.88 | convolution fusion | flops 837156864 | bytes 28098560 | tf_op jit(solution)/shard_map/while/body/eval_jaxpr/hqk,khd->qhd/dot_general | solution.py:74
  180.0 3.6 fusion.76
  184.1 8.6 %fusion.70 = f32[1024,3072]{1,0:T(8,128)} fusion(bf16[768,3072]{1,0:T(8,128)(2,1)S(1)} %bitcast.116, f32[1024,768]{0,1:T(8,128)S(1)} %get-tuple-element.159, f32[768]{0:T(1024)S(1)} %get-tuple-element.124, f32[768]{0:T(1024)S(1)} %get-tuple-element.122, f32[1024]{0:T(1024)S(1)} %fusion.52, f32[1024]{0:T(1024)S(1)} %broadcast_multiply_fusion), kind=kOutput, calls=%fused_computation.140 | convolution fusion | flops 4835770368 | bytes 20461568 | tf_op jit(solution)/shard_map/dot_general | solution.py:28
  192.7 10.5 %add_convert_fusion = bf16[1024,768]{0,1:T(8,128)(2,1)} fusion(f32[1024,768]{0,1:T(8,128)S(1)} %get-tuple-element.159, bf16[3072,768]{1,0:T(8,128)(2,1)S(1)} %bitcast.140, f32[768]{0:T(1024)S(1)} %get-tuple-element.123, f32[1024,3072]{1,0:T(8,128)} %fusion.70, f32[3072]{0:T(1024)S(1)} %add.197), kind=kOutput, calls=%fused_computation.74 | convolution fusion | flops 4866441216 | bytes 22035456 | tf_op jit(solution)/shard_map/dot_general | solution.py:28
  203.2 2.6 copy.73
  205.7 15.7 %convert_reduce_fusion = (f32[3072]{0:T(1024)S(1)}, bf16[1024,3072]{1,0:T(8,128)(2,1)S(1)}) fusion(f32[1024,3072]{1,0:T(8,128)} %fusion.70, f32[3072]{0:T(1024)S(1)} %add.197, bf16[3072,768]{1,0:T(8,128)(2,1)} %get-tuple-element.80, bf16[1024,768]{0,1:T(8,128)(2,1)S(1)} %copy.65), kind=kOutput, calls=%fused_computation.18 | convolution fusion | flops 4906546176 | bytes 25190400 | tf_op jit(solution)/shard_map/dot_general | solution.py:38
  221.5 15.5 %convolution_convert_fusion.refs_3_ = bf16[3072,768]{1,0:T(8,128)(2,1)} fusion(bf16[1024,768]{0,1:T(8,128)(2,1)S(1)} %copy.65, f32[1024,3072]{1,0:T(8,128)} %fusion.70, f32[3072]{0:T(1024)S(1)} %add.197), kind=kOutput, calls=%fused_computation.34 | convolution fusion | flops 4868014080 | bytes 18886656 | tf_op jit(solution)/shard_map/dot_general | solution.py:32
  237.0 6.7 %fusion.78 = (f32[768]{0:T(1024)S(1)}, f32[1024,768]{1,0:T(8,128)}) fusion(bf16[1024,3072]{1,0:T(8,128)(2,1)S(1)} %get-tuple-element.169, bf16[768,3072]{1,0:T(8,128)(2,1)S(1)} %bitcast.118), kind=kOutput, calls=%fused_computation.148 | convolution fusion | flops 4832623616 | bytes 14158848 | tf_op jit(solution)/shard_map/dot_general | solution.py:38
  243.7 3.8 copy.66
  247.5 3.0 multiply_reduce_fusion.2
  251.2 7.6 %convolution_convert_fusion.1.refs_2_ = bf16[768,3072]{1,0:T(8,128)(2,1)} fusion(bf16[1024,3072]{1,0:T(8,128)(2,1)S(1)} %copy-done.50, f32[1024,768]{0,1:T(8,128)S(1)} %copy-done.5, f32[768]{0:T(1024)S(1)} %get-tuple-element.124, f32[768]{0:T(1024)S(1)} %get-tuple-element.122, f32[1024]{0:T(1024)S(1)} %fusion.52, f32[1024]{0:T(1024)S(1)} %broadcast_multiply_fusion), kind=kOutput, calls=%fused_computation.35 | convolution fusion | flops 4838129664 | bytes 14170112 | tf_op jit(solution)/shard_map/dot_general | solution.py:32
  262.2 2.4 convolution_convert_fusion.4.refs_1_
  268.1 3.9 fusion.40
  272.0 13.5 %fusion.35 = bf16[1024,12,64]{0,2,1:T(8,128)(2,1)} fusion(f32[512,12,64]{0,2,1:T(8,128)} %fusion.40, bf16[512,12,64]{0,2,1:T(8,128)(2,1)} %bitcast.123, f32[12,512]{1,0:T(8,128)S(1)} %copy-done.33, f32[12,512,1024]{2,1,0:T(8,128)} %get-tuple-element.155, pred[512,1024]{1,0:T(8,128)(4,1)S(1)} %copy-done.16), kind=kOutput, calls=%fused_computation.65 | convolution fusion | flops 832045056 | bytes 29646848 | tf_op jit(solution)/shard_map/while/body/eval_jaxpr/hqk,qhd->khd/dot_general | solution.py:114
  285.5 7.9 %multiply_reduce_fusion.1 = (f32[12,512]{1,0:T(8,128)S(1)}, f32[12,512,512]{1,2,0:T(8,128)}) fusion(f32[12,512]{1,0:T(8,128)S(1)} %copy-done.34, f32[12,512,512]{1,2,0:T(8,128)S(1)} %bitcast.98, pred[512,512]{0,1:T(8,128)(4,1)S(1)} %copy-done.23, bf16[512,12,64]{0,2,1:T(8,128)(2,1)} %bitcast.122, bf16[512,12,64]{0,2,1:T(8,128)(2,1)S(1)} %bitcast.120), kind=kOutput, calls=%fused_computation.21 | convolution fusion | flops 418375680 | bytes 27049984 | tf_op jit(solution)/shard_map/while/body/eval_jaxpr/qhd,khd->hqk/dot_general | solution.py:94
  293.4 7.2 %multiply_convert_fusion.1 = bf16[12,512,512]{1,2,0:T(8,128)(2,1)S(1)} fusion(f32[12,512,512]{1,2,0:T(8,128)} %get-tuple-element.161, f32[12,512]{1,0:T(8,128)S(1)} %get-tuple-element.160, f32[12,512]{1,0:T(8,128)S(1)} %copy-done.34, f32[12,512,512]{1,2,0:T(8,128)S(1)} %bitcast.98, pred[512,512]{0,1:T(8,128)(4,1)S(1)} %copy-done.23), kind=kLoop, calls=%fused_computation.20 | loop fusion | flops 18874368 | bytes 31768576 | tf_op jit(solution)/shard_map/while/body/eval_jaxpr/convert_element_type | solution.py:98
  300.6 2.0 fusion.46
  302.7 3.1 multiply_bitcast_fusion
  305.8 20.1 %multiply_reduce_fusion = (f32[12,512]{1,0:T(8,128)S(1)}, f32[12,512,1024]{2,1,0:T(8,128)}) fusion(f32[12,512]{1,0:T(8,128)S(1)} %copy-done.33, f32[12,512,1024]{2,1,0:T(8,128)} %get-tuple-element.155, pred[512,1024]{1,0:T(8,128)(4,1)S(1)} %copy-done.16, bf16[512,12,64]{0,2,1:T(8,128)(2,1)S(1)} %bitcast.124, bf16[1024,12,64]{0,2,1:T(8,128)(2,1)} %bitcast.111), kind=kOutput, calls=%fused_computation.1 | convolution fusion | flops 836757504 | bytes 53264384 | tf_op jit(solution)/shard_map/while/body/eval_jaxpr/qhd,khd->hqk/dot_general | solution.py:94
  326.0 17.9 %multiply_convert_fusion = bf16[12,512,1024]{2,1,0:T(8,128)(2,1)S(1)} fusion(f32[12,512,1024]{2,1,0:T(8,128)} %get-tuple-element.163, f32[12,512]{1,0:T(8,128)S(1)} %get-tuple-element.162, f32[12,512]{1,0:T(8,128)S(1)} %copy-done.33, f32[12,512,1024]{2,1,0:T(8,128)} %get-tuple-element.155, pred[512,1024]{1,0:T(8,128)(4,1)} %fusion.37), kind=kLoop, calls=%fused_computation | loop fusion | flops 37748736 | bytes 63488000 | tf_op jit(solution)/shard_map/while/body/eval_jaxpr/convert_element_type | solution.py:98
  343.9 3.6 fusion.36
  347.5 6.3 %fusion.45 = bf16[512,12,64]{0,2,1:T(8,128)(2,1)} fusion(bf16[1024,12,64]{0,2,1:T(8,128)(2,1)} %bitcast.99, bf16[12,512,1024]{2,1,0:T(8,128)(2,1)S(1)} %multiply_convert_fusion), kind=kOutput, calls=%fused_computation.89 | convolution fusion | flops 806092800 | bytes 14942208 | tf_op jit(solution)/shard_map/while/body/eval_jaxpr/hqk,khd->qhd/dot_general | solution.py:100
  356.1 7.6 %fusion.77 = (f32[768]{0:T(1024)S(1)}, f32[1024,768]{1,0:T(8,128)}) fusion(bf16[768,2304]{1,0:T(8,128)(2,1)} %get-tuple-element.77, bf16[1024,768]{0,1:T(8,128)(2,1)S(1)} %bitcast.126, bf16[1024,768]{0,1:T(8,128)(2,1)S(1)} %bitcast.105, bf16[1024,768]{0,1:T(8,128)(2,1)S(1)} %bitcast.112), kind=kOutput, calls=%fused_computation.147 | convolution fusion | flops 3638820096 | bytes 11406336 | tf_op jit(solution)/shard_map/dot_general | solution.py:38
  363.7 3.9 copy.70
  367.6 2.6 fusion.32
  372.6 3.3 convert_reduce_fusion.2
  375.9 5.9 %convolution_convert_fusion.2.refs_0_ = bf16[768,2304]{1,0:T(8,128)(2,1)} fusion(bf16[1024,768]{0,1:T(8,128)(2,1)S(1)} %copy-done.3, f32[768]{0:T(1024)S(1)} %copy-done.45, f32[768]{0:T(1024)S(1)} %copy-done.39, f32[1024]{0:T(1024)S(1)} %copy-done.41, f32[1024]{0:T(1024)S(1)} %copy-done.37, bf16[1024,768]{0,1:T(8,128)(2,1)S(1)} %bitcast.127, ...), kind=kOutput, calls=%fused_computation.36 | convolution fusion | flops 3644522496 | bytes 9844736 | tf_op jit(solution)/shard_map/dot_general | solution.py:32
  381.8 3.7 copy.74
  385.5 2.5 fusion.68
  389.6 86.7 %scatter_gradients.1 = (f32[24,2304]{1,0:T(8,128)}, f32[24,768]{1,0:T(8,128)}, f32[24,3072]{1,0:T(8,128)}, f32[96,768]{1,0:T(8,128)}, f32[16,768]{1,0:T(8,128)}) custom-call(bf16[768,2304]{1,0:T(8,128)(2,1)} %convolution_convert_fusion.2.refs_0_, bf16[768,768]{1,0:T(8,128)(2,1)} %convolution_convert_fusion.4.refs_1_, ...), custom_call_target="tpu_custom_call" | custom-call | tf_op jit(solution)/shard_map/scatter_gradients/pallas_call | solution.py:542
  (179 shorter events, 38.8 us)
Async XLA Ops:
  3.6 4.8 copy-start.35
  3.8 134.0 %copy-start.22 = (pred[512,512]{0,1:T(8,128)(4,1)}, pred[512,512]{0,1:T(8,128)(4,1)S(1)}, u32[]{:S(2)}) copy-start(pred[512,512]{0,1:T(8,128)(4,1)S(1)} %fusion.49) | copy-start | bytes 786436
  7.7 172.3 %copy-start.2 = (bf16[1024,768]{0,1:T(8,128)(2,1)}, bf16[1024,768]{0,1:T(8,128)(2,1)S(1)}, u32[]{:S(2)}) copy-start(bf16[1024,768]{0,1:T(8,128)(2,1)S(1)} %copy.56) | copy-start | bytes 4718596
  7.9 97.8 %copy-start.36 = (f32[1024]{0:T(1024)}, f32[1024]{0:T(1024)S(1)}, u32[]{:S(2)}) copy-start(f32[1024]{0:T(1024)S(1)} %broadcast_multiply_fusion.1) | copy-start | bytes 12292
  9.0 96.7 %copy-start.40 = (f32[1024]{0:T(1024)}, f32[1024]{0:T(1024)S(1)}, u32[]{:S(2)}) copy-start(f32[1024]{0:T(1024)S(1)} %fusion.51) | copy-start | bytes 12292
  10.7 210.7 %copy-start.10 = (bf16[1024,768]{0,1:T(8,128)(2,1)}, bf16[1024,768]{0,1:T(8,128)(2,1)S(1)}, u32[]{:S(2)}) copy-start(bf16[1024,768]{0,1:T(8,128)(2,1)S(1)} %copy.65) | copy-start | bytes 4718596
  97.7 8.0 %copy-start.38 = (f32[768]{0:T(1024)}, f32[768]{0:T(1024)S(1)}, u32[]{:S(2)}) copy-start(f32[768]{0:T(1024)S(1)} %get-tuple-element.129) | copy-start | bytes 9220
  97.7 8.0 %copy-start.44 = (f32[768]{0:T(1024)}, f32[768]{0:T(1024)S(1)}, u32[]{:S(2)}) copy-start(f32[768]{0:T(1024)S(1)} %get-tuple-element.128) | copy-start | bytes 9220
  133.9 4.6 copy-start.1
  138.5 5.6 %copy-start.13 = (bf16[1024,768]{0,1:T(8,128)(2,1)S(1)}, bf16[1024,768]{0,1:T(8,128)(2,1)}, u32[]{:S(2)}) copy-start(bf16[1024,768]{0,1:T(8,128)(2,1)} %copy.63) | copy-start | bytes 4718596
  138.5 5.6 %copy-start.14 = (pred[512,1024]{1,0:T(8,128)(4,1)S(1)}, pred[512,1024]{1,0:T(8,128)(4,1)}, u32[]{:S(2)}) copy-start(pred[512,1024]{1,0:T(8,128)(4,1)} %fusion.37) | copy-start | bytes 1572868
  138.5 5.6 %copy-start.18 = (bf16[512,768]{0,1:T(8,128)(2,1)S(1)}, bf16[512,768]{0,1:T(8,128)(2,1)}, u32[]{:S(2)}) copy-start(bf16[512,768]{0,1:T(8,128)(2,1)} %copy.62) | copy-start | bytes 2359300
  144.1 10.6 %copy-start.15 = (pred[512,1024]{1,0:T(8,128)(4,1)S(1)}, pred[512,1024]{1,0:T(8,128)(4,1)}, u32[]{:S(2)}) copy-start(pred[512,1024]{1,0:T(8,128)(4,1)} %fusion.37) | copy-start | bytes 1572868
  154.7 15.4 %copy-start = (f32[12,512,1024]{2,1,0:T(8,128)S(1)}, f32[12,512,1024]{2,1,0:T(8,128)}, u32[]{:S(2)}) copy-start(f32[12,512,1024]{2,1,0:T(8,128)} %get-tuple-element.155) | copy-start | bytes 75497472
  179.9 4.1 slice-start.3
  180.0 4.1 slice-start.4
  180.0 12.7 %slice-start.7 = ((s8[4718592]{0:T(1024)(128)(4,1)}), s8[4194304]{0:T(1024)(128)(4,1)S(1)}, s32[]{:S(2)}) async-start(s8[4718592]{0:T(1024)(128)(4,1)} %bitcast.139), calls=%async_computation.7 | async-start | bytes 8388608
  183.6 9.0 %copy-start.4 = (f32[1024,768]{0,1:T(8,128)}, f32[1024,768]{0,1:T(8,128)S(1)}, u32[]{:S(2)}) copy-start(f32[1024,768]{0,1:T(8,128)S(1)} %get-tuple-element.159) | copy-start | bytes 9437188
  184.1 8.6 %slice-start.8 = ((s8[4718592]{0:T(1024)(128)(4,1)}), s8[524288]{0:T(1024)(128)(4,1)S(1)}, s32[]{:S(2)}) async-start(s8[4718592]{0:T(1024)(128)(4,1)} %bitcast.139), calls=%async_computation.8 | async-start | bytes 1048576
  192.7 44.3 %slice-start.5 = ((s8[4718592]{0:T(1024)(128)(4,1)}), s8[524288]{0:T(1024)(128)(4,1)S(1)}, s32[]{:S(2)}) async-start(s8[4718592]{0:T(1024)(128)(4,1)} %bitcast.117), calls=%async_computation.5 | async-start | bytes 1048576
  205.7 31.2 %slice-start.6 = ((s8[4718592]{0:T(1024)(128)(4,1)}), s8[4194304]{0:T(1024)(128)(4,1)S(1)}, s32[]{:S(2)}) async-start(s8[4718592]{0:T(1024)(128)(4,1)} %bitcast.117), calls=%async_computation.6 | async-start | bytes 8388608
  221.5 15.5 %copy-start.49 = (bf16[1024,3072]{1,0:T(8,128)(2,1)}, bf16[1024,3072]{1,0:T(8,128)(2,1)S(1)}, u32[]{:S(2)}) copy-start(bf16[1024,3072]{1,0:T(8,128)(2,1)S(1)} %get-tuple-element.169) | copy-start | bytes 18874372
  243.7 3.8 copy-start.5
  247.5 3.7 copy-start.50
  251.2 7.7 %copy-start.9 = (f32[1024,768]{0,1:T(8,128)S(1)}, f32[1024,768]{0,1:T(8,128)}, u32[]{:S(2)}) copy-start(f32[1024,768]{0,1:T(8,128)} %copy.66) | copy-start | bytes 9437188
  260.3 7.7 %slice-start = ((s8[12582912]{0:T(1024)(128)(4,1)}), s8[4194304]{0:T(1024)(128)(4,1)S(1)}, s32[]{:S(2)}) async-start(s8[12582912]{0:T(1024)(128)(4,1)} %bitcast.97), calls=%async_computation | async-start | bytes 8388608
  262.2 2.4 copy-start.46
  262.2 5.8 %slice-start.1 = ((s8[12582912]{0:T(1024)(128)(4,1)}), s8[4194304]{0:T(1024)(128)(4,1)S(1)}, s32[]{:S(2)}) async-start(s8[12582912]{0:T(1024)(128)(4,1)} %bitcast.97), calls=%async_computation.1 | async-start | bytes 8388608
  264.6 3.4 slice-start.2
  268.1 4.0 copy-start.16
  268.1 3.9 copy-start.33
  272.0 13.5 %copy-start.28 = (bf16[512,768]{0,1:T(8,128)(2,1)S(1)}, bf16[512,768]{0,1:T(8,128)(2,1)}, u32[]{:S(2)}) copy-start(bf16[512,768]{0,1:T(8,128)(2,1)} %copy.57) | copy-start | bytes 2359300
  293.4 7.2 %copy-start.17 = (bf16[512,768]{0,1:T(8,128)(2,1)S(1)}, bf16[512,768]{0,1:T(8,128)(2,1)}, u32[]{:S(2)}) copy-start(bf16[512,768]{0,1:T(8,128)(2,1)} %copy.59) | copy-start | bytes 2359300
  302.7 3.2 copy-start.30
  326.0 17.9 %copy-start.19 = (bf16[512,768]{0,1:T(8,128)(2,1)S(1)}, bf16[512,768]{0,1:T(8,128)(2,1)}, u32[]{:S(2)}) copy-start(bf16[512,768]{0,1:T(8,128)(2,1)} %copy.62) | copy-start | bytes 2359300
  326.0 17.9 %copy-start.27 = (f32[512,12,64]{0,2,1:T(8,128)S(1)}, f32[512,12,64]{0,2,1:T(8,128)}, u32[]{:S(2)}) copy-start(f32[512,12,64]{0,2,1:T(8,128)} %multiply_bitcast_fusion) | copy-start | bytes 4718596
  355.4 8.2 %copy-start.24 = (bf16[1024,12,64]{0,2,1:T(8,128)(2,1)}, bf16[1024,12,64]{0,2,1:T(8,128)(2,1)S(1)}, u32[]{:S(2)}) copy-start(bf16[1024,12,64]{0,2,1:T(8,128)(2,1)S(1)} %pad_maximum_fusion.2) | copy-start | bytes 4718596
  363.6 3.9 copy-start.3
  363.6 3.9 copy-start.37
  363.7 3.9 copy-start.39
  367.6 2.6 copy-start.43
  367.6 2.8 copy-start.6
  367.6 2.8 copy-start.41
  370.2 2.4 copy-start.12
  372.6 3.4 copy-start.25
  372.6 3.4 copy-start.32
  372.6 3.4 copy-start.45
  381.8 3.7 copy-start.26
  (12 other events, 20.3 us)

commit v2 on v0

--- a/solution.py
+++ b/solution.py
@@ -1,6 +1,8 @@
 import jax
 import jax.numpy as jnp
 from jax import lax
+from jax.experimental import pallas as pl
+from jax.experimental.pallas import tpu as pltpu
 from jax.sharding import PartitionSpec as P
 
 HEADS = 12
@@ -118,7 +120,7 @@
     return (jnp.concatenate(query_parts, axis=0), grad_keys, grad_values)
 
 
-def per_device(
+def plain_device(
     tokens,
     doc_ids,
     cotangent,
@@ -274,6 +276,913 @@
     )
 
 
+MESH = pl.DeviceIdType.MESH
+F32 = jnp.float32
+BF16 = jnp.bfloat16
+WIDTH = 768
+HIDDEN = 3072
+TOKENS = 1024
+QKV = 3 * WIDTH
+PAIRS = 6
+QUERY_ROWS = 256
+KEY_WINDOWS = ((0, 256), (0, 512), (0, 768), (256, 1024))
+DOCUMENTS = 6
+FAR_BELOW = 2.0**100
+STRIP = 128
+TILE = 256
+VMEM_LIMIT = 63 * 2**20
+GELU_A = 0.7978845608028654
+GELU_B = 0.044715
+
+GATHER_UNITS = (
+    ("qkv", 0, 384),
+    ("qkv", 768, 384),
+    ("qkv", 1536, 384),
+    ("out", 0, 384),
+    ("down", 0, 128),
+    ("down", 128, 128),
+    ("down", 256, 128),
+    ("up", 0, 384),
+    ("up", 768, 384),
+    ("up", 1536, 384),
+    ("up", 2304, 384),
+)
+SCATTER_UNITS = (
+    ("up", 0, 384),
+    ("up", 768, 384),
+    ("up", 1536, 384),
+    ("up", 2304, 384),
+    ("down", 0, 128),
+    ("down", 128, 128),
+    ("down", 256, 128),
+    ("out", 0, 384),
+    ("qkv", 0, 384),
+    ("qkv", 768, 384),
+    ("qkv", 1536, 384),
+)
+SHARD_ROWS = {"qkv": 24, "out": 24, "up": 24, "down": 96}
+COLUMNS = {"qkv": QKV, "out": WIDTH, "up": HIDDEN, "down": WIDTH}
+NAMES = ("qkv", "out", "up", "down")
+
+
+def fits(mesh):
+    return mesh.shape["dp"] == 4 and mesh.shape["fsdp"] == 8
+
+
+def padded(rows):
+    return -(-rows // 16) * 16
+
+
+def aligned(value, step):
+    return pl.multiple_of(value, step)
+
+
+def dot_nt(a, b):
+    return lax.dot_general(a, b, (((1,), (1,)), ((), ())), preferred_element_type=F32)
+
+
+def dot_nn(a, b):
+    return lax.dot_general(a, b, (((1,), (0,)), ((), ())), preferred_element_type=F32)
+
+
+def dot_tn(a, b):
+    return lax.dot_general(a, b, (((0,), (0,)), ((), ())), preferred_element_type=F32)
+
+
+class Place:
+    def __init__(self):
+        self.dp = lax.axis_index("dp")
+        self.fsdp = lax.axis_index("fsdp")
+        self.core = lax.rem(self.fsdp, 2)
+        self.z = lax.div(self.fsdp, 2)
+        x = lax.rem(self.dp, 2)
+        y = lax.div(self.dp, 2)
+        self.dp_x = y * 2 + (1 - x)
+        self.dp_y = (1 - y) * 2 + x
+        self.dp_far = 3 - self.dp
+        core = self.core
+        self.near = self.dp_x * (1 - core) + self.dp_y * core
+        self.next = self.dp_y * (1 - core) + self.dp_x * core
+        self.chip = self.dp * 4 + self.z
+        self.partner = (self.dp, self.z * 2 + (1 - core))
+        self.at_near = (self.near, self.fsdp)
+        self.at_next = (self.next, self.fsdp)
+
+    def along_z(self, step):
+        z = lax.rem(self.z + step, 4)
+        return (self.dp, z * 2 + self.core)
+
+    def greet(self):
+        barrier = pltpu.get_barrier_semaphore()
+        others = [self.partner, (self.dp_x, self.fsdp), (self.dp_y, self.fsdp), (self.dp_far, self.fsdp)]
+        others += [self.along_z(step) for step in (1, 2, 3)]
+        for other in others:
+            pl.semaphore_signal(barrier, inc=1, device_id=other, device_id_type=MESH)
+        pl.semaphore_wait(barrier, len(others))
+
+
+def remote(source, target, sems, index, device):
+    return pltpu.make_async_remote_copy(
+        src_ref=source,
+        dst_ref=target,
+        send_sem=sems[0].at[index],
+        recv_sem=sems[1].at[index],
+        device_id=device,
+        device_id_type=MESH,
+    )
+
+
+class SmallSum:
+    def __init__(self, place, buffers, landed, sems):
+        self.place, self.buffers, self.landed, self.sems = place, buffers, landed, sems
+
+    @staticmethod
+    def scratch():
+        return [
+            pltpu.VMEM((3, 16, WIDTH), F32),
+            pltpu.VMEM((7, 16, WIDTH), F32),
+            pltpu.SemaphoreType.DMA((7,)),
+            pltpu.SemaphoreType.DMA((7,)),
+        ]
+
+    def copies(self, stage):
+        p = self.place
+        if stage == 0:
+            devices = [p.partner]
+        elif stage == 1:
+            devices = [(dp, p.fsdp) for dp in (p.dp_x, p.dp_y, p.dp_far)]
+        else:
+            devices = [p.along_z(step) for step in (1, 2, 3)]
+        first = (0, 1, 4)[stage]
+        return [
+            remote(self.buffers.at[stage], self.landed.at[first + i], self.sems, first + i, device)
+            for i, device in enumerate(devices)
+        ]
+
+    def begin(self, value):
+        self.buffers[0] = value
+        for copy in self.copies(0):
+            copy.start()
+
+    def middle(self):
+        for copy in self.copies(0):
+            copy.wait()
+        self.buffers[1] = self.buffers[0] + self.landed[0]
+        for copy in self.copies(1):
+            copy.start()
+
+    def last(self):
+        for copy in self.copies(1):
+            copy.wait()
+        self.buffers[2] = (self.buffers[1] + self.landed[1]) + (self.landed[2] + self.landed[3])
+        for copy in self.copies(2):
+            copy.start()
+
+    def end(self):
+        for copy in self.copies(2):
+            copy.wait()
+        return (self.buffers[2] + self.landed[4]) + (self.landed[5] + self.landed[6])
+
+
+class GatherUnit:
+    SEMS = 11
+
+    def __init__(self, place, unit, shard, full, pair_out, pair_in, send_sems, recv_sems):
+        self.place = place
+        self.name, self.first, self.width = unit
+        self.rows = SHARD_ROWS[self.name]
+        self.shard, self.full = shard, full
+        self.pair_out, self.pair_in = pair_out, pair_in
+        self.sems = (send_sems, recv_sems)
+
+    def part_of(self, core):
+        if self.name != "qkv":
+            return self.shard[:, pl.ds(aligned(self.first + 384 * core, 128), self.width)]
+        start = self.first // 3 + 128 * core
+        parts = [self.shard[:, pl.ds(aligned(start + WIDTH * i, 128), 128)] for i in range(3)]
+        return jnp.concatenate(parts, axis=1)
+
+    def columns(self):
+        return pl.ds(aligned(self.first + 384 * self.place.core, 128), self.width)
+
+    def group(self, dp):
+        rows = 8 * self.rows
+        return self.full.at[pl.ds(aligned(dp * rows, 16), rows), self.columns()]
+
+    def block(self):
+        rows = 2 * self.rows
+        return self.full.at[pl.ds(aligned(self.place.chip * rows, 16), rows), self.columns()]
+
+    def copy(self, index):
+        p = self.place
+        if index == 0:
+            return remote(self.pair_out, self.pair_in, self.sems, 0, p.partner)
+        if index < 4:
+            return remote(self.block(), self.block(), self.sems, index, p.along_z(index))
+        dp = (p.dp, p.dp, p.near, p.dp, p.near, p.next, p.dp_far)[index - 4]
+        device = p.at_near if index == 4 else p.at_next if index < 7 else p.partner
+        return remote(self.group(dp), self.group(dp), self.sems, index, device)
+
+    def start(self, *indices):
+        for index in indices:
+            self.copy(index).start()
+
+    def landed(self, *indices):
+        for index in indices:
+            self.copy(index).wait_recv()
+
+    def pair(self):
+        self.pair_out[0 : self.rows] = self.part_of(1 - self.place.core)
+        if self.rows % 16:
+            rest = padded(self.rows) - self.rows
+            self.pair_out[self.rows :] = jnp.zeros((rest, self.width), BF16)
+        self.start(0)
+
+    def along_z(self):
+        self.landed(0)
+        own = self.part_of(self.place.core).astype(F32)
+        came = self.pair_in[0 : self.rows].astype(F32)
+        first = self.place.core == 0
+        block = jnp.concatenate([jnp.where(first, own, came), jnp.where(first, came, own)], axis=0)
+        self.block()[...] = block.astype(BF16)
+        self.start(1, 2, 3)
+
+    def to_near(self):
+        self.landed(1, 2, 3)
+        self.start(4, 5, 7)
+
+    def to_next(self):
+        self.landed(4)
+        self.start(6, 8)
+
+    def to_core(self):
+        self.landed(5)
+        self.start(9)
+        self.landed(6)
+        self.start(10)
+
+    def arrived(self):
+        self.landed(7, 8, 9, 10)
+
+    def finish(self):
+        for index in range(self.SEMS):
+            self.copy(index).wait_send()
+
+
+class ScatterUnit:
+    SEMS = 8
+
+    def __init__(self, place, unit, partial, target, halves, from_next, from_near, from_z, pair, send_sems, recv_sems):
+        self.place = place
+        self.name, self.first, self.width = unit
+        self.rows = SHARD_ROWS[self.name]
+        self.partial, self.target = partial, target
+        self.halves, self.from_next, self.from_near = halves, from_next, from_near
+        self.from_z, self.pair_buffer = from_z, pair
+        self.sems = (send_sems, recv_sems)
+
+    @staticmethod
+    def scratch(unit):
+        name, _, width = unit
+        rows = SHARD_ROWS[name]
+        return [
+            pltpu.VMEM((32 * rows, width), BF16),
+            pltpu.VMEM((2, 8 * rows, width), BF16),
+            pltpu.VMEM((8 * rows, width), BF16),
+            pltpu.VMEM((3, 2 * rows, width), BF16),
+            pltpu.VMEM((3, rows, width), F32),
+        ]
+
+    def columns(self, core):
+        first = 0 if self.name == "qkv" else self.first
+        return pl.ds(aligned(first + 384 * core, 128), self.width)
+
+    def group(self, dp):
+        rows = 8 * self.rows
+        return self.halves.at[pl.ds(aligned(dp * rows, 16), rows)]
+
+    def z_block(self, step):
+        z = lax.rem(self.place.z + step, 4)
+        rows = 2 * self.rows
+        return self.halves.at[pl.ds(aligned((self.place.dp * 4 + z) * rows, 16), rows)]
+
+    def copy(self, index):
+        p = self.place
+        if index == 0:
+            source = self.partial.at[pl.ds(0, 32 * self.rows), self.columns(1 - p.core)]
+            return remote(source, self.halves, self.sems, 0, p.partner)
+        if index < 3:
+            dp = (p.next, p.dp_far)[index - 1]
+            return remote(self.group(dp), self.from_next.at[index - 1], self.sems, index, p.at_next)
+        if index == 3:
+            return remote(self.group(p.near), self.from_near, self.sems, 3, p.at_near)
+        if index < 7:
+            step = index - 3
+            return remote(self.z_block(step), self.from_z.at[step - 1], self.sems, index, p.along_z(step))
+        return remote(self.pair_buffer.at[0], self.pair_buffer.at[2], self.sems, 7, p.partner)
+
+    def start(self, *indices):
+        for index in indices:
+            self.copy(index).start()
+
+    def landed(self, *indices):
+        for index in indices:
+            self.copy(index).wait_recv()
+
+    def add(self, former, latter, rows):
+        step = 192
+
+        def body(index, carry):
+            at = pl.ds(aligned(index * step, 16), step)
+            former[at] = (former[at].astype(F32) + latter(at).astype(F32)).astype(BF16)
+            return carry
+
+        lax.fori_loop(0, rows // step, body, 0)
+
+    def to_partner(self):
+        self.start(0)
+
+    def to_next(self):
+        self.landed(0)
+        mine = self.columns(self.place.core)
+        self.add(self.halves, lambda at: self.partial[at, mine], 32 * self.rows)
+        self.start(1, 2)
+
+    def to_near(self):
+        p = self.place
+        self.landed(1, 2)
+        self.add(self.group(p.near), lambda at: self.from_next[1, at], 8 * self.rows)
+        self.start(3)
+        self.add(self.group(p.dp), lambda at: self.from_next[0, at], 8 * self.rows)
+
+    def along_z(self):
+        self.landed(3)
+        self.add(self.group(self.place.dp), lambda at: self.from_near[at], 8 * self.rows)
+        self.start(4, 5, 6)
+
+    def to_pair(self):
+        self.landed(4, 5, 6)
+        rows = self.rows
+        came = [self.from_z[i].astype(F32) for i in range(3)]
+        block = (self.z_block(0)[...].astype(F32) + came[0]) + (came[1] + came[2])
+        first = self.place.core == 0
+        self.pair_buffer[0] = jnp.where(first, block[rows:], block[:rows])
+        self.pair_buffer[1] = jnp.where(first, block[:rows], block[rows:])
+        self.start(7)
+
+    def store(self):
+        self.landed(7)
+        for source, core in ((1, self.place.core), (2, 1 - self.place.core)):
+            if self.name != "qkv":
+                self.target[:, self.columns(core)] = self.pair_buffer[source]
+                continue
+            start = self.first // 3 + 128 * core
+            for i in range(3):
+                columns = pl.ds(aligned(start + WIDTH * i, 128), 128)
+                self.target[:, columns] = self.pair_buffer[source, :, 128 * i : 128 * i + 128]
+
+    def finish(self):
+        for index in range(self.SEMS):
+            self.copy(index).wait_send()
+
+
+STAGES = {
+    "P": "to_partner",
+    "A": "to_next",
+    "B": "to_near",
+    "Z": "along_z",
+    "D": "to_pair",
+    "S": "store",
+    "z": "along_z",
+    "n": "to_near",
+    "x": "to_next",
+    "c": "to_core",
+    "r": "arrived",
+}
+
+
+def run_stages(units, text):
+    for step in text.split():
+        getattr(units[int(step[1:])], STAGES[step[0]])()
+
+
+def strips(body, carry=0):
+    def run(index, carry):
+        return body(pl.ds(aligned(index * STRIP, STRIP), STRIP), carry)
+
+    return lax.fori_loop(0, TOKENS // STRIP, run, carry)
+
+
+def standardized(values):
+    average = jnp.mean(values, axis=-1, keepdims=True)
+    centred = values - average
+    variance = jnp.mean(centred * centred, axis=-1, keepdims=True)
+    scale = lax.rsqrt(variance + norm_eps)
+    return centred * scale, scale
+
+
+def back_through_norm(grad, xhat, scale, gains):
+    lifted = grad * gains
+    return scale * (
+        lifted
+        - jnp.mean(lifted, axis=-1, keepdims=True)
+        - xhat * jnp.mean(lifted * xhat, axis=-1, keepdims=True)
+    )
+
+
+def column_sum(values):
+    return jnp.sum(values, axis=0, keepdims=True)
+
+
+def gelu_and_slope(h):
+    square = h * h
+    bent = GELU_A + GELU_A * GELU_B * square
+    gate = 0.5 + 0.5 * jnp.tanh(h * bent)
+    active = h * gate
+    slope = gate + active * (1.0 - gate) * (6.0 * bent - 4.0 * GELU_A)
+    return active, slope
+
+
+def document_lanes(documents, query_side, key_side):
+    lane = lax.rem(lax.broadcasted_iota(jnp.int32, (TOKENS, 128), 1), 64)
+    own = jnp.broadcast_to(documents.astype(F32), (128, TOKENS)).T == lane.astype(F32)
+    query_side[...] = jnp.where(own, 1.0, 0.0).astype(BF16)
+    key_side[...] = jnp.where(own | (lane >= DOCUMENTS), 0.0, -FAR_BELOW).astype(BF16)
+
+
+def causal_corner(causal):
+    key = lax.broadcasted_iota(jnp.int32, (QUERY_ROWS, QUERY_ROWS), 0)
+    query = lax.broadcasted_iota(jnp.int32, (QUERY_ROWS, QUERY_ROWS), 1)
+    causal[...] = jnp.where(key <= query, 0.0, -FAR_BELOW)
+
+
+class Pair:
+    def __init__(self, wide, pair, block, query_side, key_side):
+        start, stop = KEY_WINDOWS[block]
+        self.keys = pl.ds(start, stop - start)
+        self.rows = pl.ds(block * QUERY_ROWS, QUERY_ROWS)
+        first = pair * 384
+        self.at = [pl.ds(aligned(first + 128 * i, 128), 128) for i in range(3)]
+        self.q = wide[self.rows, self.at[0]]
+        self.k = wide[self.keys, self.at[1]]
+        self.v = wide[self.keys, self.at[2]]
+        self.query_side, self.key_side = query_side[self.rows], key_side[self.keys]
+        self.start, self.stop = start, stop
+
+    def choose(self, head, inside, outside):
+        low = lax.broadcasted_iota(jnp.int32, inside.shape, 1) < 64
+        return jnp.where(low, inside, outside) if head == 0 else jnp.where(low, outside, inside)
+
+    def only(self, head, values):
+        return self.choose(head, values, jnp.zeros_like(values))
+
+    def scores(self, head, causal):
+        scores = dot_nt(self.choose(head, self.k, self.key_side), self.choose(head, self.q, self.query_side))
+        wide = self.stop - self.start - QUERY_ROWS
+        corner = scores[wide:] + causal[...]
+        return jnp.concatenate([scores[:wide], corner], axis=0) if wide else corner
+
+
+def attend(wide, pair, block, query_side, key_side, causal, attended, logsums):
+    p = Pair(wide, pair, block, query_side, key_side)
+    weights, sums = [], []
+    for head in range(2):
+        scores = p.scores(head, causal)
+        highest = jnp.max(scores, axis=0, keepdims=True)
+        raised = jnp.exp(scores - highest)
+        summed = column_sum(raised)
+        weights.append(raised.astype(BF16))
+        sums.append(jnp.broadcast_to(summed, (HEAD_DIM, QUERY_ROWS)))
+        logsums[2 * pair + head, :, p.rows] = highest + jnp.log(summed)
+    values = jnp.concatenate([p.only(head, p.v) for head in range(2)], axis=0)
+    out = dot_tn(values, jnp.concatenate(weights, axis=0)) / jnp.concatenate(sums, axis=0)
+    attended[p.rows, pl.ds(aligned(pair * 128, 128), 128)] = out.T.astype(BF16)
+
+
+def attend_back(wide, pair, block, query_side, key_side, causal, attended, grad_attended, logsums, key_sum, value_sum):
+    p = Pair(wide, pair, block, query_side, key_side)
+    features = pl.ds(aligned(pair * 128, 128), 128)
+    incoming = grad_attended[p.rows, features]
+    inner = (incoming.astype(F32) * attended[p.rows, features].astype(F32)).T
+    probs, slopes = [], []
+    for head in range(2):
+        delta = column_sum(inner[64 * head : 64 * head + 64])
+        prob = jnp.exp(p.scores(head, causal) - logsums[2 * pair + head, :, p.rows])
+        grad_prob = dot_nt(p.v, p.only(head, incoming))
+        probs.append(prob.astype(BF16))
+        slopes.append((prob * (grad_prob - delta)).astype(BF16))
+    both = lambda values: jnp.concatenate([p.only(head, values) for head in range(2)], axis=0)
+    value_part = dot_nn(jnp.concatenate(probs, axis=1), both(incoming))
+    key_part = dot_nn(jnp.concatenate(slopes, axis=1), both(p.q))
+    query_part = dot_tn(both(p.k), jnp.concatenate(slopes, axis=0))
+    wide[p.rows, p.at[0]] = (query_part.T * HEAD_DIM**-0.5).astype(BF16)
+    inside = p.stop - p.start - QUERY_ROWS
+    if inside:
+        earlier = pl.ds(p.start, inside)
+        key_sum[earlier] += key_part[:inside]
+        value_sum[earlier] += value_part[:inside]
+    newest = pl.ds(p.stop - QUERY_ROWS, QUERY_ROWS)
+    key_sum[newest] = key_part[inside:]
+    value_sum[newest] = value_part[inside:]
+
+
+def layer_kernel(*refs):
+    refs = list(refs)
+
+    def take(count):
+        taken = refs[:count]
+        del refs[:count]
+        return taken
+
+    tokens, documents, cotangent = take(3)
+    shards = dict(zip(NAMES, take(4)))
+    (small,) = take(1)
+    layer_out, grad_tokens = take(2)
+    targets = dict(zip(NAMES, take(4)))
+    (small_out,) = take(1)
+    weights = dict(zip(NAMES, take(4)))
+    wq, wo, wu, wd = (weights[name] for name in NAMES)
+    wide, norm, norm_t, attended, seed, act, act_t, slope = take(8)
+    middle, outer, grad_norm = take(3)
+    logsums, query_side, key_side, causal, vectors, qkv_bias, qkv_scale, sums = take(8)
+    pair_buffers = take(2 * len(GATHER_UNITS))
+    scatter_buffers = take(5 * len(SCATTER_UNITS))
+    gather_sems, scatter_sems = take(2), take(2)
+    first_small, last_small = take(4), take(4)
+    (local_sems,) = take(1)
+
+    place = Place()
+    coming = [
+        GatherUnit(
+            place,
+            unit,
+            shards[unit[0]],
+            weights[unit[0]],
+            *pair_buffers[2 * i : 2 * i + 2],
+            gather_sems[0].at[i],
+            gather_sems[1].at[i],
+        )
+        for i, unit in enumerate(GATHER_UNITS)
+    ]
+    partials = {"up": wu, "down": wd, "out": wo}
+    qkv_partials = (slope, act_t, norm)
+    leaving = [
+        ScatterUnit(
+            place,
+            unit,
+            partials[unit[0]] if unit[0] != "qkv" else qkv_partials[unit[1] // WIDTH],
+            targets[unit[0]],
+            *scatter_buffers[5 * i : 5 * i + 5],
+            scatter_sems[0].at[i],
+            scatter_sems[1].at[i],
+        )
+        for i, unit in enumerate(SCATTER_UNITS)
+    ]
+
+    def gathering(text):
+        run_stages(coming, text)
+
+    def scattering(text):
+        run_stages(leaving, text)
+
+    place.greet()
+    total = SmallSum(place, first_small[0], first_small[1], first_small[2:])
+    total.begin(small[...])
+    for unit in coming:
+        unit.pair()
+    gathering("z0")
+    total.middle()
+    gathering("z1")
+    total.last()
+    gathering("z2 n0")
+    document_lanes(documents[...], query_side, key_side)
+    causal_corner(causal)
+    vectors[...] = total.end()
+    gathering("x0 n1 z3")
+    gain_one, offset_one = vectors[0:1], vectors[1:2]
+    for pair in range(PAIRS):
+        at = slice(128 * pair, 128 * pair + 128)
+        first = 384 * pair
+        qkv_bias[:, first : first + 128] = vectors[2:3, at]
+        qkv_bias[:, first + 128 : first + 256] = jnp.zeros((1, 128), F32)
+        qkv_bias[:, first + 256 : first + 384] = vectors[3:4, at]
+        qkv_scale[:, first : first + 128] = jnp.full((1, 128), HEAD_DIM**-0.5, F32)
+        qkv_scale[:, first + 128 : first + 384] = jnp.ones((1, 256), F32)
+
+    def norm_one(rows, carry):
+        xhat, _ = standardized(tokens[rows].astype(F32))
+        norm[rows] = (xhat * gain_one + offset_one).astype(BF16)
+        return carry
+
+    strips(norm_one)
+    gathering("c0 x1 n2 z4")
+
+    def forward_group(group, carry):
+        for number, text in enumerate(("r0", "c1 x2 n3 z5 r1", "c3 x4 n5 z7 r2")):
+            pl.when(group == number)(lambda text=text: gathering(text))
+        for n in range(3):
+            columns = pl.ds(aligned(group * WIDTH + n * TILE, 128), TILE)
+            projected = dot_nn(norm[...], wq[:, columns]) + qkv_bias[:, columns]
+            wide[:, columns] = (projected * qkv_scale[:, columns]).astype(BF16)
+
+        def forward_pair(half, carry):
+            pair = 2 * group + half
+            for block in range(4):
+                attend(wide, pair, block, query_side, key_side, causal, attended, logsums)
+            for number, text in ((2, "c2 x3 n4 z6"), (4, "c4 x5 n6 z8 r3"), (5, "c5 x6 n7 z9")):
+                pl.when(pair == number)(lambda text=text: gathering(text))
+            return carry
+
+        return lax.fori_loop(0, 2, forward_pair, carry)
+
+    lax.fori_loop(0, 3, forward_group, 0)
+
+    for n in range(3):
+        at = slice(n * TILE, n * TILE + TILE)
+        branch = dot_nn(attended[...], wo[:, at]) + vectors[4:5, at]
+        middle[:, at] = tokens[:, at].astype(F32) + branch_scale * branch
+    gathering("c6 x7 n8 z10 r4")
+    gain_two, offset_two = vectors[5:6], vectors[6:7]
+
+    def norm_two(rows, down_bias):
+        xhat, _ = standardized(middle[rows])
+        norm[rows] = (xhat * gain_two + offset_two).astype(BF16)
+        scaled = (branch_scale * cotangent[rows].astype(F32)).astype(BF16)
+        seed[rows] = scaled
+        outer[rows] = jnp.zeros((STRIP, WIDTH), F32)
+        grad_norm[rows] = jnp.zeros((STRIP, WIDTH), F32)
+        return down_bias + column_sum(scaled.astype(F32))
+
+    sums[7:8] = strips(norm_two, jnp.zeros((1, WIDTH), F32))
+    norm_t[0:WIDTH] = norm[...].T
+    norm_t[WIDTH:] = jnp.ones((16, TOKENS), BF16)
+    gathering("c7 x8 n9 r5 r6 r7")
+
+    def feed_forward(step, carry):
+        for n in range(3):
+            at = slice(n * TILE, n * TILE + TILE)
+            columns = pl.ds(aligned(step * WIDTH + n * TILE, 128), TILE)
+            bias = vectors[pl.ds(8 + step, 1), at]
+            hidden = dot_nn(norm[...], wu[:, columns]) + bias
+            grad_active = dot_nt(seed[...], wd[columns])
+            active, bent = gelu_and_slope(hidden)
+            act[:, at] = active.astype(BF16)
+            slope[:, at] = (grad_active * bent).astype(BF16)
+        here = pl.ds(aligned(step * WIDTH, 128), WIDTH)
+        for n in range(3):
+            at = slice(n * TILE, n * TILE + TILE)
+            outer[:, at] += dot_nn(act[...], wd[here, at])
+            grad_norm[:, at] += dot_nt(slope[...], wu[at, here])
+        for number, text in enumerate(("c8 x9 n10", "c9 x10", "c10", "")):
+            pl.when(step == number)(lambda text=text: gathering(text))
+        for number in range(4):
+            def own_columns(number=number):
+                coming[7 + number].finish()
+                if number == 0:
+                    for unit in coming[:7]:
+                        unit.finish()
+
+            pl.when(step == number)(own_columns)
+        act_t[...] = act[...].T
+        for n in range(3):
+            at = slice(n * TILE, n * TILE + TILE)
+            columns = pl.ds(aligned(step * WIDTH + n * TILE, 128), TILE)
+            grad = dot_nn(norm_t[...], slope[:, at])
+            wu[:, columns] = grad[:WIDTH].astype(BF16)
+            sums[pl.ds(8 + step, 1), at] = grad[WIDTH : WIDTH + 1]
+            wd[here, at] = dot_nn(act_t[...], seed[:, at]).astype(BF16)
+        for number, text in enumerate(("P0", "P1 A0", "B0 A1 P2", "Z0 B1 A2 P3 P4")):
+            pl.when(step == number)(lambda text=text: scattering(text))
+        for number, text in enumerate(("r8", "r9", "r10", "")):
+            pl.when(step == number)(lambda text=text: gathering(text))
+        return carry
+
+    lax.fori_loop(0, 4, feed_forward, 0)
+
+    def back_two(rows, carry):
+        mid = middle[rows]
+        slope[rows] = (mid + branch_scale * (outer[rows] + vectors[7:8])).astype(BF16)
+        xhat, scale = standardized(mid)
+        grad = grad_norm[rows]
+        grad_middle = cotangent[rows].astype(F32) + back_through_norm(grad, xhat, scale, gain_two)
+        middle[rows] = grad_middle
+        grad_branch = (branch_scale * grad_middle).astype(BF16)
+        seed[rows] = grad_branch
+        parts = (column_sum(grad_branch.astype(F32)), column_sum(grad * xhat), column_sum(grad))
+        return tuple(former + part for former, part in zip(carry, parts))
+
+    zero = jnp.zeros((1, WIDTH), F32)
+    sums[4:5], sums[5:6], sums[6:7] = strips(back_two, (zero, zero, zero))
+    out_copy = pltpu.make_async_copy(slope, layer_out, local_sems.at[0])
+    out_copy.start()
+    scattering("D0 Z1 B2 A3 P5")
+
+    for n in range(3):
+        at = slice(n * TILE, n * TILE + TILE)
+        act[:, at] = dot_nt(seed[...], wo[at]).astype(BF16)
+    scattering("S0 D1 Z2 B3 A4 P6")
+    act_t[...] = attended[...].T
+    for n in range(3):
+        at = slice(n * TILE, n * TILE + TILE)
+        wo[:, at] = dot_nn(act_t[...], seed[:, at]).astype(BF16)
+    scattering("S1 D2 Z3 B4 A5 P7")
+    strips(norm_one)
+    norm_t[0:WIDTH] = norm[...].T
+    out_copy.wait()
+
+    key_sum, value_sum = outer.at[:, 0:128], outer.at[:, 128:256]
+    pair_texts = (
+        "S2 D3 Z4 B5 A6",
+        "S3 D4 Z5 B6 A7",
+        "S4 D5 Z6 B7",
+        "S5 D6 Z7 A8",
+        "S6 D7 B8",
+        "S7 Z8 A9",
+    )
+
+    def backward_group(group, carry):
+        def backward_pair(half, carry):
+            pair = 2 * group + half
+            for block in range(4):
+                attend_back(
+                    wide, pair, block, query_side, key_side, causal, attended, act, logsums, key_sum, value_sum
+                )
+            first = pair * 384
+            wide[:, pl.ds(aligned(first + 128, 128), 128)] = key_sum[...].astype(BF16)
+            wide[:, pl.ds(aligned(first + 256, 128), 128)] = value_sum[...].astype(BF16)
+            for number, text in enumerate(pair_texts):
+                pl.when(pair == number)(lambda text=text: scattering(text))
+            return carry
+
+        lax.fori_loop(0, 2, backward_pair, carry)
+        for number in range(3):
+            def weight_grads(number=number):
+                partial = qkv_partials[number]
+                rows = []
+                for n in range(3):
+                    at = slice(n * TILE, n * TILE + TILE)
+                    columns = slice(number * WIDTH + n * TILE, number * WIDTH + n * TILE + TILE)
+                    grad = dot_nn(norm_t[...], wide[:, columns])
+                    partial[0:WIDTH, at] = grad[:WIDTH].astype(BF16)
+                    rows.append(grad[WIDTH : WIDTH + 1])
+                row = jnp.concatenate(rows, axis=1)
+                at = slice(number * 256, number * 256 + 256)
+                sums[2:3, at] = jnp.concatenate([row[:, 0:128], row[:, 384:512]], axis=1)
+                sums[3:4, at] = jnp.concatenate([row[:, 256:384], row[:, 640:768]], axis=1)
+                scattering(("P8", "P9", "P10")[number])
+
+            pl.when(group == number)(weight_grads)
+        return carry
+
+    lax.fori_loop(0, 3, backward_group, 0)
+
+    for n in range(3):
+        at = slice(n * TILE, n * TILE + TILE)
+        grad_norm[:, at] = dot_nt(wide[...], wq[at])
+    scattering("D8 B9 A10")
+
+    def back_one(rows, carry):
+        xhat, scale = standardized(tokens[rows].astype(F32))
+        grad = grad_norm[rows]
+        middle[rows] += back_through_norm(grad, xhat, scale, gain_one)
+        return carry[0] + column_sum(grad * xhat), carry[1] + column_sum(grad)
+
+    sums[0:1], sums[1:2] = strips(back_one, (zero, zero))
+    tokens_copy = pltpu.make_async_copy(middle, grad_tokens, local_sems.at[1])
+    tokens_copy.start()
+    sums[12:16] = jnp.zeros((4, WIDTH), F32)
+    total = SmallSum(place, last_small[0], last_small[1], last_small[2:])
+    total.begin(sums[...])
+    scattering("S8 Z9 B10")
+    total.middle()
+    scattering("D9 Z10")
+    total.last()
+    scattering("S9 D10")
+    small_out[...] = total.end()
+    scattering("S10")
+    for unit in leaving:
+        unit.finish()
+    tokens_copy.wait()
+
+
+def layer(tokens, documents, cotangent, shards, small):
+    vmem = pl.BlockSpec(memory_space=pltpu.VMEM)
+    anywhere = pl.BlockSpec(memory_space=pl.ANY)
+    out_shape = [jax.ShapeDtypeStruct((TOKENS, WIDTH), BF16), jax.ShapeDtypeStruct((TOKENS, WIDTH), F32)]
+    out_shape += [jax.ShapeDtypeStruct((SHARD_ROWS[n], COLUMNS[n]), F32) for n in NAMES]
+    out_shape.append(jax.ShapeDtypeStruct((16, WIDTH), F32))
+    scratch = [pltpu.VMEM((32 * SHARD_ROWS[n], COLUMNS[n]), BF16) for n in NAMES]
+    scratch += [
+        pltpu.VMEM((TOKENS, QKV), BF16),
+        pltpu.VMEM((TOKENS, WIDTH), BF16),
+        pltpu.VMEM((WIDTH + 16, TOKENS), BF16),
+        pltpu.VMEM((TOKENS, WIDTH), BF16),
+        pltpu.VMEM((TOKENS, WIDTH), BF16),
+        pltpu.VMEM((TOKENS, WIDTH), BF16),
+        pltpu.VMEM((WIDTH, TOKENS), BF16),
+        pltpu.VMEM((TOKENS, WIDTH), BF16),
+        pltpu.VMEM((TOKENS, WIDTH), F32),
+        pltpu.VMEM((TOKENS, WIDTH), F32),
+        pltpu.VMEM((TOKENS, WIDTH), F32),
+        pltpu.VMEM((HEADS, 1, TOKENS), F32),
+        pltpu.VMEM((TOKENS, 128), BF16),
+        pltpu.VMEM((TOKENS, 128), BF16),
+        pltpu.VMEM((QUERY_ROWS, QUERY_ROWS), F32),
+        pltpu.VMEM((16, WIDTH), F32),
+        pltpu.VMEM((1, QKV), F32),
+        pltpu.VMEM((1, QKV), F32),
+        pltpu.VMEM((16, WIDTH), F32),
+    ]
+    for name, _, width in GATHER_UNITS:
+        scratch += [pltpu.VMEM((padded(SHARD_ROWS[name]), width), BF16)] * 2
+    for unit in SCATTER_UNITS:
+        scratch += ScatterUnit.scratch(unit)
+    scratch += [pltpu.SemaphoreType.DMA((len(GATHER_UNITS), GatherUnit.SEMS))] * 2
+    scratch += [pltpu.SemaphoreType.DMA((len(SCATTER_UNITS), ScatterUnit.SEMS))] * 2
+    scratch += SmallSum.scratch() + SmallSum.scratch()
+    scratch.append(pltpu.SemaphoreType.DMA((2,)))
+    return pl.pallas_call(
+        layer_kernel,
+        name="layer",
+        out_shape=out_shape,
+        in_specs=[vmem] * 8,
+        out_specs=[anywhere] * 2 + [vmem] * 5,
+        scratch_shapes=scratch,
+        compiler_params=pltpu.CompilerParams(collective_id=0, has_side_effects=True, vmem_limit_bytes=VMEM_LIMIT),
+        cost_estimate=pl.CostEstimate(flops=50 * 10**9, bytes_accessed=30 * 10**6, transcendentals=20 * 10**6),
+    )(tokens, documents, cotangent, *[shards[n] for n in NAMES], small)
+
+
+def device_number():
+    return lax.axis_index("dp") * 8 + lax.axis_index("fsdp")
+
+
+def spread(vectors, hidden_vector):
+    number = device_number()
+    stacked = jnp.stack([v.astype(F32) for v in vectors])
+    placed = lax.dynamic_update_slice(jnp.zeros((16, WIDTH), F32), stacked, (0, 24 * number))
+    return lax.dynamic_update_slice(placed, hidden_vector.astype(F32)[None], (8 + number // 8, 96 * (number % 8)))
+
+
+def own_parts(total):
+    number = device_number()
+    parts = lax.dynamic_slice(total[:8], (0, 24 * number), (8, 24))
+    hidden_part = lax.dynamic_slice(total, (8 + number // 8, 96 * (number % 8)), (1, 96))
+    return [parts[i] for i in range(8)], hidden_part[0]
+
+
+def fused_device(
+    tokens,
+    doc_ids,
+    cotangent,
+    first_gain,
+    first_offset,
+    qkv_weight,
+    query_bias,
+    value_bias,
+    out_weight,
+    out_bias,
+    second_gain,
+    second_offset,
+    up_weight,
+    up_bias,
+    down_weight,
+    down_bias,
+):
+    shards = {"qkv": qkv_weight, "out": out_weight, "up": up_weight, "down": down_weight}
+    vectors = (
+        first_gain,
+        first_offset,
+        query_bias,
+        value_bias,
+        out_bias,
+        second_gain,
+        second_offset,
+        down_bias,
+    )
+    layer_out, grad_tokens, *matrices, total = layer(
+        tokens, doc_ids, cotangent, shards, spread(vectors, up_bias)
+    )
+    parts, up_part = own_parts(total)
+    return (
+        layer_out,
+        grad_tokens,
+        parts[0],
+        parts[1],
+        matrices[0],
+        parts[2],
+        parts[3],
+        matrices[1],
+        parts[4],
+        parts[5],
+        parts[6],
+        matrices[2],
+        up_part,
+        matrices[3],
+        parts[7],
+    )
+
+
 def solution(mesh):
     placed = (
         P(("dp", "fsdp"), None),
@@ -294,7 +1203,7 @@
         P(("dp", "fsdp")),
     )
     return jax.shard_map(
-        per_device,
+        fused_device if fits(mesh) else plain_device,
         mesh=mesh,
         in_specs=placed,
         out_specs=(

time: 850 us -> 212 us (0.25)
  waiting for transfers between devices: 408 us -> 0 us
  matrix products: 205 us -> 0 us
  Pallas kernels: 0 us -> 198 us
  blocking collectives: 85 us -> 0 us
  other arithmetic: 64.5 us -> 0.66 us
  local copies, waits for them, and re-layouts: 62.7 us -> 12.1 us
  between operations: 15.3 us -> 0.74 us
    reduce_scatter x4 -> x0, waiting for transfers between devices: 314 us -> none  [the longest x1 142 us: per_device(): lax.psum_scatter(grad_up_weight, ('dp', 'fsdp'), scatter_dimension=0, til...]
    dot_general x24 -> x0, matrix products: 205 us -> none  [the longest x4 34.6 us: contract_rows(): lax.dot_general(former, latter, (((0,), (0,)), ((), ())), preferred_eleme...]
    pallas_call x0 -> x1, Pallas kernels: none -> 198 us  [layer(): pl.pallas_call(layer_kernel, name='layer', out_shape=out_shape, in_specs=...]
    all_gather x4 -> x0, waiting for transfers between devices: 91.3 us -> none  [the longest x1 54.4 us: per_device(): lax.all_gather(down_weight, ('dp', 'fsdp'), axis=0, tiled=True)]
    unnamed x2 -> x0, blocking collectives: 85 us -> none
    convert_element_type x13 -> x0, other arithmetic: 30.5 us -> none  [the longest x2 24.8 us: attend_row_back(): grad_scores = (probs * (grad_probs - inner_sum)).astype(jnp.bfloat16)]
    reduce_sum x11 -> x0, other arithmetic: 29.4 us -> none  [the longest x2 14.5 us: attend_row(): summed = jnp.sum(raised, axis=-1, keepdims=True)]
    unnamed x161 -> x18, local copies, waits for them, and re-layouts: 34 us -> 7.85 us
  transfers between devices with their start and end apart: 8 -> 0, of which waited for: 6 -> 0; matrix products, arithmetic and copies ran while one was open for 30% -> 0% of each run, Pallas kernels for 0% -> 0%
where the time goes in v2:
time: 212 us
  Pallas kernels  198 us (93%)
  local copies, waits for them, and re-layouts  12.1 us (6%)
    pallas_call x1, Pallas kernels, layer(): pl.pallas_call(layer_kernel, name='layer', out_shape=out_shape, in_specs=...  198 us
    unnamed x18, local copies, waits for them, and re-layouts  7.85 us

profile of v2, /device:TPU:0, one launch (start us, length us, event | category | flops | bytes accessed | tf_op | source)
XLA Modules:
  0.0 211.8 jit_solution(11020568965427746385)
XLA Ops:
  0.7 0.7 bitcast_convert_fusion
  1.3 0.8 stack.46
  2.1 0.5 dynamic_update_slice.6
  2.7 0.2 dynamic_update_slice.7.refs_7_
  2.9 0.0 copy-start.5
  2.9 0.6 copy-done.5
  3.5 198.3 %layer.1 = (bf16[1024,768]{1,0:T(8,128)(2,1)}, f32[1024,768]{1,0:T(8,128)}, f32[24,2304]{1,0:T(8,128)}, f32[24,768]{1,0:T(8,128)}, f32[24,3072]{1,0:T(8,128)}, /*index=5*/f32[96,768]{1,0:T(8,128)}, f32[16,768]{1,0:T(8,128)}) custom-call(bf16[1024,768]{1,0:T(8,128)(2,1)} %refs_0_.1, s32[1,1024]{1,0:T(1,128)} %refs_1_.1, bf16[1024,768]{1,0:T(8,128)(2,1)} %refs_2_.1, ...), custom_call_target="tpu_custom_call" | custom-call | flops 49999998976 | bytes 30000000 | tf_op jit(solution)/shard_map/layer/pallas_call | solution.py:1104
  201.9 1.3 dynamic-slice_bitcast_fusion
  203.1 0.7 slice.27
  203.9 0.1 constant_dynamic-slice_fusion
  204.0 0.5 slice_bitcast_fusion
  204.5 0.0 copy-start
  204.5 2.8 %copy.39 = bf16[1024,768]{1,0:T(8,128)(2,1)} copy(bf16[1024,768]{1,0:T(8,128)(2,1)} %get-tuple-element.52) | data formatting | bytes 3145728
  207.3 0.0 copy-done
  207.3 0.0 copy-start.3
  207.3 0.0 copy-start.4
  207.3 0.0 copy-start.2
  207.3 0.0 copy-start.1
  207.3 1.7 copy.40
  209.0 0.0 copy-done.3
  209.0 0.7 copy.41
  209.7 0.0 copy-done.4
  209.7 0.6 copy.42
  210.3 0.0 copy-done.2
  210.3 0.7 copy.43
  211.0 0.0 copy-done.1
  211.0 0.7 copy.44
  (2 shorter events, 0.0 us)
Async XLA Ops:
  2.9 0.6 copy-start.5
  204.5 2.8 %copy-start = (f32[1024,768]{1,0:T(8,128)S(1)}, f32[1024,768]{1,0:T(8,128)}, u32[]{:S(2)}) copy-start(f32[1024,768]{1,0:T(8,128)} %get-tuple-element.53) | copy-start | bytes 9437188
  207.3 1.7 copy-start.3
  207.3 2.4 %copy-start.4 = (f32[24,768]{1,0:T(8,128)S(1)}, f32[24,768]{1,0:T(8,128)}, u32[]{:S(2)}) copy-start(f32[24,768]{1,0:T(8,128)} %get-tuple-element.59) | copy-start | bytes 221188
  207.3 3.0 %copy-start.2 = (f32[24,3072]{1,0:T(8,128)S(1)}, f32[24,3072]{1,0:T(8,128)}, u32[]{:S(2)}) copy-start(f32[24,3072]{1,0:T(8,128)} %get-tuple-element.63) | copy-start | bytes 884740
  207.3 3.7 %copy-start.1 = (f32[96,768]{1,0:T(8,128)S(1)}, f32[96,768]{1,0:T(8,128)}, u32[]{:S(2)}) copy-start(f32[96,768]{1,0:T(8,128)} %get-tuple-element.65) | copy-start | bytes 884740

commit v3 on v2

--- a/solution.py
+++ b/solution.py
@@ -294,43 +294,20 @@
 GELU_A = 0.7978845608028654
 GELU_B = 0.044715
 
-GATHER_UNITS = (
-    ("qkv", 0, 384),
-    ("qkv", 768, 384),
-    ("qkv", 1536, 384),
-    ("out", 0, 384),
-    ("down", 0, 128),
-    ("down", 128, 128),
-    ("down", 256, 128),
-    ("up", 0, 384),
-    ("up", 768, 384),
-    ("up", 1536, 384),
-    ("up", 2304, 384),
+GATHER_UNITS = (("qkv", 0), ("qkv", 1), ("qkv", 2), ("out", 0)) + tuple(
+    (name, part) for part in range(4) for name in ("up", "down")
 )
-SCATTER_UNITS = (
-    ("up", 0, 384),
-    ("up", 768, 384),
-    ("up", 1536, 384),
-    ("up", 2304, 384),
-    ("down", 0, 128),
-    ("down", 128, 128),
-    ("down", 256, 128),
-    ("out", 0, 384),
-    ("qkv", 0, 384),
-    ("qkv", 768, 384),
-    ("qkv", 1536, 384),
-)
-SHARD_ROWS = {"qkv": 24, "out": 24, "up": 24, "down": 96}
-COLUMNS = {"qkv": QKV, "out": WIDTH, "up": HIDDEN, "down": WIDTH}
+SCATTER_UNITS = GATHER_UNITS[4:] + GATHER_UNITS[3:4] + GATHER_UNITS[:3]
+ROWS = 24
+HALF = 384
+SHARDS = {"qkv": (24, 2304), "out": (24, 768), "up": (24, 3072), "down": (96, 768)}
 NAMES = ("qkv", "out", "up", "down")
+DEVICES = 32
+HIDDEN_PARTS = 4
 
 
 def fits(mesh):
     return mesh.shape["dp"] == 4 and mesh.shape["fsdp"] == 8
-
-
-def padded(rows):
-    return -(-rows // 16) * 16
 
 
 def aligned(value, step):
@@ -364,6 +341,7 @@
         self.near = self.dp_x * (1 - core) + self.dp_y * core
         self.next = self.dp_y * (1 - core) + self.dp_x * core
         self.chip = self.dp * 4 + self.z
+        self.number = self.dp * 8 + self.fsdp
         self.partner = (self.dp, self.z * 2 + (1 - core))
         self.at_near = (self.near, self.fsdp)
         self.at_next = (self.next, self.fsdp)
@@ -393,14 +371,15 @@
 
 
 class SmallSum:
-    def __init__(self, place, buffers, landed, sems):
-        self.place, self.buffers, self.landed, self.sems = place, buffers, landed, sems
+    def __init__(self, place, source, target, buffers, landed, send_sems, recv_sems):
+        self.place, self.source, self.target = place, source, target
+        self.buffers, self.landed, self.sems = buffers, landed, (send_sems, recv_sems)
 
     @staticmethod
-    def scratch():
+    def scratch(shape, dtype):
         return [
-            pltpu.VMEM((3, 16, WIDTH), F32),
-            pltpu.VMEM((7, 16, WIDTH), F32),
+            pltpu.VMEM((3, *shape), dtype),
+            pltpu.VMEM((7, *shape), dtype),
             pltpu.SemaphoreType.DMA((7,)),
             pltpu.SemaphoreType.DMA((7,)),
         ]
@@ -419,8 +398,8 @@
             for i, device in enumerate(devices)
         ]
 
-    def begin(self, value):
-        self.buffers[0] = value
+    def begin(self):
+        self.buffers[0] = self.source[...].astype(self.buffers.dtype)
         for copy in self.copies(0):
             copy.start()
 
@@ -431,7 +410,7 @@
         for copy in self.copies(1):
             copy.start()
 
-    def last(self):
+    def later(self):
         for copy in self.copies(1):
             copy.wait()
         self.buffers[2] = (self.buffers[1] + self.landed[1]) + (self.landed[2] + self.landed[3])
@@ -441,7 +420,8 @@
     def end(self):
         for copy in self.copies(2):
             copy.wait()
-        return (self.buffers[2] + self.landed[4]) + (self.landed[5] + self.landed[6])
+        total = (self.buffers[2] + self.landed[4]) + (self.landed[5] + self.landed[6])
+        self.target[...] = total.astype(self.target.dtype)
 
 
 class GatherUnit:
@@ -449,29 +429,30 @@
 
     def __init__(self, place, unit, shard, full, pair_out, pair_in, send_sems, recv_sems):
         self.place = place
-        self.name, self.first, self.width = unit
-        self.rows = SHARD_ROWS[self.name]
+        self.name, self.part = unit
         self.shard, self.full = shard, full
         self.pair_out, self.pair_in = pair_out, pair_in
         self.sems = (send_sems, recv_sems)
 
-    def part_of(self, core):
-        if self.name != "qkv":
-            return self.shard[:, pl.ds(aligned(self.first + 384 * core, 128), self.width)]
-        start = self.first // 3 + 128 * core
-        parts = [self.shard[:, pl.ds(aligned(start + WIDTH * i, 128), 128)] for i in range(3)]
-        return jnp.concatenate(parts, axis=1)
-
-    def columns(self):
-        return pl.ds(aligned(self.first + 384 * self.place.core, 128), self.width)
+    def columns_of(self, core):
+        if self.name == "qkv":
+            start = 2 * self.part * 128 + 128 * core
+            parts = [self.shard[:, pl.ds(aligned(start + WIDTH * i, 128), 128)] for i in range(3)]
+            return jnp.concatenate(parts, axis=1).astype(F32)
+        start = WIDTH * self.part if self.name == "up" else 0
+        columns = self.shard[:, pl.ds(aligned(start + HALF * core, 128), HALF)].astype(F32)
+        return columns[ROWS * self.part : ROWS * self.part + ROWS] if self.name == "down" else columns
+
+    def rows_at(self, first, count):
+        columns = pl.ds(aligned(HALF * self.place.core, 128), HALF)
+        return self.full.at[pl.ds(aligned(first, 16), count), columns]
 
     def group(self, dp):
-        rows = 8 * self.rows
-        return self.full.at[pl.ds(aligned(dp * rows, 16), rows), self.columns()]
-
-    def block(self):
-        rows = 2 * self.rows
-        return self.full.at[pl.ds(aligned(self.place.chip * rows, 16), rows), self.columns()]
+        return self.rows_at(dp * (8 * ROWS), 8 * ROWS)
+
+    def block(self, dp=None):
+        chip = self.place.chip if dp is None else dp * 4 + self.place.z
+        return self.rows_at(chip * (2 * ROWS), 2 * ROWS)
 
     def copy(self, index):
         p = self.place
@@ -492,28 +473,29 @@
             self.copy(index).wait_recv()
 
     def pair(self):
-        self.pair_out[0 : self.rows] = self.part_of(1 - self.place.core)
-        if self.rows % 16:
-            rest = padded(self.rows) - self.rows
-            self.pair_out[self.rows :] = jnp.zeros((rest, self.width), BF16)
+        self.pair_out[0:ROWS] = self.columns_of(1 - self.place.core).astype(BF16)
+        self.pair_out[ROWS:] = jnp.zeros((32 - ROWS, HALF), BF16)
         self.start(0)
 
-    def along_z(self):
+    def assemble(self):
         self.landed(0)
-        own = self.part_of(self.place.core).astype(F32)
-        came = self.pair_in[0 : self.rows].astype(F32)
+        own = self.columns_of(self.place.core)
+        came = self.pair_in[0:ROWS].astype(F32)
         first = self.place.core == 0
         block = jnp.concatenate([jnp.where(first, own, came), jnp.where(first, came, own)], axis=0)
         self.block()[...] = block.astype(BF16)
+
+    def along_z(self):
+        self.assemble()
         self.start(1, 2, 3)
 
     def to_near(self):
         self.landed(1, 2, 3)
-        self.start(4, 5, 7)
+        self.start(4, 7)
 
     def to_next(self):
         self.landed(4)
-        self.start(6, 8)
+        self.start(5, 6, 8)
 
     def to_core(self):
         self.landed(5)
@@ -534,42 +516,36 @@
 
     def __init__(self, place, unit, partial, target, halves, from_next, from_near, from_z, pair, send_sems, recv_sems):
         self.place = place
-        self.name, self.first, self.width = unit
-        self.rows = SHARD_ROWS[self.name]
+        self.name, self.part = unit
         self.partial, self.target = partial, target
         self.halves, self.from_next, self.from_near = halves, from_next, from_near
         self.from_z, self.pair_buffer = from_z, pair
         self.sems = (send_sems, recv_sems)
 
     @staticmethod
-    def scratch(unit):
-        name, _, width = unit
-        rows = SHARD_ROWS[name]
+    def scratch():
         return [
-            pltpu.VMEM((32 * rows, width), BF16),
-            pltpu.VMEM((2, 8 * rows, width), BF16),
-            pltpu.VMEM((8 * rows, width), BF16),
-            pltpu.VMEM((3, 2 * rows, width), BF16),
-            pltpu.VMEM((3, rows, width), F32),
+            pltpu.VMEM((WIDTH, HALF), BF16),
+            pltpu.VMEM((2, 8 * ROWS, HALF), BF16),
+            pltpu.VMEM((8 * ROWS, HALF), BF16),
+            pltpu.VMEM((3, 2 * ROWS, HALF), BF16),
+            pltpu.VMEM((3, ROWS, HALF), F32),
         ]
 
     def columns(self, core):
-        first = 0 if self.name == "qkv" else self.first
-        return pl.ds(aligned(first + 384 * core, 128), self.width)
+        return pl.ds(aligned(HALF * core, 128), HALF)
 
     def group(self, dp):
-        rows = 8 * self.rows
-        return self.halves.at[pl.ds(aligned(dp * rows, 16), rows)]
-
-    def z_block(self, step):
-        z = lax.rem(self.place.z + step, 4)
-        rows = 2 * self.rows
-        return self.halves.at[pl.ds(aligned((self.place.dp * 4 + z) * rows, 16), rows)]
+        return self.halves.at[pl.ds(aligned(dp * (8 * ROWS), 16), 8 * ROWS)]
+
+    def z_block(self, step, dp=None):
+        chip = (self.place.dp if dp is None else dp) * 4 + lax.rem(self.place.z + step, 4)
+        return self.halves.at[pl.ds(aligned(chip * (2 * ROWS), 16), 2 * ROWS)]
 
     def copy(self, index):
         p = self.place
         if index == 0:
-            source = self.partial.at[pl.ds(0, 32 * self.rows), self.columns(1 - p.core)]
+            source = self.partial.at[pl.ds(0, WIDTH), self.columns(1 - p.core)]
             return remote(source, self.halves, self.sems, 0, p.partner)
         if index < 3:
             dp = (p.next, p.dp_far)[index - 1]
@@ -605,41 +581,48 @@
     def to_next(self):
         self.landed(0)
         mine = self.columns(self.place.core)
-        self.add(self.halves, lambda at: self.partial[at, mine], 32 * self.rows)
+        self.add(self.halves, lambda at: self.partial[at, mine], WIDTH)
         self.start(1, 2)
 
     def to_near(self):
         p = self.place
         self.landed(1, 2)
-        self.add(self.group(p.near), lambda at: self.from_next[1, at], 8 * self.rows)
+        self.add(self.group(p.near), lambda at: self.from_next[1, at], 8 * ROWS)
         self.start(3)
-        self.add(self.group(p.dp), lambda at: self.from_next[0, at], 8 * self.rows)
+        self.add(self.group(p.dp), lambda at: self.from_next[0, at], 8 * ROWS)
 
     def along_z(self):
         self.landed(3)
-        self.add(self.group(self.place.dp), lambda at: self.from_near[at], 8 * self.rows)
+        self.add(self.group(self.place.dp), lambda at: self.from_near[at], 8 * ROWS)
         self.start(4, 5, 6)
 
     def to_pair(self):
         self.landed(4, 5, 6)
-        rows = self.rows
         came = [self.from_z[i].astype(F32) for i in range(3)]
-        block = (self.z_block(0)[...].astype(F32) + came[0]) + (came[1] + came[2])
+        self.halve((self.z_block(0)[...].astype(F32) + came[0]) + (came[1] + came[2]))
+        self.start(7)
+
+    def halve(self, block):
         first = self.place.core == 0
-        self.pair_buffer[0] = jnp.where(first, block[rows:], block[:rows])
-        self.pair_buffer[1] = jnp.where(first, block[:rows], block[rows:])
-        self.start(7)
+        self.pair_buffer[0] = jnp.where(first, block[ROWS:], block[:ROWS])
+        self.pair_buffer[1] = jnp.where(first, block[:ROWS], block[ROWS:])
 
     def store(self):
         self.landed(7)
+        self.put()
+
+    def put(self):
         for source, core in ((1, self.place.core), (2, 1 - self.place.core)):
-            if self.name != "qkv":
-                self.target[:, self.columns(core)] = self.pair_buffer[source]
-                continue
-            start = self.first // 3 + 128 * core
-            for i in range(3):
-                columns = pl.ds(aligned(start + WIDTH * i, 128), 128)
-                self.target[:, columns] = self.pair_buffer[source, :, 128 * i : 128 * i + 128]
+            if self.name == "qkv":
+                start = 2 * self.part * 128 + 128 * core
+                for i in range(3):
+                    columns = pl.ds(aligned(start + WIDTH * i, 128), 128)
+                    self.target[:, columns] = self.pair_buffer[source, :, 128 * i : 128 * i + 128]
+            elif self.name == "down":
+                self.target[ROWS * self.part : ROWS * self.part + ROWS, self.columns(core)] = self.pair_buffer[source]
+            else:
+                start = WIDTH * self.part + HALF * core
+                self.target[:, pl.ds(aligned(start, 128), HALF)] = self.pair_buffer[source]
 
     def finish(self):
         for index in range(self.SEMS):
@@ -653,17 +636,17 @@
     "Z": "along_z",
     "D": "to_pair",
     "S": "store",
+    "p": "pair",
     "z": "along_z",
     "n": "to_near",
     "x": "to_next",
     "c": "to_core",
     "r": "arrived",
+    "b": "begin",
+    "m": "middle",
+    "l": "later",
+    "e": "end",
 }
-
-
-def run_stages(units, text):
-    for step in text.split():
-        getattr(units[int(step[1:])], STAGES[step[0]])()
 
 
 def strips(body, carry=0):
@@ -786,6 +769,60 @@
     value_sum[newest] = value_part[inside:]
 
 
+PLAN = {
+    "greet": "b0 p0 p1 p2",
+    "packed": "m0 z0 p3 p4 p5",
+    "group0": "n0 z3 p6 n1 z4 p7 x0 n2 z5 p8 x1 n3 z6 p9 c0 x2 n4 z7 p10 r0",
+    "pair0": "x3",
+    "pair1": "c1 x4",
+    "group1": "n5 z8 p11 n6 z9 r1",
+    "qkv1": "c2",
+    "pair2": "n7 z10",
+    "pair3": "c3 x5",
+    "group2": "r2",
+    "qkv2": "x6",
+    "pair5": "c4 x7",
+    "joined": "r3",
+    "branch": "n8 z11",
+    "norm": "c5 n9 n10",
+    "step0": "r4 r5",
+    "hidden0": "c6 x8 x9",
+    "outer0": "c7 n11",
+    "grads0": "x10 P0 P1",
+    "step1": "r6 r7",
+    "hidden1": "c8 x11 A0",
+    "outer1": "c9 A1",
+    "grads1": "c10 P2 P3",
+    "step2": "r8 r9",
+    "hidden2": "c11 A2 A3",
+    "outer2": "B0",
+    "grads2": "B1 P4 P5",
+    "step3": "r10 r11",
+    "hidden3": "Z0 B2 A4 A5",
+    "outer3": "Z1",
+    "grads3": "D0 Z2 B3 P6 P7",
+    "back": "D1 B4 S0 A6 A7",
+    "attended": "D2 Z3 S1",
+    "out": "S2 P8",
+    "first": "Z4 B5 A8 b1",
+    "pair_back0": "D3 B6 m1",
+    "pair_back1": "D4 Z5 B7 S3 l1",
+    "qkv_grads0": "Z6 S4 P9",
+    "pair_back2": "D5 Z7 B8 A9 e1",
+    "pair_back3": "D6 S5",
+    "qkv_grads1": "Z8 D7 S6 P10",
+    "pair_back4": "B9 S7 A10",
+    "pair_back5": "D8",
+    "qkv_grads2": "Z9 S8 P11",
+    "tokens0": "B10",
+    "tokens1": "A11",
+    "half": "b2 D9 Z10",
+    "last": "m2 S9 B11 l2 Z11 D10 S10 D11 S11 e2",
+    "documents": "l0 z1 z2",
+    "vectors": "e0",
+}
+
+
 def layer_kernel(*refs):
     refs = list(refs)
 
@@ -794,43 +831,53 @@
         del refs[:count]
         return taken
 
-    tokens, documents, cotangent = take(3)
+    tokens_in, documents, cotangent_in = take(3)
     shards = dict(zip(NAMES, take(4)))
-    (small,) = take(1)
+    (packed,) = take(1)
     layer_out, grad_tokens = take(2)
     targets = dict(zip(NAMES, take(4)))
     (small_out,) = take(1)
-    weights = dict(zip(NAMES, take(4)))
-    wq, wo, wu, wd = (weights[name] for name in NAMES)
-    wide, norm, norm_t, attended, seed, act, act_t, slope = take(8)
+    wq, wo, wu, wd = take(4)
+    tokens, cotangent, wide, norm, norm_t, attended, seed, act, act_t, slope = take(10)
     middle, outer, grad_norm = take(3)
-    logsums, query_side, key_side, causal, vectors, qkv_bias, qkv_scale, sums = take(8)
+    logsums, query_side, key_side, causal, vectors, qkv_bias, qkv_scale, early = take(8)
+    late, up_shard, up_target = take(3)
     pair_buffers = take(2 * len(GATHER_UNITS))
     scatter_buffers = take(5 * len(SCATTER_UNITS))
     gather_sems, scatter_sems = take(2), take(2)
-    first_small, last_small = take(4), take(4)
+    small_refs = [take(4) for _ in range(3)]
     (local_sems,) = take(1)
 
     place = Place()
+    up_natural, shards["up"] = shards["up"], up_shard
+    up_out, targets["up"] = targets["up"], up_target
+
+    def part(index):
+        return slice(WIDTH * index, WIDTH * index + WIDTH)
+
+    def whole(name, index):
+        if name == "out":
+            return wo
+        return wd.at[part(index)] if name == "down" else {"qkv": wq, "up": wu}[name].at[:, part(index)]
+
     coming = [
         GatherUnit(
             place,
             unit,
             shards[unit[0]],
-            weights[unit[0]],
+            whole(*unit),
             *pair_buffers[2 * i : 2 * i + 2],
             gather_sems[0].at[i],
             gather_sems[1].at[i],
         )
         for i, unit in enumerate(GATHER_UNITS)
     ]
-    partials = {"up": wu, "down": wd, "out": wo}
-    qkv_partials = (slope, act_t, norm)
+    qkv_partials = (slope.at[0:WIDTH], act_t.at[:, 0:WIDTH], norm.at[0:WIDTH])
     leaving = [
         ScatterUnit(
             place,
             unit,
-            partials[unit[0]] if unit[0] != "qkv" else qkv_partials[unit[1] // WIDTH],
+            qkv_partials[unit[1]] if unit[0] == "qkv" else whole(*unit),
             targets[unit[0]],
             *scatter_buffers[5 * i : 5 * i + 5],
             scatter_sems[0].at[i],
@@ -839,26 +886,50 @@
         for i, unit in enumerate(SCATTER_UNITS)
     ]
 
-    def gathering(text):
-        run_stages(coming, text)
-
-    def scattering(text):
-        run_stages(leaving, text)
-
+    vector_sums = [
+        SmallSum(place, source, target, *refs)
+        for source, target, refs in zip((vectors, early, late), (vectors, early, late), small_refs)
+    ]
+
+    def run(text):
+        for step in text.split():
+            units = vector_sums if step[0] in "bmle" else coming if step[0].islower() else leaving
+            getattr(units[int(step[1:])], STAGES[step[0]])()
+
+    def after(name, index=None, count=0):
+        if index is None:
+            run(PLAN.get(name, ""))
+            return
+        for number in range(count):
+            text = PLAN.get(name + str(number), "")
+            if text:
+                pl.when(index == number)(lambda text=text: run(text))
+
+    loads = [
+        pltpu.make_async_copy(source, target, local_sems.at[2 + i])
+        for i, (source, target) in enumerate(((tokens_in, tokens), (cotangent_in, cotangent)))
+    ]
+    for load in loads:
+        load.start()
+    vectors[...] = jnp.zeros_like(vectors)
+    for row in range(12):
+        vectors[row : row + 1, 0:ROWS] = packed[:, ROWS * row : ROWS * row + ROWS]
+    vectors[...] = pltpu.roll(vectors[...], place.number * ROWS, 1)
     place.greet()
-    total = SmallSum(place, first_small[0], first_small[1], first_small[2:])
-    total.begin(small[...])
-    for unit in coming:
-        unit.pair()
-    gathering("z0")
-    total.middle()
-    gathering("z1")
-    total.last()
-    gathering("z2 n0")
+    after("greet")
+    up = up_natural[...].astype(F32)
+    step = ROWS * HIDDEN_PARTS
+    up_shard[...] = jnp.concatenate(
+        [up[:, step * d + ROWS * j : step * d + ROWS * j + ROWS] for j in range(HIDDEN_PARTS) for d in range(DEVICES)],
+        axis=1,
+    ).astype(BF16)
+    after("packed")
     document_lanes(documents[...], query_side, key_side)
     causal_corner(causal)
-    vectors[...] = total.end()
-    gathering("x0 n1 z3")
+    after("documents")
+    for load in loads:
+        load.wait()
+    after("vectors")
     gain_one, offset_one = vectors[0:1], vectors[1:2]
     for pair in range(PAIRS):
         at = slice(128 * pair, 128 * pair + 128)
@@ -875,33 +946,33 @@
         return carry
 
     strips(norm_one)
-    gathering("c0 x1 n2 z4")
+    after("one")
 
     def forward_group(group, carry):
-        for number, text in enumerate(("r0", "c1 x2 n3 z5 r1", "c3 x4 n5 z7 r2")):
-            pl.when(group == number)(lambda text=text: gathering(text))
+        after("group", group, 3)
         for n in range(3):
             columns = pl.ds(aligned(group * WIDTH + n * TILE, 128), TILE)
             projected = dot_nn(norm[...], wq[:, columns]) + qkv_bias[:, columns]
             wide[:, columns] = (projected * qkv_scale[:, columns]).astype(BF16)
+        after("qkv", group, 3)
 
         def forward_pair(half, carry):
             pair = 2 * group + half
             for block in range(4):
                 attend(wide, pair, block, query_side, key_side, causal, attended, logsums)
-            for number, text in ((2, "c2 x3 n4 z6"), (4, "c4 x5 n6 z8 r3"), (5, "c5 x6 n7 z9")):
-                pl.when(pair == number)(lambda text=text: gathering(text))
+            after("pair", pair, PAIRS)
             return carry
 
         return lax.fori_loop(0, 2, forward_pair, carry)
 
     lax.fori_loop(0, 3, forward_group, 0)
 
+    after("joined")
     for n in range(3):
         at = slice(n * TILE, n * TILE + TILE)
         branch = dot_nn(attended[...], wo[:, at]) + vectors[4:5, at]
         middle[:, at] = tokens[:, at].astype(F32) + branch_scale * branch
-    gathering("c6 x7 n8 z10 r4")
+    after("branch")
     gain_two, offset_two = vectors[5:6], vectors[6:7]
 
     def norm_two(rows, down_bias):
@@ -913,12 +984,14 @@
         grad_norm[rows] = jnp.zeros((STRIP, WIDTH), F32)
         return down_bias + column_sum(scaled.astype(F32))
 
-    sums[7:8] = strips(norm_two, jnp.zeros((1, WIDTH), F32))
+    early[3:4] = strips(norm_two, jnp.zeros((1, WIDTH), F32))
     norm_t[0:WIDTH] = norm[...].T
     norm_t[WIDTH:] = jnp.ones((16, TOKENS), BF16)
-    gathering("c7 x8 n9 r5 r6 r7")
+    after("norm")
 
     def feed_forward(step, carry):
+        here = pl.ds(aligned(step * WIDTH, 128), WIDTH)
+        after("step", step, 4)
         for n in range(3):
             at = slice(n * TILE, n * TILE + TILE)
             columns = pl.ds(aligned(step * WIDTH + n * TILE, 128), TILE)
@@ -928,33 +1001,27 @@
             active, bent = gelu_and_slope(hidden)
             act[:, at] = active.astype(BF16)
             slope[:, at] = (grad_active * bent).astype(BF16)
-        here = pl.ds(aligned(step * WIDTH, 128), WIDTH)
+        after("hidden", step, 4)
         for n in range(3):
             at = slice(n * TILE, n * TILE + TILE)
             outer[:, at] += dot_nn(act[...], wd[here, at])
             grad_norm[:, at] += dot_nt(slope[...], wu[at, here])
-        for number, text in enumerate(("c8 x9 n10", "c9 x10", "c10", "")):
-            pl.when(step == number)(lambda text=text: gathering(text))
+        after("outer", step, 4)
         for number in range(4):
-            def own_columns(number=number):
-                coming[7 + number].finish()
-                if number == 0:
-                    for unit in coming[:7]:
-                        unit.finish()
-
-            pl.when(step == number)(own_columns)
+            def sent(number=number):
+                for unit in coming[4 + 2 * number : 6 + 2 * number]:
+                    unit.finish()
+
+            pl.when(step == number)(sent)
         act_t[...] = act[...].T
         for n in range(3):
             at = slice(n * TILE, n * TILE + TILE)
             columns = pl.ds(aligned(step * WIDTH + n * TILE, 128), TILE)
             grad = dot_nn(norm_t[...], slope[:, at])
             wu[:, columns] = grad[:WIDTH].astype(BF16)
-            sums[pl.ds(8 + step, 1), at] = grad[WIDTH : WIDTH + 1]
+            early[pl.ds(4 + step, 1), at] = grad[WIDTH : WIDTH + 1]
             wd[here, at] = dot_nn(act_t[...], seed[:, at]).astype(BF16)
-        for number, text in enumerate(("P0", "P1 A0", "B0 A1 P2", "Z0 B1 A2 P3 P4")):
-            pl.when(step == number)(lambda text=text: scattering(text))
-        for number, text in enumerate(("r8", "r9", "r10", "")):
-            pl.when(step == number)(lambda text=text: gathering(text))
+        after("grads", step, 4)
         return carry
 
     lax.fori_loop(0, 4, feed_forward, 0)
@@ -972,33 +1039,28 @@
         return tuple(former + part for former, part in zip(carry, parts))
 
     zero = jnp.zeros((1, WIDTH), F32)
-    sums[4:5], sums[5:6], sums[6:7] = strips(back_two, (zero, zero, zero))
+    early[0:1], early[1:2], early[2:3] = strips(back_two, (zero, zero, zero))
     out_copy = pltpu.make_async_copy(slope, layer_out, local_sems.at[0])
     out_copy.start()
-    scattering("D0 Z1 B2 A3 P5")
+    after("back")
 
     for n in range(3):
         at = slice(n * TILE, n * TILE + TILE)
         act[:, at] = dot_nt(seed[...], wo[at]).astype(BF16)
-    scattering("S0 D1 Z2 B3 A4 P6")
+    after("attended")
+    for unit in coming[:4]:
+        unit.finish()
     act_t[...] = attended[...].T
     for n in range(3):
         at = slice(n * TILE, n * TILE + TILE)
         wo[:, at] = dot_nn(act_t[...], seed[:, at]).astype(BF16)
-    scattering("S1 D2 Z3 B4 A5 P7")
+    after("out")
     strips(norm_one)
     norm_t[0:WIDTH] = norm[...].T
     out_copy.wait()
+    after("first")
 
     key_sum, value_sum = outer.at[:, 0:128], outer.at[:, 128:256]
-    pair_texts = (
-        "S2 D3 Z4 B5 A6",
-        "S3 D4 Z5 B6 A7",
-        "S4 D5 Z6 B7",
-        "S5 D6 Z7 A8",
-        "S6 D7 B8",
-        "S7 Z8 A9",
-    )
 
     def backward_group(group, carry):
         def backward_pair(half, carry):
@@ -1010,26 +1072,24 @@
             first = pair * 384
             wide[:, pl.ds(aligned(first + 128, 128), 128)] = key_sum[...].astype(BF16)
             wide[:, pl.ds(aligned(first + 256, 128), 128)] = value_sum[...].astype(BF16)
-            for number, text in enumerate(pair_texts):
-                pl.when(pair == number)(lambda text=text: scattering(text))
+            after("pair_back", pair, PAIRS)
             return carry
 
         lax.fori_loop(0, 2, backward_pair, carry)
         for number in range(3):
             def weight_grads(number=number):
-                partial = qkv_partials[number]
                 rows = []
                 for n in range(3):
                     at = slice(n * TILE, n * TILE + TILE)
                     columns = slice(number * WIDTH + n * TILE, number * WIDTH + n * TILE + TILE)
                     grad = dot_nn(norm_t[...], wide[:, columns])
-                    partial[0:WIDTH, at] = grad[:WIDTH].astype(BF16)
+                    qkv_partials[number][:, at] = grad[:WIDTH].astype(BF16)
                     rows.append(grad[WIDTH : WIDTH + 1])
                 row = jnp.concatenate(rows, axis=1)
                 at = slice(number * 256, number * 256 + 256)
-                sums[2:3, at] = jnp.concatenate([row[:, 0:128], row[:, 384:512]], axis=1)
-                sums[3:4, at] = jnp.concatenate([row[:, 256:384], row[:, 640:768]], axis=1)
-                scattering(("P8", "P9", "P10")[number])
+                late[2:3, at] = jnp.concatenate([row[:, 0:128], row[:, 384:512]], axis=1)
+                late[3:4, at] = jnp.concatenate([row[:, 256:384], row[:, 640:768]], axis=1)
+                after("qkv_grads" + str(number))
 
             pl.when(group == number)(weight_grads)
         return carry
@@ -1039,7 +1099,7 @@
     for n in range(3):
         at = slice(n * TILE, n * TILE + TILE)
         grad_norm[:, at] = dot_nt(wide[...], wq[at])
-    scattering("D8 B9 A10")
+        after("tokens" + str(n))
 
     def back_one(rows, carry):
         xhat, scale = standardized(tokens[rows].astype(F32))
@@ -1047,32 +1107,42 @@
         middle[rows] += back_through_norm(grad, xhat, scale, gain_one)
         return carry[0] + column_sum(grad * xhat), carry[1] + column_sum(grad)
 
-    sums[0:1], sums[1:2] = strips(back_one, (zero, zero))
+    late[0:1], late[1:2] = strips(back_one, (zero, zero))
     tokens_copy = pltpu.make_async_copy(middle, grad_tokens, local_sems.at[1])
     tokens_copy.start()
-    sums[12:16] = jnp.zeros((4, WIDTH), F32)
-    total = SmallSum(place, last_small[0], last_small[1], last_small[2:])
-    total.begin(sums[...])
-    scattering("S8 Z9 B10")
-    total.middle()
-    scattering("D9 Z10")
-    total.last()
-    scattering("S9 D10")
-    small_out[...] = total.end()
-    scattering("S10")
+    after("half")
+    up = up_target[...]
+    up_out[...] = jnp.concatenate(
+        [
+            up[:, WIDTH * j + ROWS * d : WIDTH * j + ROWS * d + ROWS]
+            for d in range(DEVICES)
+            for j in range(HIDDEN_PARTS)
+        ],
+        axis=1,
+    )
+    after("last")
+    back = lax.rem(DEVICES - place.number, DEVICES) * ROWS
+    small_out[0:8] = pltpu.roll(early[...], back, 1)[:, 0:128]
+    small_out[8:12] = pltpu.roll(late[...], back, 1)[:, 0:128]
+    small_out[12:16] = jnp.zeros((4, 128), F32)
     for unit in leaving:
         unit.finish()
     tokens_copy.wait()
 
 
-def layer(tokens, documents, cotangent, shards, small):
+def layer(tokens, documents, cotangent, shards, packed):
     vmem = pl.BlockSpec(memory_space=pltpu.VMEM)
     anywhere = pl.BlockSpec(memory_space=pl.ANY)
     out_shape = [jax.ShapeDtypeStruct((TOKENS, WIDTH), BF16), jax.ShapeDtypeStruct((TOKENS, WIDTH), F32)]
-    out_shape += [jax.ShapeDtypeStruct((SHARD_ROWS[n], COLUMNS[n]), F32) for n in NAMES]
-    out_shape.append(jax.ShapeDtypeStruct((16, WIDTH), F32))
-    scratch = [pltpu.VMEM((32 * SHARD_ROWS[n], COLUMNS[n]), BF16) for n in NAMES]
-    scratch += [
+    out_shape += [jax.ShapeDtypeStruct(SHARDS[n], F32) for n in NAMES]
+    out_shape.append(jax.ShapeDtypeStruct((16, 128), F32))
+    scratch = [
+        pltpu.VMEM((WIDTH, QKV), BF16),
+        pltpu.VMEM((WIDTH, WIDTH), BF16),
+        pltpu.VMEM((WIDTH, HIDDEN), BF16),
+        pltpu.VMEM((HIDDEN, WIDTH), BF16),
+        pltpu.VMEM((TOKENS, WIDTH), BF16),
+        pltpu.VMEM((TOKENS, WIDTH), BF16),
         pltpu.VMEM((TOKENS, QKV), BF16),
         pltpu.VMEM((TOKENS, WIDTH), BF16),
         pltpu.VMEM((WIDTH + 16, TOKENS), BF16),
@@ -1091,44 +1161,63 @@
         pltpu.VMEM((16, WIDTH), F32),
         pltpu.VMEM((1, QKV), F32),
         pltpu.VMEM((1, QKV), F32),
-        pltpu.VMEM((16, WIDTH), F32),
+        pltpu.VMEM((8, WIDTH), F32),
+        pltpu.VMEM((4, WIDTH), F32),
+        pltpu.VMEM(SHARDS["up"], BF16),
+        pltpu.VMEM(SHARDS["up"], F32),
     ]
-    for name, _, width in GATHER_UNITS:
-        scratch += [pltpu.VMEM((padded(SHARD_ROWS[name]), width), BF16)] * 2
-    for unit in SCATTER_UNITS:
-        scratch += ScatterUnit.scratch(unit)
+    scratch += [pltpu.VMEM((32, HALF), BF16)] * (2 * len(GATHER_UNITS))
+    for _ in SCATTER_UNITS:
+        scratch += ScatterUnit.scratch()
     scratch += [pltpu.SemaphoreType.DMA((len(GATHER_UNITS), GatherUnit.SEMS))] * 2
     scratch += [pltpu.SemaphoreType.DMA((len(SCATTER_UNITS), ScatterUnit.SEMS))] * 2
-    scratch += SmallSum.scratch() + SmallSum.scratch()
-    scratch.append(pltpu.SemaphoreType.DMA((2,)))
+    for shape, dtype in (((16, WIDTH), BF16), ((8, WIDTH), F32), ((4, WIDTH), F32)):
+        scratch += SmallSum.scratch(shape, dtype)
+    scratch.append(pltpu.SemaphoreType.DMA((4,)))
     return pl.pallas_call(
         layer_kernel,
         name="layer",
         out_shape=out_shape,
-        in_specs=[vmem] * 8,
+        in_specs=[anywhere, vmem, anywhere] + [vmem] * 5,
         out_specs=[anywhere] * 2 + [vmem] * 5,
         scratch_shapes=scratch,
         compiler_params=pltpu.CompilerParams(collective_id=0, has_side_effects=True, vmem_limit_bytes=VMEM_LIMIT),
         cost_estimate=pl.CostEstimate(flops=50 * 10**9, bytes_accessed=30 * 10**6, transcendentals=20 * 10**6),
-    )(tokens, documents, cotangent, *[shards[n] for n in NAMES], small)
-
-
-def device_number():
-    return lax.axis_index("dp") * 8 + lax.axis_index("fsdp")
-
-
-def spread(vectors, hidden_vector):
-    number = device_number()
-    stacked = jnp.stack([v.astype(F32) for v in vectors])
-    placed = lax.dynamic_update_slice(jnp.zeros((16, WIDTH), F32), stacked, (0, 24 * number))
-    return lax.dynamic_update_slice(placed, hidden_vector.astype(F32)[None], (8 + number // 8, 96 * (number % 8)))
-
-
-def own_parts(total):
-    number = device_number()
-    parts = lax.dynamic_slice(total[:8], (0, 24 * number), (8, 24))
-    hidden_part = lax.dynamic_slice(total, (8 + number // 8, 96 * (number % 8)), (1, 96))
-    return [parts[i] for i in range(8)], hidden_part[0]
+    )(tokens, documents, cotangent, *[shards[n] for n in NAMES], packed)
+
+
+def results_kernel(*refs):
+    sources, parts, targets, vectors = refs[:6], refs[6], refs[7:13], refs[13:22]
+    held, (sems_in, sems_out) = refs[22:28], refs[28:]
+    copies_in = [pltpu.make_async_copy(a, b, sems_in.at[i]) for i, (a, b) in enumerate(zip(sources, held))]
+    copies_out = [pltpu.make_async_copy(a, b, sems_out.at[i]) for i, (a, b) in enumerate(zip(held, targets))]
+    for copy in copies_in:
+        copy.start()
+    for target, row in zip(vectors, (8, 9, 10, 11, 0, 1, 2, 3)):
+        target[...] = parts[row, 0:ROWS]
+    vectors[8][...] = jnp.concatenate([parts[4 + j : 5 + j, 0:ROWS] for j in range(HIDDEN_PARTS)], axis=1)[0]
+    for copy_in, copy_out in zip(copies_in, copies_out):
+        copy_in.wait()
+        copy_out.start()
+    for copy in copies_out:
+        copy.wait()
+
+
+def results(arrays, parts):
+    vmem = pl.BlockSpec(memory_space=pltpu.VMEM)
+    anywhere = pl.BlockSpec(memory_space=pl.ANY)
+    out_shape = [jax.ShapeDtypeStruct(a.shape, a.dtype) for a in arrays]
+    out_shape += [jax.ShapeDtypeStruct((ROWS,), F32)] * 8 + [jax.ShapeDtypeStruct((ROWS * HIDDEN_PARTS,), F32)]
+    scratch = [pltpu.VMEM(a.shape, a.dtype) for a in arrays]
+    return pl.pallas_call(
+        results_kernel,
+        name="results",
+        out_shape=out_shape,
+        in_specs=[anywhere] * 6 + [vmem],
+        out_specs=[anywhere] * 6 + [vmem] * 9,
+        scratch_shapes=scratch + [pltpu.SemaphoreType.DMA((6,))] * 2,
+        compiler_params=pltpu.CompilerParams(vmem_limit_bytes=VMEM_LIMIT),
+    )(*arrays, parts)
 
 
 def fused_device(
@@ -1159,27 +1248,28 @@
         second_gain,
         second_offset,
         down_bias,
-    )
-    layer_out, grad_tokens, *matrices, total = layer(
-        tokens, doc_ids, cotangent, shards, spread(vectors, up_bias)
-    )
-    parts, up_part = own_parts(total)
+        up_bias,
+        jnp.zeros((96,), BF16),
+    )
+    packed = jnp.concatenate(vectors).astype(F32)[None]
+    *arrays, parts = layer(tokens, doc_ids, cotangent, shards, packed)
+    layer_out, grad_tokens, grad_qkv, grad_out, grad_up, grad_down, *small = results(arrays, parts)
     return (
         layer_out,
         grad_tokens,
-        parts[0],
-        parts[1],
-        matrices[0],
-        parts[2],
-        parts[3],
-        matrices[1],
-        parts[4],
-        parts[5],
-        parts[6],
-        matrices[2],
-        up_part,
-        matrices[3],
-        parts[7],
+        small[0],
+        small[1],
+        grad_qkv,
+        small[2],
+        small[3],
+        grad_out,
+        small[4],
+        small[5],
+        small[6],
+        grad_up,
+        small[8],
+        grad_down,
+        small[7],
     )
 
 

time: 212 us -> 178 us (0.84)
  Pallas kernels: 198 us -> 175 us
  local copies, waits for them, and re-layouts: 12.1 us -> 0.89 us
    pallas_call x1, Pallas kernels: 198 us -> 169 us  [layer(): pl.pallas_call(layer_kernel, name='layer', out_shape=out_shape, in_specs=...]
    unnamed x18 -> x0, local copies, waits for them, and re-layouts: 7.85 us -> none
    pallas_call x0 -> x1, Pallas kernels: none -> 5.65 us  [results(): pl.pallas_call(results_kernel, name='results', out_shape=out_shape, in_sp...]
where the time goes in v3:
time: 178 us; the launch traced here: 177 us
  Pallas kernels  175 us (98%)
    pallas_call x1, Pallas kernels, layer(): pl.pallas_call(layer_kernel, name='layer', out_shape=out_shape, in_specs=...  169 us
    pallas_call x1, Pallas kernels, results(): pl.pallas_call(results_kernel, name='results', out_shape=out_shape, in_sp...  5.65 us

profile of v3, /device:TPU:0, one launch (start us, length us, event | category | flops | bytes accessed | tf_op | source)
XLA Modules:
  0.0 177.4 jit_solution(2738427885975099308)
XLA Ops:
  0.7 0.9 concatenate.37
  1.5 0.6 convert_element_type.10.refs_7_
  2.1 169.4 %layer.1 = (bf16[1024,768]{1,0:T(8,128)(2,1)}, f32[1024,768]{1,0:T(8,128)}, f32[24,2304]{1,0:T(8,128)}, f32[24,768]{1,0:T(8,128)}, f32[24,3072]{1,0:T(8,128)}, /*index=5*/f32[96,768]{1,0:T(8,128)}, f32[16,128]{1,0:T(8,128)}) custom-call(bf16[1024,768]{1,0:T(8,128)(2,1)} %refs_0_.1, s32[1,1024]{1,0:T(1,128)} %refs_1_.1, bf16[1024,768]{1,0:T(8,128)(2,1)} %refs_2_.1, ...), custom_call_target="tpu_custom_call" | custom-call | flops 49999998976 | bytes 30000000 | tf_op jit(solution)/shard_map/layer/pallas_call | solution.py:1177
  171.5 5.6 %results.1 = (bf16[1024,768]{1,0:T(8,128)(2,1)}, f32[1024,768]{1,0:T(8,128)}, f32[24,2304]{1,0:T(8,128)}, f32[24,768]{1,0:T(8,128)}, f32[24,3072]{1,0:T(8,128)},...) custom-call(bf16[1024,768]{1,0:T(8,128)(2,1)} %get-tuple-element.37., ...), custom_call_target="tpu_custom_call" | custom-call | tf_op jit(solution)/shard_map/results/pallas_call | solution.py:1212
  (1 shorter events, 0.0 us)

commit v4 on v3

--- a/solution.py
+++ b/solution.py
@@ -288,16 +288,17 @@
 KEY_WINDOWS = ((0, 256), (0, 512), (0, 768), (256, 1024))
 DOCUMENTS = 6
 FAR_BELOW = 2.0**100
-STRIP = 128
+STRIP = 256
 TILE = 256
 VMEM_LIMIT = 63 * 2**20
 GELU_A = 0.7978845608028654
 GELU_B = 0.044715
 
-GATHER_UNITS = (("qkv", 0), ("qkv", 1), ("qkv", 2), ("out", 0)) + tuple(
-    (name, part) for part in range(4) for name in ("up", "down")
-)
-SCATTER_UNITS = GATHER_UNITS[4:] + GATHER_UNITS[3:4] + GATHER_UNITS[:3]
+GATHER_UNITS = tuple(("qkv", 0, first, 128) for first in (0, 128, 256))
+GATHER_UNITS += (("qkv", 1, 0, 384), ("qkv", 2, 0, 384), ("out", 0, 0, 384))
+GATHER_UNITS += tuple((name, part, 0, 384) for part in range(4) for name in ("up", "down"))
+SCATTER_UNITS = GATHER_UNITS[6:] + (("out", 0, 0, 384), ("qkv", 0, 0, 384), ("qkv", 1, 0, 384))
+SCATTER_UNITS += tuple(("qkv", 2, first, 128) for first in (0, 128, 256))
 ROWS = 24
 HALF = 384
 SHARDS = {"qkv": (24, 2304), "out": (24, 768), "up": (24, 3072), "down": (96, 768)}
@@ -429,7 +430,7 @@
 
     def __init__(self, place, unit, shard, full, pair_out, pair_in, send_sems, recv_sems):
         self.place = place
-        self.name, self.part = unit
+        self.name, self.part, self.first, self.width = unit
         self.shard, self.full = shard, full
         self.pair_out, self.pair_in = pair_out, pair_in
         self.sems = (send_sems, recv_sems)
@@ -437,14 +438,15 @@
     def columns_of(self, core):
         if self.name == "qkv":
             start = 2 * self.part * 128 + 128 * core
-            parts = [self.shard[:, pl.ds(aligned(start + WIDTH * i, 128), 128)] for i in range(3)]
+            chosen = range(self.first // 128, (self.first + self.width) // 128)
+            parts = [self.shard[:, pl.ds(aligned(start + WIDTH * i, 128), 128)] for i in chosen]
             return jnp.concatenate(parts, axis=1).astype(F32)
         start = WIDTH * self.part if self.name == "up" else 0
-        columns = self.shard[:, pl.ds(aligned(start + HALF * core, 128), HALF)].astype(F32)
+        columns = self.shard[:, pl.ds(aligned(start + HALF * core + self.first, 128), self.width)].astype(F32)
         return columns[ROWS * self.part : ROWS * self.part + ROWS] if self.name == "down" else columns
 
     def rows_at(self, first, count):
-        columns = pl.ds(aligned(HALF * self.place.core, 128), HALF)
+        columns = pl.ds(aligned(HALF * self.place.core + self.first, 128), self.width)
         return self.full.at[pl.ds(aligned(first, 16), count), columns]
 
     def group(self, dp):
@@ -474,7 +476,7 @@
 
     def pair(self):
         self.pair_out[0:ROWS] = self.columns_of(1 - self.place.core).astype(BF16)
-        self.pair_out[ROWS:] = jnp.zeros((32 - ROWS, HALF), BF16)
+        self.pair_out[ROWS:] = jnp.zeros((32 - ROWS, self.width), BF16)
         self.start(0)
 
     def assemble(self):
@@ -516,24 +518,24 @@
 
     def __init__(self, place, unit, partial, target, halves, from_next, from_near, from_z, pair, send_sems, recv_sems):
         self.place = place
-        self.name, self.part = unit
+        self.name, self.part, self.first, self.width = unit
         self.partial, self.target = partial, target
         self.halves, self.from_next, self.from_near = halves, from_next, from_near
         self.from_z, self.pair_buffer = from_z, pair
         self.sems = (send_sems, recv_sems)
 
     @staticmethod
-    def scratch():
+    def scratch(width):
         return [
-            pltpu.VMEM((WIDTH, HALF), BF16),
-            pltpu.VMEM((2, 8 * ROWS, HALF), BF16),
-            pltpu.VMEM((8 * ROWS, HALF), BF16),
-            pltpu.VMEM((3, 2 * ROWS, HALF), BF16),
-            pltpu.VMEM((3, ROWS, HALF), F32),
+            pltpu.VMEM((WIDTH, width), BF16),
+            pltpu.VMEM((2, 8 * ROWS, width), BF16),
+            pltpu.VMEM((8 * ROWS, width), BF16),
+            pltpu.VMEM((3, 2 * ROWS, width), BF16),
+            pltpu.VMEM((3, ROWS, width), F32),
         ]
 
     def columns(self, core):
-        return pl.ds(aligned(HALF * core, 128), HALF)
+        return pl.ds(aligned(HALF * core + self.first, 128), self.width)
 
     def group(self, dp):
         return self.halves.at[pl.ds(aligned(dp * (8 * ROWS), 16), 8 * ROWS)]
@@ -570,7 +572,7 @@
 
         def body(index, carry):
             at = pl.ds(aligned(index * step, 16), step)
-            former[at] = (former[at].astype(F32) + latter(at).astype(F32)).astype(BF16)
+            former[at] = former[at] + latter(at)
             return carry
 
         lax.fori_loop(0, rows // step, body, 0)
@@ -615,38 +617,33 @@
         for source, core in ((1, self.place.core), (2, 1 - self.place.core)):
             if self.name == "qkv":
                 start = 2 * self.part * 128 + 128 * core
-                for i in range(3):
-                    columns = pl.ds(aligned(start + WIDTH * i, 128), 128)
-                    self.target[:, columns] = self.pair_buffer[source, :, 128 * i : 128 * i + 128]
+                for number in range(self.width // 128):
+                    columns = pl.ds(aligned(start + WIDTH * (self.first // 128 + number), 128), 128)
+                    self.target[:, columns] = self.pair_buffer[source, :, 128 * number : 128 * number + 128]
             elif self.name == "down":
                 self.target[ROWS * self.part : ROWS * self.part + ROWS, self.columns(core)] = self.pair_buffer[source]
             else:
-                start = WIDTH * self.part + HALF * core
-                self.target[:, pl.ds(aligned(start, 128), HALF)] = self.pair_buffer[source]
+                start = WIDTH * self.part + HALF * core + self.first
+                self.target[:, pl.ds(aligned(start, 128), self.width)] = self.pair_buffer[source]
 
     def finish(self):
         for index in range(self.SEMS):
             self.copy(index).wait_send()
 
 
-STAGES = {
-    "P": "to_partner",
-    "A": "to_next",
-    "B": "to_near",
-    "Z": "along_z",
-    "D": "to_pair",
-    "S": "store",
-    "p": "pair",
-    "z": "along_z",
-    "n": "to_near",
-    "x": "to_next",
-    "c": "to_core",
-    "r": "arrived",
-    "b": "begin",
-    "m": "middle",
-    "l": "later",
-    "e": "end",
-}
+class Stage:
+    def __init__(self, kind, method):
+        self.kind, self.method = kind, method
+
+    def __getitem__(self, unit):
+        return self.kind, self.method, unit
+
+
+p, z, n = Stage(0, "pair"), Stage(0, "along_z"), Stage(0, "to_near")
+x, c, r = Stage(0, "to_next"), Stage(0, "to_core"), Stage(0, "arrived")
+G, A, B = Stage(1, "to_partner"), Stage(1, "to_next"), Stage(1, "to_near")
+Z, D, S = Stage(1, "along_z"), Stage(1, "to_pair"), Stage(1, "store")
+b, m, l, e = Stage(2, "begin"), Stage(2, "middle"), Stage(2, "later"), Stage(2, "end")
 
 
 def strips(body, carry=0):
@@ -742,7 +739,9 @@
     attended[p.rows, pl.ds(aligned(pair * 128, 128), 128)] = out.T.astype(BF16)
 
 
-def attend_back(wide, pair, block, query_side, key_side, causal, attended, grad_attended, logsums, key_sum, value_sum):
+def attend_back(
+    wide, pair, block, query_side, key_side, causal, attended, grad_attended, logsums, query_grad, key_sum, value_sum
+):
     p = Pair(wide, pair, block, query_side, key_side)
     features = pl.ds(aligned(pair * 128, 128), 128)
     incoming = grad_attended[p.rows, features]
@@ -758,7 +757,7 @@
     value_part = dot_nn(jnp.concatenate(probs, axis=1), both(incoming))
     key_part = dot_nn(jnp.concatenate(slopes, axis=1), both(p.q))
     query_part = dot_tn(both(p.k), jnp.concatenate(slopes, axis=0))
-    wide[p.rows, p.at[0]] = (query_part.T * HEAD_DIM**-0.5).astype(BF16)
+    query_grad[:, p.rows] = (query_part * HEAD_DIM**-0.5).astype(BF16)
     inside = p.stop - p.start - QUERY_ROWS
     if inside:
         earlier = pl.ds(p.start, inside)
@@ -769,58 +768,59 @@
     value_sum[newest] = value_part[inside:]
 
 
-PLAN = {
-    "greet": "b0 p0 p1 p2",
-    "packed": "m0 z0 p3 p4 p5",
-    "group0": "n0 z3 p6 n1 z4 p7 x0 n2 z5 p8 x1 n3 z6 p9 c0 x2 n4 z7 p10 r0",
-    "pair0": "x3",
-    "pair1": "c1 x4",
-    "group1": "n5 z8 p11 n6 z9 r1",
-    "qkv1": "c2",
-    "pair2": "n7 z10",
-    "pair3": "c3 x5",
-    "group2": "r2",
-    "qkv2": "x6",
-    "pair5": "c4 x7",
-    "joined": "r3",
-    "branch": "n8 z11",
-    "norm": "c5 n9 n10",
-    "step0": "r4 r5",
-    "hidden0": "c6 x8 x9",
-    "outer0": "c7 n11",
-    "grads0": "x10 P0 P1",
-    "step1": "r6 r7",
-    "hidden1": "c8 x11 A0",
-    "outer1": "c9 A1",
-    "grads1": "c10 P2 P3",
-    "step2": "r8 r9",
-    "hidden2": "c11 A2 A3",
-    "outer2": "B0",
-    "grads2": "B1 P4 P5",
-    "step3": "r10 r11",
-    "hidden3": "Z0 B2 A4 A5",
-    "outer3": "Z1",
-    "grads3": "D0 Z2 B3 P6 P7",
-    "back": "D1 B4 S0 A6 A7",
-    "attended": "D2 Z3 S1",
-    "out": "S2 P8",
-    "first": "Z4 B5 A8 b1",
-    "pair_back0": "D3 B6 m1",
-    "pair_back1": "D4 Z5 B7 S3 l1",
-    "qkv_grads0": "Z6 S4 P9",
-    "pair_back2": "D5 Z7 B8 A9 e1",
-    "pair_back3": "D6 S5",
-    "qkv_grads1": "Z8 D7 S6 P10",
-    "pair_back4": "B9 S7 A10",
-    "pair_back5": "D8",
-    "qkv_grads2": "Z9 S8 P11",
-    "tokens0": "B10",
-    "tokens1": "A11",
-    "half": "b2 D9 Z10",
-    "last": "m2 S9 B11 l2 Z11 D10 S10 D11 S11 e2",
-    "documents": "l0 z1 z2",
-    "vectors": "e0",
-}
+PLAN = dict(
+        greet=(p[1], p[4],),
+        packed=(p[8], p[5], p[2], p[12], z[1], p[10], p[0], p[6], b[0], z[2], m[0], p[7], p[3], p[11], z[0],
+        z[3],),
+        documents=(n[1], p[13], n[2], n[0], z[4], z[5], l[0], z[6], p[9], x[1],),
+        vectors=(z[7], z[8], x[2], n[3], z[9], c[1], x[0], n[4], x[3], c[0], z[13], x[4], n[5], r[1], c[2],
+        e[0],),
+        one=(r[0], c[3],),
+        seed=(n[6], r[2],),
+        qkv0=(x[5],),
+        pair0=(n[7], c[4],),
+        pair1=(z[11],),
+        group1=(n[8], z[10], r[3],),
+        qkv1=(x[6], r[4], n[9], z[12],),
+        pair2=(x[7],),
+        qkv2=(x[9], c[5],),
+        pair5=(x[8], n[10],),
+        joined=(c[6], r[5],),
+        branch=(c[7],),
+        norm=(r[6],),
+        step0=(r[7], n[12], n[11], c[9], n[13],),
+        hidden0=(x[10], r[9],),
+        outer0=(c[8],),
+        step1=(G[0], x[11], r[8], G[1],),
+        hidden1=(A[0], c[10], x[12],),
+        outer1=(c[11], r[10],),
+        grads1=(x[13], G[3], r[11],),
+        step2=(A[1],),
+        hidden2=(c[12],),
+        outer2=(G[2], A[3], c[13],),
+        grads2=(A[2],),
+        step3=(B[1], r[12], G[5], r[13],),
+        hidden3=(B[0], G[4],),
+        outer3=(A[4], A[5],),
+        grads3=(G[6], B[2],),
+        back=(B[3], Z[0],),
+        attended=(Z[1], A[6], b[1],),
+        first=(G[7], B[4],),
+        pair_back0=(m[1], A[7], Z[2],),
+        pair_back1=(Z[4],),
+        qkv_grads0=(l[1], B[5], G[8], Z[3], G[9], B[6],),
+        pair_back2=(A[9],),
+        pair_back3=(B[7],),
+        qkv_grads1=(Z[5], A[8], Z[6], G[10],),
+        pair_back4=(A[10], Z[7], B[9],),
+        qkv_grads2=(G[12], D[1], G[13], B[8],),
+        tokens0=(Z[9], G[11], D[2], D[0], A[12], D[4], B[10],),
+        tokens1=(A[13], Z[8], A[11],),
+        half=(Z[10], B[13], b[2], D[3], B[12], m[2], D[5], D[6], B[11], S[5], e[1], D[9], Z[13], S[4], S[6],
+        S[3], Z[12], Z[11], D[7], D[8], l[2], D[13], S[1], D[10], S[7], S[8], S[9], S[13], S[2], D[12], S[0],
+        D[11], S[12],),
+        last=(S[10], e[2], S[11],),
+)
 
 
 def layer_kernel(*refs):
@@ -841,7 +841,7 @@
     tokens, cotangent, wide, norm, norm_t, attended, seed, act, act_t, slope = take(10)
     middle, outer, grad_norm = take(3)
     logsums, query_side, key_side, causal, vectors, qkv_bias, qkv_scale, early = take(8)
-    late, up_shard, up_target = take(3)
+    late, up_shard, up_target, first_t = take(4)
     pair_buffers = take(2 * len(GATHER_UNITS))
     scatter_buffers = take(5 * len(SCATTER_UNITS))
     gather_sems, scatter_sems = take(2), take(2)
@@ -865,7 +865,7 @@
             place,
             unit,
             shards[unit[0]],
-            whole(*unit),
+            whole(*unit[:2]),
             *pair_buffers[2 * i : 2 * i + 2],
             gather_sems[0].at[i],
             gather_sems[1].at[i],
@@ -877,7 +877,7 @@
         ScatterUnit(
             place,
             unit,
-            qkv_partials[unit[1]] if unit[0] == "qkv" else whole(*unit),
+            qkv_partials[unit[1]] if unit[0] == "qkv" else whole(*unit[:2]),
             targets[unit[0]],
             *scatter_buffers[5 * i : 5 * i + 5],
             scatter_sems[0].at[i],
@@ -891,19 +891,18 @@
         for source, target, refs in zip((vectors, early, late), (vectors, early, late), small_refs)
     ]
 
-    def run(text):
-        for step in text.split():
-            units = vector_sums if step[0] in "bmle" else coming if step[0].islower() else leaving
-            getattr(units[int(step[1:])], STAGES[step[0]])()
+    def run(steps):
+        for kind, method, unit in steps:
+            getattr((coming, leaving, vector_sums)[kind][unit], method)()
 
     def after(name, index=None, count=0):
         if index is None:
-            run(PLAN.get(name, ""))
+            run(PLAN.get(name, ()))
             return
         for number in range(count):
-            text = PLAN.get(name + str(number), "")
-            if text:
-                pl.when(index == number)(lambda text=text: run(text))
+            steps = PLAN.get(name + str(number), ())
+            if steps:
+                pl.when(index == number)(lambda steps=steps: run(steps))
 
     loads = [
         pltpu.make_async_copy(source, target, local_sems.at[2 + i])
@@ -947,6 +946,18 @@
 
     strips(norm_one)
     after("one")
+    first_t[0:WIDTH] = norm[...].T
+    first_t[WIDTH:] = jnp.ones((16, TOKENS), BF16)
+
+    def seed_one(rows, down_bias):
+        scaled = (branch_scale * cotangent[rows].astype(F32)).astype(BF16)
+        seed[rows] = scaled
+        outer[rows] = jnp.zeros((STRIP, WIDTH), F32)
+        grad_norm[rows] = jnp.zeros((STRIP, WIDTH), F32)
+        return down_bias + column_sum(scaled.astype(F32))
+
+    early[3:4] = strips(seed_one, jnp.zeros((1, WIDTH), F32))
+    after("seed")
 
     def forward_group(group, carry):
         after("group", group, 3)
@@ -975,16 +986,12 @@
     after("branch")
     gain_two, offset_two = vectors[5:6], vectors[6:7]
 
-    def norm_two(rows, down_bias):
+    def norm_two(rows, carry):
         xhat, _ = standardized(middle[rows])
         norm[rows] = (xhat * gain_two + offset_two).astype(BF16)
-        scaled = (branch_scale * cotangent[rows].astype(F32)).astype(BF16)
-        seed[rows] = scaled
-        outer[rows] = jnp.zeros((STRIP, WIDTH), F32)
-        grad_norm[rows] = jnp.zeros((STRIP, WIDTH), F32)
-        return down_bias + column_sum(scaled.astype(F32))
-
-    early[3:4] = strips(norm_two, jnp.zeros((1, WIDTH), F32))
+        return carry
+
+    strips(norm_two)
     norm_t[0:WIDTH] = norm[...].T
     norm_t[WIDTH:] = jnp.ones((16, TOKENS), BF16)
     after("norm")
@@ -1009,7 +1016,7 @@
         after("outer", step, 4)
         for number in range(4):
             def sent(number=number):
-                for unit in coming[4 + 2 * number : 6 + 2 * number]:
+                for unit in coming[6 + 2 * number : 8 + 2 * number]:
                     unit.finish()
 
             pl.when(step == number)(sent)
@@ -1048,18 +1055,17 @@
         at = slice(n * TILE, n * TILE + TILE)
         act[:, at] = dot_nt(seed[...], wo[at]).astype(BF16)
     after("attended")
-    for unit in coming[:4]:
+    for unit in coming[:6]:
         unit.finish()
     act_t[...] = attended[...].T
     for n in range(3):
         at = slice(n * TILE, n * TILE + TILE)
         wo[:, at] = dot_nn(act_t[...], seed[:, at]).astype(BF16)
     after("out")
-    strips(norm_one)
-    norm_t[0:WIDTH] = norm[...].T
     out_copy.wait()
     after("first")
 
+    query_grad = norm_t.at[0:128]
     key_sum, value_sum = outer.at[:, 0:128], outer.at[:, 128:256]
 
     def backward_group(group, carry):
@@ -1067,9 +1073,21 @@
             pair = 2 * group + half
             for block in range(4):
                 attend_back(
-                    wide, pair, block, query_side, key_side, causal, attended, act, logsums, key_sum, value_sum
+                    wide,
+                    pair,
+                    block,
+                    query_side,
+                    key_side,
+                    causal,
+                    attended,
+                    act,
+                    logsums,
+                    query_grad,
+                    key_sum,
+                    value_sum,
                 )
             first = pair * 384
+            wide[:, pl.ds(aligned(first, 128), 128)] = query_grad[...].T
             wide[:, pl.ds(aligned(first + 128, 128), 128)] = key_sum[...].astype(BF16)
             wide[:, pl.ds(aligned(first + 256, 128), 128)] = value_sum[...].astype(BF16)
             after("pair_back", pair, PAIRS)
@@ -1082,7 +1100,7 @@
                 for n in range(3):
                     at = slice(n * TILE, n * TILE + TILE)
                     columns = slice(number * WIDTH + n * TILE, number * WIDTH + n * TILE + TILE)
-                    grad = dot_nn(norm_t[...], wide[:, columns])
+                    grad = dot_nn(first_t[...], wide[:, columns])
                     qkv_partials[number][:, at] = grad[:WIDTH].astype(BF16)
                     rows.append(grad[WIDTH : WIDTH + 1])
                 row = jnp.concatenate(rows, axis=1)
@@ -1165,10 +1183,12 @@
         pltpu.VMEM((4, WIDTH), F32),
         pltpu.VMEM(SHARDS["up"], BF16),
         pltpu.VMEM(SHARDS["up"], F32),
+        pltpu.VMEM((WIDTH + 16, TOKENS), BF16),
     ]
-    scratch += [pltpu.VMEM((32, HALF), BF16)] * (2 * len(GATHER_UNITS))
-    for _ in SCATTER_UNITS:
-        scratch += ScatterUnit.scratch()
+    for unit in GATHER_UNITS:
+        scratch += [pltpu.VMEM((32, unit[3]), BF16)] * 2
+    for unit in SCATTER_UNITS:
+        scratch += ScatterUnit.scratch(unit[3])
     scratch += [pltpu.SemaphoreType.DMA((len(GATHER_UNITS), GatherUnit.SEMS))] * 2
     scratch += [pltpu.SemaphoreType.DMA((len(SCATTER_UNITS), ScatterUnit.SEMS))] * 2
     for shape, dtype in (((16, WIDTH), BF16), ((8, WIDTH), F32), ((4, WIDTH), F32)):

time: 178 us -> 162 us (0.910)
  Pallas kernels: 175 us -> 160 us
    pallas_call x1, Pallas kernels: 169 us -> 154 us  [layer(): pl.pallas_call(layer_kernel, name='layer', out_shape=out_shape, in_specs=...]
where the time goes in v4:
time: 162 us
  Pallas kernels  160 us (99%)
    pallas_call x1, Pallas kernels, layer(): pl.pallas_call(layer_kernel, name='layer', out_shape=out_shape, in_specs=...  154 us
    pallas_call x1, Pallas kernels, results(): pl.pallas_call(results_kernel, name='results', out_shape=out_shape, in_sp...  5.65 us

profile of v4, /device:TPU:0, one launch (start us, length us, event | category | flops | bytes accessed | tf_op | source)
XLA Modules:
  0.0 162.1 jit_solution(9606123468429911162)
XLA Ops:
  0.7 0.9 concatenate.37
  1.5 0.6 convert_element_type.10.refs_7_
  2.1 154.1 %layer.1 = (bf16[1024,768]{1,0:T(8,128)(2,1)}, f32[1024,768]{1,0:T(8,128)}, f32[24,2304]{1,0:T(8,128)}, f32[24,768]{1,0:T(8,128)}, f32[24,3072]{1,0:T(8,128)}, /*index=5*/f32[96,768]{1,0:T(8,128)}, f32[16,128]{1,0:T(8,128)}) custom-call(bf16[1024,768]{1,0:T(8,128)(2,1)} %refs_0_.1, s32[1,1024]{1,0:T(1,128)} %refs_1_.1, bf16[1024,768]{1,0:T(8,128)(2,1)} %refs_2_.1, ...), custom_call_target="tpu_custom_call" | custom-call | flops 49999998976 | bytes 30000000 | tf_op jit(solution)/shard_map/layer/pallas_call | solution.py:1197
  156.2 5.6 %results.1 = (bf16[1024,768]{1,0:T(8,128)(2,1)}, f32[1024,768]{1,0:T(8,128)}, f32[24,2304]{1,0:T(8,128)}, f32[24,768]{1,0:T(8,128)}, f32[24,3072]{1,0:T(8,128)},...) custom-call(bf16[1024,768]{1,0:T(8,128)(2,1)} %get-tuple-element.37., ...), custom_call_target="tpu_custom_call" | custom-call | tf_op jit(solution)/shard_map/results/pallas_call | solution.py:1232
  (1 shorter events, 0.0 us)

commit v5 on v4

--- a/solution.py
+++ b/solution.py
@@ -508,8 +508,8 @@
     def arrived(self):
         self.landed(7, 8, 9, 10)
 
-    def finish(self):
-        for index in range(self.SEMS):
+    def finish(self, last=0):
+        for index in range(self.SEMS - last):
             self.copy(index).wait_send()
 
 
@@ -626,8 +626,8 @@
                 start = WIDTH * self.part + HALF * core + self.first
                 self.target[:, pl.ds(aligned(start, 128), self.width)] = self.pair_buffer[source]
 
-    def finish(self):
-        for index in range(self.SEMS):
+    def finish(self, last=0):
+        for index in range(self.SEMS - last):
             self.copy(index).wait_send()
 
 
@@ -816,10 +816,10 @@
         qkv_grads2=(G[12], D[1], G[13], B[8],),
         tokens0=(Z[9], G[11], D[2], D[0], A[12], D[4], B[10],),
         tokens1=(A[13], Z[8], A[11],),
-        half=(Z[10], B[13], b[2], D[3], B[12], m[2], D[5], D[6], B[11], S[5], e[1], D[9], Z[13], S[4], S[6],
-        S[3], Z[12], Z[11], D[7], D[8], l[2], D[13], S[1], D[10], S[7], S[8], S[9], S[13], S[2], D[12], S[0],
-        D[11], S[12],),
-        last=(S[10], e[2], S[11],),
+        half=(Z[10], B[13], b[2], D[3], B[12], m[2], D[5], D[6], B[11], S[5], e[1], D[9], Z[13], S[3], Z[12],
+        Z[11], S[6], S[0], S[2], S[4],),
+        last=(D[7], D[8], l[2], D[13], S[1], D[10], S[7], S[8], S[9], S[13], D[12], D[11], S[12], S[10], e[2],
+        S[11],),
 )
 
 
@@ -1055,8 +1055,7 @@
         at = slice(n * TILE, n * TILE + TILE)
         act[:, at] = dot_nt(seed[...], wo[at]).astype(BF16)
     after("attended")
-    for unit in coming[:6]:
-        unit.finish()
+    coming[5].finish()
     act_t[...] = attended[...].T
     for n in range(3):
         at = slice(n * TILE, n * TILE + TILE)
@@ -1138,12 +1137,16 @@
         ],
         axis=1,
     )
-    after("last")
     back = lax.rem(DEVICES - place.number, DEVICES) * ROWS
     small_out[0:8] = pltpu.roll(early[...], back, 1)[:, 0:128]
+    for unit in coming[:5] + leaving[:9]:
+        unit.finish(1)
+    after("last")
     small_out[8:12] = pltpu.roll(late[...], back, 1)[:, 0:128]
     small_out[12:16] = jnp.zeros((4, 128), F32)
-    for unit in leaving:
+    for unit in coming[:5] + leaving[:9]:
+        unit.copy(unit.SEMS - 1).wait_send()
+    for unit in leaving[9:]:
         unit.finish()
     tokens_copy.wait()
 

time: 162 us -> 162 us (level)
  no operation moved by 1% of the time
where the time goes in v5:
time: 162 us
  Pallas kernels  159 us (98%)
    pallas_call x1, Pallas kernels, layer(): pl.pallas_call(layer_kernel, name='layer', out_shape=out_shape, in_specs=...  154 us
    pallas_call x1, Pallas kernels, results(): pl.pallas_call(results_kernel, name='results', out_shape=out_shape, in_sp...  5.65 us

profile of v5, /device:TPU:0, one launch (start us, length us, event | category | flops | bytes accessed | tf_op | source)
XLA Modules:
  0.0 161.6 jit_solution(5864505866406629038)
XLA Ops:
  0.7 0.9 concatenate.37
  1.5 0.6 convert_element_type.10.refs_7_
  2.1 153.7 %layer.1 = (bf16[1024,768]{1,0:T(8,128)(2,1)}, f32[1024,768]{1,0:T(8,128)}, f32[24,2304]{1,0:T(8,128)}, f32[24,768]{1,0:T(8,128)}, f32[24,3072]{1,0:T(8,128)}, /*index=5*/f32[96,768]{1,0:T(8,128)}, f32[16,128]{1,0:T(8,128)}) custom-call(bf16[1024,768]{1,0:T(8,128)(2,1)} %refs_0_.1, s32[1,1024]{1,0:T(1,128)} %refs_1_.1, bf16[1024,768]{1,0:T(8,128)(2,1)} %refs_2_.1, ...), custom_call_target="tpu_custom_call" | custom-call | flops 49999998976 | bytes 30000000 | tf_op jit(solution)/shard_map/layer/pallas_call | solution.py:1200
  155.8 5.6 %results.1 = (bf16[1024,768]{1,0:T(8,128)(2,1)}, f32[1024,768]{1,0:T(8,128)}, f32[24,2304]{1,0:T(8,128)}, f32[24,768]{1,0:T(8,128)}, f32[24,3072]{1,0:T(8,128)},...) custom-call(bf16[1024,768]{1,0:T(8,128)(2,1)} %get-tuple-element.37., ...), custom_call_target="tpu_custom_call" | custom-call | tf_op jit(solution)/shard_map/results/pallas_call | solution.py:1235
  (1 shorter events, 0.0 us)
